TPU v7x, 32 devices: a whole 2x2x4 slice. The times are simulated.
32 devices in a mesh: slab: 4 (over y, core), grp: 8 (over z, x).
Axes of the slice: x: 2, y: 2, z: 4, core: 2. Of those that a mesh axis runs over, the one named last changes fastest.
Arguments:
- node_feats: bfloat16 [262144, 128], P(('slab', 'grp')), may hold values from -6 to 6
- cotangent: bfloat16 [262144, 128], P(('slab', 'grp')), may hold values from -6 to 6
- fine_adjacency: bfloat16 [4096, 64, 768], P(('slab', 'grp')), may hold values from -0.21875 to 0.21875
- fine_columns: int32 [4096, 12], P(('slab', 'grp')), may hold values from 0 to 143, as said below
- pool_one: bfloat16 [512, 64, 512], P(('slab', 'grp')), may hold values from -0.25 to 0.25
- pool_one_columns: int32 [512, 8], P(('slab', 'grp')), may hold values from 0 to 127
- count_one: int32 [32], P(('slab', 'grp')), may hold values from 256 to 1024, as said below
- owner_one: int32 [32768], P(('slab', 'grp')), may hold values from 0 to 4095, as said below
- adjacency_one: bfloat16 [256, 64, 512], P(('slab', 'grp')), may hold values from -0.25 to 0.25
- columns_one: int32 [256, 8], P(('slab', 'grp')), may hold values from 0 to 63
- pool_two: bfloat16 [128, 64, 512], P(('slab', 'grp')), may hold values from -0.25 to 0.25
- pool_two_columns: int32 [128, 8], P(('slab', 'grp')), may hold values from 0 to 7
- count_two: int32 [32], P(('slab', 'grp')), may hold values from 64 to 256, as said below
- owner_two: int32 [8192], P(('slab', 'grp')), may hold values from 0 to 1023, as said below
- adjacency_two: bfloat16 [64, 64, 512], P(('slab', 'grp')), may hold values from -0.25 to 0.25
- columns_two: int32 [64, 8], P(('slab', 'grp')), may hold values from 0 to 15
- weight_in: bfloat16 [3, 256, 128], replicated, may hold values from -0.375 to 0.375
- weight_out: bfloat16 [3, 128, 128], replicated, may hold values from -0.5 to 0.5
- biases: float32 [3, 128], replicated, may hold values from -3 to 3
Outputs:
- node_out: bfloat16 [262144, 128], P(('slab', 'grp'))
- grad_feats: bfloat16 [262144, 128], P(('slab', 'grp'))
- grad_weight_in: float32 [3, 256, 128], replicated
- grad_weight_out: float32 [3, 128, 128], replicated
- grad_biases: float32 [3, 128], replicated
Inputs may be any that keep to these rules, and one draw needn't show every extreme that they name: `fine_columns`: row block r of a device reads blocks r to r + 16 of its extended rows. `count_one`: the 8 counts of one slab sum to 4096, and one of them equals 1024. `owner_one`: the live slots of a device are its first count_one slots. In one slab the live slots' values take each value below 4096 exactly once; value v names row v % 512 of device v // 512 of the slab. At most 128 live slots of one device name rows of one device, and in every slab some device has exactly that many for every device. Values of other slots are unused. `count_two`: the 8 counts of one slab sum to 1024, and one of them equals 256. `owner_two`: the live slots of a device are its first count_two slots. In one slab the live slots' values take each value below 1024 exactly once; value v names row v % 128 of device v // 128 of the slab. At most 32 live slots of one device name rows of one device, and in every slab some device has exactly that many for every device. Values of other slots are unused.
All inputs are finite; a program needn't handle non-finite values.
Results may differ from a plain program's by a relative error of at most 0.012.
Values may be sent and summed in bfloat16 or wider, within the bound.
No kernel may reach another device: no remote copies, remote signals or barrier semaphores. Data moves between devices by JAX's collectives and lax.ppermute only.
A program may use at most 320 MiB of HBM per device.

v0:
```python
import math

import jax
import jax.numpy as jnp
from jax import lax
from jax.sharding import PartitionSpec as P

HALO = 512


def with_halo(cells, sides, width):
    for axis, dim in sides:
        count = lax.axis_size(axis)
        ends = count - 1
        head = lax.slice_in_dim(cells, 0, width, axis=dim)
        tail = lax.slice_in_dim(cells, cells.shape[dim] - width, cells.shape[dim], axis=dim)
        cells = jnp.concatenate(
            [
                lax.ppermute(tail, axis, [(i, (i + 1) % count) for i in range(ends)]),
                cells,
                lax.ppermute(head, axis, [((i + 1) % count, i) for i in range(ends)]),
            ],
            axis=dim,
        )
    return cells


def block_apply(blocks, columns, context):
    block_count, block_rows, span = blocks.shape
    feature = context.shape[1]
    tiles = context.reshape(-1, block_rows, feature)
    picked = tiles[columns].reshape(block_count, span, feature)
    product = jnp.einsum("rij,rjh->rih", blocks, picked, preferred_element_type=jnp.float32)
    return product.reshape(block_count * block_rows, feature)


def block_transpose(blocks, columns, row_grads, targets):
    block_count, block_rows, span = blocks.shape
    feature = row_grads.shape[1]
    pieces = row_grads.reshape(block_count, block_rows, feature)
    spread = jnp.einsum("rij,rih->rjh", blocks, pieces, preferred_element_type=jnp.float32)
    spread = spread.reshape(block_count * columns.shape[1], block_rows, feature)
    summed = jax.ops.segment_sum(spread, columns.reshape(-1), num_segments=targets)
    return summed.reshape(targets * block_rows, feature)


def restrict(blocks, columns, source, live_mask):
    pooled = block_apply(blocks, columns, source)
    return jnp.where(live_mask[:, None], pooled, 0.0).astype(jnp.bfloat16)


def layer_forward(node_rows, message, weight_in, weight_out, bias_row):
    joined = jnp.concatenate([node_rows, message], axis=1)
    pre_act = jnp.dot(joined, weight_in, preferred_element_type=jnp.float32) + bias_row
    hidden = jax.nn.silu(pre_act).astype(jnp.bfloat16)
    result = node_rows.astype(jnp.float32) + jnp.dot(
        hidden, weight_out, preferred_element_type=jnp.float32
    )
    return (result.astype(jnp.bfloat16), pre_act, hidden)


def layer_backward(
    cotan_rows, node_rows, message, hidden, pre_act, weight_in, weight_out, blocks, columns, targets
):
    grad_low = cotan_rows.astype(jnp.bfloat16)
    delta_out = lax.dot_general(
        hidden, grad_low, (((0,), (0,)), ((), ())), preferred_element_type=jnp.float32
    )
    grad_hidden = lax.dot_general(
        grad_low, weight_out, (((1,), (1,)), ((), ())), preferred_element_type=jnp.float32
    )
    sigmoid_pre = jax.nn.sigmoid(pre_act)
    grad_pre = grad_hidden * sigmoid_pre * (1.0 + pre_act * (1.0 - sigmoid_pre))
    grad_pre_low = grad_pre.astype(jnp.bfloat16)
    delta_bias = jnp.sum(grad_pre, axis=0)
    joined = jnp.concatenate([node_rows, message], axis=1)
    delta_in = lax.dot_general(
        joined, grad_pre_low, (((0,), (0,)), ((), ())), preferred_element_type=jnp.float32
    )
    grad_joined = lax.dot_general(
        grad_pre_low, weight_in, (((1,), (1,)), ((), ())), preferred_element_type=jnp.float32
    )
    feature = node_rows.shape[1]
    grad_rows = cotan_rows + grad_joined[:, :feature]
    grad_message = grad_joined[:, feature:].astype(jnp.bfloat16)
    grad_context = block_transpose(blocks, columns, grad_message, targets)
    return ((delta_in, delta_out, delta_bias), grad_rows, grad_context)


def pack_layout(owners, live_mask, groups, balance):
    slot_count = owners.shape[0]
    capacity = slot_count // groups
    target = owners // balance
    onehot = (
        (target[:, None] == jnp.arange(groups, dtype=jnp.int32)[None, :]) & live_mask[:, None]
    ).astype(jnp.int32)
    slot_ranks = jnp.sum(onehot * jnp.cumsum(onehot, axis=0), axis=1) - 1
    place_at = jnp.where(live_mask, target * capacity + slot_ranks, groups * capacity)
    row_table = (
        jnp.full((groups * capacity,), balance, jnp.int32)
        .at[place_at]
        .set(owners % balance, mode="drop")
    )
    return (place_at, row_table.reshape(groups, capacity))


def pack_values(values, place_at, groups):
    capacity = values.shape[0] // groups
    buffer = (
        jnp.zeros((groups * capacity, values.shape[1]), values.dtype)
        .at[place_at]
        .set(values, mode="drop")
    )
    return buffer.reshape(groups, capacity, values.shape[1])


def place_rows(received, row_table, balance):
    feature = received.shape[-1]
    flat = received.reshape(-1, feature)
    return (
        jnp.zeros((balance, feature), received.dtype)
        .at[row_table.reshape(-1)]
        .set(flat, mode="drop")
    )


def pick_rows(table, row_table):
    balance = table.shape[0]
    flat = row_table.reshape(-1)
    taken = jnp.take(table, jnp.clip(flat, 0, balance - 1), axis=0)
    taken = jnp.where((flat < balance)[:, None], taken, jnp.zeros_like(taken))
    return taken.reshape(row_table.shape[0], row_table.shape[1], table.shape[1])


def unpack_rows(received, place_at, live_mask):
    feature = received.shape[-1]
    flat = received.reshape(-1, feature)
    taken = jnp.take(flat, jnp.clip(place_at, 0, flat.shape[0] - 1), axis=0)
    return jnp.where(live_mask[:, None], taken, jnp.zeros_like(taken))


def body(
    node_feats,
    cotangent,
    fine_adjacency,
    fine_columns,
    pool_one,
    pool_one_columns,
    count_one,
    owner_one,
    adjacency_one,
    columns_one,
    pool_two,
    pool_two_columns,
    count_two,
    owner_two,
    adjacency_two,
    columns_two,
    weight_in,
    weight_out,
    biases,
):
    groups = lax.axis_size("grp")
    block_rows = fine_adjacency.shape[1]
    fine_rows = node_feats.shape[0]
    slots_one = owner_one.shape[0]
    balance_one = slots_one // 2
    slots_two = owner_two.shape[0]
    balance_two = slots_two // 2
    extended = with_halo(node_feats, (("grp", 0),), HALO)
    message0 = block_apply(fine_adjacency, fine_columns, extended).astype(jnp.bfloat16)
    result0, pre_act0, hidden0 = layer_forward(
        node_feats, message0, weight_in[0], weight_out[0], biases[0]
    )
    live_one = jnp.arange(slots_one) < count_one[0]
    coarse_one = restrict(pool_one, pool_one_columns, result0, live_one)
    place_one, sent_one = pack_layout(owner_one, live_one, groups, balance_one)
    got_values, rows_one = (
        lax.all_to_all(
            pack_values(coarse_one, place_one, groups),
            "grp",
            split_axis=0,
            concat_axis=0,
            tiled=True,
        ),
        lax.all_to_all(sent_one, "grp", split_axis=0, concat_axis=0, tiled=True),
    )
    own_one = place_rows(got_values, rows_one, balance_one)
    context_one = lax.all_gather(own_one, "grp", axis=0, tiled=True)
    message_one = block_apply(adjacency_one, columns_one, context_one).astype(jnp.bfloat16)
    result1, pre_act1, hidden1 = layer_forward(
        own_one, message_one, weight_in[1], weight_out[1], biases[1]
    )
    live_two = jnp.arange(slots_two) < count_two[0]
    coarse_two = restrict(pool_two, pool_two_columns, result1, live_two)
    place_two, sent_two = pack_layout(owner_two, live_two, groups, balance_two)
    got_two, rows_two = (
        lax.all_to_all(
            pack_values(coarse_two, place_two, groups),
            "grp",
            split_axis=0,
            concat_axis=0,
            tiled=True,
        ),
        lax.all_to_all(sent_two, "grp", split_axis=0, concat_axis=0, tiled=True),
    )
    own_two = place_rows(got_two, rows_two, balance_two)
    context_two = lax.all_gather(own_two, "grp", axis=0, tiled=True)
    message_two = block_apply(adjacency_two, columns_two, context_two).astype(jnp.bfloat16)
    result2, pre_act2, hidden2 = layer_forward(
        own_two, message_two, weight_in[2], weight_out[2], biases[2]
    )
    returned_two = lax.all_to_all(
        pick_rows(result2, rows_two), "grp", split_axis=0, concat_axis=0, tiled=True
    )
    back_two = unpack_rows(returned_two, place_two, live_two)
    up_one = (
        result1.astype(jnp.float32)
        + block_transpose(pool_two, pool_two_columns, back_two, balance_one // block_rows)
    ).astype(jnp.bfloat16)
    returned_one = lax.all_to_all(
        pick_rows(up_one, rows_one), "grp", split_axis=0, concat_axis=0, tiled=True
    )
    back_one = unpack_rows(returned_one, place_one, live_one)
    node_out = (
        result0.astype(jnp.float32)
        + block_transpose(pool_one, pool_one_columns, back_one, fine_rows // block_rows)
    ).astype(jnp.bfloat16)
    grad_slots_one = restrict(pool_one, pool_one_columns, cotangent, live_one)
    arrived_one = lax.all_to_all(
        pack_values(grad_slots_one, place_one, groups),
        "grp",
        split_axis=0,
        concat_axis=0,
        tiled=True,
    )
    grad_up_one = place_rows(arrived_one, rows_one, balance_one)
    grad_slots_two = restrict(pool_two, pool_two_columns, grad_up_one, live_two)
    arrived_two = lax.all_to_all(
        pack_values(grad_slots_two, place_two, groups),
        "grp",
        split_axis=0,
        concat_axis=0,
        tiled=True,
    )
    grad_out_two = place_rows(arrived_two, rows_two, balance_two)
    sums_two, grad_rows_two, grad_ctx_two = layer_backward(
        grad_out_two.astype(jnp.float32),
        own_two,
        message_two,
        hidden2,
        pre_act2,
        weight_in[2],
        weight_out[2],
        adjacency_two,
        columns_two,
        groups * balance_two // block_rows,
    )
    grad_own_two = grad_rows_two + lax.psum_scatter(
        grad_ctx_two.astype(jnp.bfloat16), "grp", scatter_dimension=0, tiled=True
    ).astype(jnp.float32)
    sent_back_two = lax.all_to_all(
        pick_rows(grad_own_two.astype(jnp.bfloat16), rows_two),
        "grp",
        split_axis=0,
        concat_axis=0,
        tiled=True,
    )
    grad_coarse_two = unpack_rows(sent_back_two, place_two, live_two)
    grad_out_one = grad_up_one.astype(jnp.float32) + block_transpose(
        pool_two, pool_two_columns, grad_coarse_two, balance_one // block_rows
    )
    sums_one, grad_rows_one, grad_ctx_one = layer_backward(
        grad_out_one,
        own_one,
        message_one,
        hidden1,
        pre_act1,
        weight_in[1],
        weight_out[1],
        adjacency_one,
        columns_one,
        groups * balance_one // block_rows,
    )
    grad_own_one = grad_rows_one + lax.psum_scatter(
        grad_ctx_one.astype(jnp.bfloat16), "grp", scatter_dimension=0, tiled=True
    ).astype(jnp.float32)
    sent_back_one = lax.all_to_all(
        pick_rows(grad_own_one.astype(jnp.bfloat16), rows_one),
        "grp",
        split_axis=0,
        concat_axis=0,
        tiled=True,
    )
    grad_coarse_one = unpack_rows(sent_back_one, place_one, live_one)
    grad_out_zero = cotangent.astype(jnp.float32) + block_transpose(
        pool_one, pool_one_columns, grad_coarse_one, fine_rows // block_rows
    )
    sums_zero, grad_rows_zero, grad_ctx_zero = layer_backward(
        grad_out_zero,
        node_feats,
        message0,
        hidden0,
        pre_act0,
        weight_in[0],
        weight_out[0],
        fine_adjacency,
        fine_columns,
        (fine_rows + 2 * HALO) // block_rows,
    )
    rim_terms = jnp.concatenate([grad_ctx_zero[:HALO], grad_ctx_zero[HALO + fine_rows :]], axis=0)
    neighbour_terms = with_halo(rim_terms.astype(jnp.bfloat16), (("grp", 0),), HALO).astype(
        rim_terms.dtype
    )
    gathered_total = grad_rows_zero + grad_ctx_zero[HALO : HALO + fine_rows]
    gathered_total = gathered_total.at[:HALO].add(neighbour_terms[:HALO])
    gathered_total = gathered_total.at[fine_rows - HALO :].add(neighbour_terms[3 * HALO :])
    grad_feats = gathered_total.astype(jnp.bfloat16)
    stack_in = jnp.stack([sums_zero[0], sums_one[0], sums_two[0]])
    stack_out = jnp.stack([sums_zero[1], sums_one[1], sums_two[1]])
    stack_bias = jnp.stack([sums_zero[2], sums_one[2], sums_two[2]])
    stack_in, stack_out, stack_bias = lax.psum((stack_in, stack_out, stack_bias), ("slab", "grp"))
    inv_root = 1.0 / math.sqrt(fine_rows * groups * lax.axis_size("slab"))
    return (node_out, grad_feats, stack_in * inv_root, stack_out * inv_root, stack_bias * inv_root)


def solution(mesh):
    placed = (
        P(("slab", "grp"), None),
        P(("slab", "grp"), None),
        P(("slab", "grp"), None, None),
        P(("slab", "grp"), None),
        P(("slab", "grp"), None, None),
        P(("slab", "grp"), None),
        P(("slab", "grp")),
        P(("slab", "grp")),
        P(("slab", "grp"), None, None),
        P(("slab", "grp"), None),
        P(("slab", "grp"), None, None),
        P(("slab", "grp"), None),
        P(("slab", "grp")),
        P(("slab", "grp")),
        P(("slab", "grp"), None, None),
        P(("slab", "grp"), None),
        P(),
        P(),
        P(),
    )
    return jax.shard_map(
        body,
        mesh=mesh,
        in_specs=placed,
        out_specs=(P(("slab", "grp"), None), P(("slab", "grp"), None), P(), P(), P()),
        check_vma=False,
    )
```

profile of v0, /device:TPU:0, one launch (start us, length us, event | category | flops | bytes accessed | tf_op | source)
XLA Modules:
  0.0 1015.8 jit_solution(16176194468787256363)
XLA Ops:
  8.3 4.8 collective-permute-start
  20.4 4.9 scatter_custom_fusion
  25.2 7.6 all-to-all-start
  46.9 32.4 %gather_fusion = bf16[1536,64,128]{2,1,0:T(8,128)(2,1)} fusion(bf16[144,64,128]{2,1,0:T(8,128)(2,1)S(1)} %bitcast.259, s32[2048]{0:T(1024)S(1)} %pad_clamp_fusion), kind=kCustom, calls=%fused_computation.8 | custom fusion | bytes 50337792 | tf_op jit(solution)/shard_map/gather | solution.py:32
  79.3 14.4 %convolution_convert_fusion = bf16[128,128,64]{1,2,0:T(8,128)(2,1)S(1)} fusion(bf16[128,64,768]{2,1,0:T(8,128)(2,1)} %param.33, bf16[128,768,128]{2,1,0:T(8,128)(2,1)} %bitcast.261), kind=kOutput, calls=%fused_computation.52 | convolution fusion | flops 1611661312 | bytes 39845888 | tf_op jit(solution)/shard_map/rij,rjh->rih/dot_general | solution.py:33
  105.3 4.6 scatter_custom_fusion.1
  110.0 6.0 all-to-all-start.1
  116.4 7.8 all-to-all-done.1
  134.0 4.2 scatter_custom_fusion.8
  140.1 4.0 all-to-all-start.6
  146.7 5.6 all-to-all-done.6
  156.4 11.7 %all-gather.2.cloned.1.call-done = bf16[4096,128]{1,0:T(8,128)(2,1)} async-done(((bf16[512,128]{1,0:T(8,128)(2,1)}), bf16[4096,128]{1,0:T(8,128)(2,1)}) %all-gather.2.cloned.1.call-update) | async-done | bytes 1048592 | tf_op jit(solution)/shard_map/all_gather | solution.py:189
  181.8 4.6 all-to-all-done.3
  191.0 31.3 %all_gather.7 = bf16[1024,128]{1,0:T(8,128)(2,1)S(1)} all-gather(bf16[128,128]{1,0:T(8,128)(2,1)S(1)} %scatter_custom_fusion.5), channel_id=1, replica_groups=mesh['slab'=4,'grp'=8] {'grp'}, dimensions={0}, use_global_device_ids=true | all-gather | bytes 294912 | tf_op jit(solution)/shard_map/all_gather | solution.py:208
  230.6 60.4 %reduce-scatter.3.cloned.1.call-done = bf16[128,128]{1,0:T(8,128)(2,1)} async-done(((bf16[1024,128]{1,0:T(8,128)(2,1)}), bf16[128,128]{1,0:T(8,128)(2,1)}) %reduce-scatter.3.cloned.1.call-update) | async-done | bytes 32784 | tf_op jit(solution)/shard_map/reduce_scatter | solution.py:259
  294.0 10.3 %all_to_all.58 = bf16[8,32,128]{2,1,0:T(8,128)(2,1)S(1)} all-to-all(bf16[8,32,128]{2,1,0:T(8,128)(2,1)S(1)} %bitcast.300), channel_id=1, replica_groups=mesh['slab'=4,'grp'=8] {'grp'}, dimensions={0} | all-to-all | bytes 131072 | tf_op jit(solution)/shard_map/all_to_all | solution.py:213
  310.6 3.9 all-to-all-done.8
  326.9 7.0 scatter_fusion.4
  346.0 50.3 %reduce-scatter.5.cloned.1.call-done = bf16[512,128]{1,0:T(8,128)(2,1)} async-done(((bf16[4096,128]{1,0:T(8,128)(2,1)}), bf16[512,128]{1,0:T(8,128)(2,1)}) %reduce-scatter.5.cloned.1.call-update) | async-done | bytes 131088 | tf_op jit(solution)/shard_map/reduce_scatter | solution.py:285
  401.6 3.8 all-to-all-start.5
  405.7 7.8 all-to-all-done.5
  432.2 5.4 copy.46
  440.1 20.2 %scatter_fusion.5 = f32[128,64,128]{2,1,0:T(8,128)} fusion(f32[128,64,128]{2,1,0:T(8,128)} %broadcast.231.clone.1, s32[128]{0:T(128)S(1)} %reshape.639, f32[128,64,128]{2,1,0:T(8,128)} %bitcast.267), kind=kCustom, calls=%fused_computation.30 | custom fusion | flops 1048576 | bytes 12583424 | tf_op jit(solution)/shard_map/scatter-add | solution.py:43
  477.1 22.4 %convolution_bitcast_fusion = f32[128,768,128]{1,2,0:T(8,128)} fusion(bf16[128,64,128]{2,1,0:T(8,128)(2,1)} %bitcast.268, bf16[128,64,768]{2,1,0:T(8,128)(2,1)} %param.33), kind=kOutput, calls=%fused_computation.32 | convolution fusion | flops 1610612736 | bytes 65011712 | tf_op jit(solution)/shard_map/rij,rih->rjh/dot_general | solution.py:41
  499.5 48.8 %copy.48 = f32[128,768,128]{2,1,0:T(8,128)} copy(f32[128,768,128]{1,2,0:T(8,128)} %convolution_bitcast_fusion) | data formatting | bytes 100663296 | tf_op jit(solution)/shard_map/rij,rih->rjh/dot_general | solution.py:41
  551.1 232.0 %scatter_fusion.6 = f32[144,64,128]{2,1,0:T(8,128)} fusion(f32[144,64,128]{2,1,0:T(8,128)} %broadcast_in_dim.185, s32[1536]{0:T(1024)S(1)} %reshape.711, f32[1536,64,128]{2,1,0:T(8,128)} %bitcast.260), kind=kCustom, calls=%fused_computation.31 | custom fusion | flops 12582912 | bytes 151001088 | tf_op jit(solution)/shard_map/scatter-add | solution.py:43
  788.9 4.9 fusion.2
  798.7 41.0 %psum.23 = f32[3,128]{1,0:T(4,128)S(1)} all-reduce(f32[3,128]{1,0:T(4,128)S(1)} %pad_maximum_fusion.17), channel_id=1, replica_groups=mesh['slab'=4,'grp'=8] {'slab','grp'}, use_global_device_ids=true, to_apply=%region_30.35 | all-reduce | flops 384 | bytes 3072 | tf_op jit(solution)/shard_map/psum | solution.py:322
  843.4 5.4 copy.42
  851.3 20.2 %scatter_fusion.1 = f32[128,64,128]{2,1,0:T(8,128)} fusion(f32[128,64,128]{2,1,0:T(8,128)} %broadcast.231.clone, s32[128]{0:T(128)S(1)} %reshape.639, f32[128,64,128]{2,1,0:T(8,128)} %bitcast.266), kind=kCustom, calls=%fused_computation.22 | custom fusion | flops 1048576 | bytes 12583424 | tf_op jit(solution)/shard_map/scatter-add | solution.py:43
  871.6 4.0 fusion.3
  884.8 120.6 %all-reduce.3.cloned.1.call-done = (f32[3,256,128]{2,1,0:T(8,128)}, f32[3,128,128]{2,1,0:T(8,128)}) async-done(((f32[3,256,128]{2,1,0:T(8,128)}, f32[3,128,128]{2,1,0:T(8,128)}), (f32[3,256,128]{2,1,0:T(8,128)}, f32[3,128,128]{2,1,0:T(8,128)})) %all-reduce.3.cloned.1.call-update) | async-done | bytes 589840 | tf_op jit(solution)/shard_map/psum | solution.py:322
  (333 shorter events, 186.7 us)
Async XLA Ops:
  8.3 35.8 %collective-permute-start = (bf16[512,128]{1,0:T(8,128)(2,1)S(1)}, bf16[512,128]{1,0:T(8,128)(2,1)S(1)}, u32[]{:S(2)}, u32[]{:S(2)}) collective-permute-start(bf16[512,128]{1,0:T(8,128)(2,1)S(1)} %get-tuple-element.43), channel_id=1, source_target_pairs={{0,1},{1,2},{2,3},{3,4},{4,5},{5,6},{6,7},{8,9},{9,10},{10,11},{11... | collective-permute-start | bytes 393224 | tf_op jit(solution)/shard_map/ppermute | solution.py:19
  13.1 30.9 %collective-permute-start.1 = (bf16[512,128]{1,0:T(8,128)(2,1)S(1)}, bf16[512,128]{1,0:T(8,128)(2,1)}, u32[]{:S(2)}, u32[]{:S(2)}) collective-permute-start(bf16[512,128]{1,0:T(8,128)(2,1)S(1)} %get-tuple-element.44), channel_id=1, source_target_pairs={{1,0},{2,1},{3,2},{4,3},{5,4},{6,5},{7,6},{9,8},{10,9},{11,10},{12... | collective-permute-start | bytes 393224 | tf_op jit(solution)/shard_map/ppermute | solution.py:21
  25.2 84.8 %all-to-all-start = ((s32[8,1,128]{2,1,0:T(1,128)}), s32[8,1,128]{2,1,0:T(1,128)S(1)}, u32[]{:S(2)}, u32[]{:S(2)}) async-start(s32[8,1,128]{2,1,0:T(1,128)} %bitcast.10), calls=%async_computation | async-start | bytes 8192 | tf_op jit(solution)/shard_map/all_to_all | solution.py:186
  105.3 67.3 %copy-start.49 = (bf16[3,128,128]{2,1,0:T(8,128)(2,1)S(1)}, bf16[3,128,128]{2,1,0:T(8,128)(2,1)}, u32[]{:S(2)}) copy-start(bf16[3,128,128]{2,1,0:T(8,128)(2,1)} %param.48) | copy-start | bytes 294916
  110.0 14.2 %all-to-all-start.1 = ((bf16[8,128,128]{2,1,0:T(8,128)(2,1)}), bf16[8,128,128]{2,1,0:T(8,128)(2,1)S(1)}, u32[]{:S(2)}, u32[]{:S(2)}) async-start(bf16[8,128,128]{2,1,0:T(8,128)(2,1)} %bitcast.20), calls=%async_computation.1 | async-start | bytes 524288 | tf_op jit(solution)/shard_map/all_to_all | solution.py:179
  116.0 52.1 %all-gather.2.cloned.1.call-start = ((), (), s32[]{:S(2)}) async-start(), calls=%async_computation.12 | async-start | bytes 1179648 | tf_op jit(solution)/shard_map/all_gather | solution.py:189
  130.4 9.7 all-to-all-start.2
  140.1 12.2 %all-to-all-start.6 = ((bf16[8,128,128]{2,1,0:T(8,128)(2,1)}), bf16[8,128,128]{2,1,0:T(8,128)(2,1)S(1)}, u32[]{:S(2)}, u32[]{:S(2)}) async-start(bf16[8,128,128]{2,1,0:T(8,128)(2,1)} %bitcast.63), calls=%async_computation.6 | async-start | bytes 524288 | tf_op jit(solution)/shard_map/all_to_all | solution.py:230
  176.1 10.3 %all-to-all-start.3 = ((bf16[8,32,128]{2,1,0:T(8,128)(2,1)}), bf16[8,32,128]{2,1,0:T(8,128)(2,1)S(1)}, u32[]{:S(2)}, u32[]{:S(2)}) async-start(bf16[8,32,128]{2,1,0:T(8,128)(2,1)} %bitcast.38), calls=%async_computation.3 | async-start | bytes 131072 | tf_op jit(solution)/shard_map/all_to_all | solution.py:198
  186.4 35.9 %all-to-all-start.7 = ((bf16[8,32,128]{2,1,0:T(8,128)(2,1)}), bf16[8,32,128]{2,1,0:T(8,128)(2,1)S(1)}, u32[]{:S(2)}, u32[]{:S(2)}) async-start(bf16[8,32,128]{2,1,0:T(8,128)(2,1)} %bitcast.69), calls=%async_computation.7 | async-start | bytes 131072 | tf_op jit(solution)/shard_map/all_to_all | solution.py:239
  189.7 101.3 %reduce-scatter.3.cloned.1.call-start = ((), (), s32[]{:S(2)}) async-start(), calls=%async_computation.13 | async-start | bytes 294912 | tf_op jit(solution)/shard_map/reduce_scatter | solution.py:259
  191.0 101.7 %copy-start.21 = (bf16[128,128]{1,0:T(8,128)(2,1)}, bf16[128,128]{1,0:T(8,128)(2,1)S(1)}, u32[]{:S(2)}) copy-start(bf16[128,128]{1,0:T(8,128)(2,1)S(1)} %scatter_custom_fusion.5) | copy-start | bytes 98308
  224.2 85.0 %copy-start.48 = (s32[8,8]{1,0:T(8,128)S(1)}, s32[8,8]{1,0:T(8,128)}, u32[]{:S(2)}) copy-start(s32[8,8]{1,0:T(8,128)} %param.40) | copy-start | bytes 772
  225.9 89.5 %copy-start.25 = (bf16[128,128]{1,0:T(8,128)(2,1)}, bf16[128,128]{1,0:T(8,128)(2,1)S(1)}, u32[]{:S(2)}) copy-start(bf16[128,128]{1,0:T(8,128)(2,1)S(1)} %get-tuple-element.69) | copy-start | bytes 98308
  226.1 64.9 %copy-start.28 = (bf16[128,128]{1,0:T(8,128)(2,1)S(1)}, bf16[128,128]{1,0:T(8,128)(2,1)}, u32[]{:S(2)}) copy-start(bf16[128,128]{1,0:T(8,128)(2,1)} %copy-done.27) | copy-start | bytes 98308
  304.3 10.2 %all-to-all-start.8 = ((bf16[8,32,128]{2,1,0:T(8,128)(2,1)}), bf16[8,32,128]{2,1,0:T(8,128)(2,1)S(1)}, u32[]{:S(2)}, u32[]{:S(2)}) async-start(bf16[8,32,128]{2,1,0:T(8,128)(2,1)} %bitcast.75), calls=%async_computation.9 | async-start | bytes 131072 | tf_op jit(solution)/shard_map/all_to_all | solution.py:262
  307.7 88.6 %reduce-scatter.5.cloned.1.call-start = ((), (), s32[]{:S(2)}) async-start(), calls=%async_computation.14 | async-start | bytes 1179648 | tf_op jit(solution)/shard_map/reduce_scatter | solution.py:285
  342.6 74.4 %copy-start.22 = (bf16[128,128]{1,0:T(8,128)(2,1)S(1)}, bf16[128,128]{1,0:T(8,128)(2,1)}, u32[]{:S(2)}) copy-start(bf16[128,128]{1,0:T(8,128)(2,1)} %copy-done.21) | copy-start | bytes 98308
  342.6 74.4 %copy-start.26 = (bf16[128,128]{1,0:T(8,128)(2,1)S(1)}, bf16[128,128]{1,0:T(8,128)(2,1)}, u32[]{:S(2)}) copy-start(bf16[128,128]{1,0:T(8,128)(2,1)} %copy-done.25) | copy-start | bytes 98308
  342.6 74.4 %copy-start.37 = (bf16[2,128,64]{1,2,0:T(8,128)(2,1)S(1)}, bf16[2,128,64]{1,2,0:T(8,128)(2,1)}, u32[]{:S(2)}) copy-start(bf16[2,128,64]{1,2,0:T(8,128)(2,1)} %copy-done.36) | copy-start | bytes 98308
  342.7 74.6 %copy-start.29 = (bf16[128,128]{1,0:T(8,128)(2,1)S(1)}, bf16[128,128]{1,0:T(8,128)(2,1)}, u32[]{:S(2)}) copy-start(bf16[128,128]{1,0:T(8,128)(2,1)} %copy-done.27) | copy-start | bytes 98308
  342.7 74.6 %copy-start.72 = (f32[128,128]{1,0:T(8,128)S(1)}, f32[128,128]{1,0:T(8,128)}, u32[]{:S(2)}) copy-start(f32[128,128]{1,0:T(8,128)} %copy-done.70) | copy-start | bytes 196612
  342.7 75.4 %copy-start.19 = (bf16[512,128]{1,0:T(8,128)(2,1)S(1)}, bf16[512,128]{1,0:T(8,128)(2,1)}, u32[]{:S(2)}) copy-start(bf16[512,128]{1,0:T(8,128)(2,1)} %scatter_custom_fusion.2) | copy-start | bytes 393220
  342.7 75.4 %copy-start.34 = (bf16[512,128]{1,0:T(8,128)(2,1)S(1)}, bf16[512,128]{1,0:T(8,128)(2,1)}, u32[]{:S(2)}) copy-start(bf16[512,128]{1,0:T(8,128)(2,1)} %copy-done.33) | copy-start | bytes 393220
  342.7 75.4 %copy-start.39 = (bf16[8,128,64]{1,2,0:T(8,128)(2,1)S(1)}, bf16[8,128,64]{1,2,0:T(8,128)(2,1)}, u32[]{:S(2)}) copy-start(bf16[8,128,64]{1,2,0:T(8,128)(2,1)} %copy-done.38) | copy-start | bytes 393220
  342.7 76.3 %copy-start.32 = (bf16[512,128]{1,0:T(8,128)(2,1)S(1)}, bf16[512,128]{1,0:T(8,128)(2,1)}, u32[]{:S(2)}) copy-start(bf16[512,128]{1,0:T(8,128)(2,1)} %copy-done.31) | copy-start | bytes 393220
  346.0 74.9 %copy-start.43 = (s32[1024]{0:T(1024)S(1)}, s32[1024]{0:T(1024)}, u32[]{:S(2)}) copy-start(s32[1024]{0:T(1024)} %get-tuple-element.45) | copy-start | bytes 12292
  401.6 12.0 %all-to-all-start.5 = ((bf16[8,128,128]{2,1,0:T(8,128)(2,1)}), bf16[8,128,128]{2,1,0:T(8,128)(2,1)S(1)}, u32[]{:S(2)}, u32[]{:S(2)}) async-start(bf16[8,128,128]{2,1,0:T(8,128)(2,1)} %bitcast.53), calls=%async_computation.5 | async-start | bytes 524288 | tf_op jit(solution)/shard_map/all_to_all | solution.py:221
  413.6 11.6 %all-to-all-start.9 = ((bf16[8,128,128]{2,1,0:T(8,128)(2,1)}), bf16[8,128,128]{2,1,0:T(8,128)(2,1)S(1)}, u32[]{:S(2)}, u32[]{:S(2)}) async-start(bf16[8,128,128]{2,1,0:T(8,128)(2,1)} %bitcast.85), calls=%async_computation.11 | async-start | bytes 524288 | tf_op jit(solution)/shard_map/all_to_all | solution.py:288
  417.0 588.4 %all-reduce.3.cloned.1.call-start = ((), (), s32[]{:S(2)}) async-start(), calls=%async_computation.15 | async-start | bytes 1179648 | tf_op jit(solution)/shard_map/psum | solution.py:322
  793.8 83.8 %collective-permute-start.2 = (bf16[512,128]{1,0:T(8,128)(2,1)S(1)}, bf16[512,128]{1,0:T(8,128)(2,1)}, u32[]{:S(2)}, u32[]{:S(2)}) collective-permute-start(bf16[512,128]{1,0:T(8,128)(2,1)S(1)} %bitcast.285), channel_id=1, source_target_pairs={{0,1},{1,2},{2,3},{3,4},{4,5},{5,6},{6,7},{8,9},{9,10},{10,11},{11... | collective-permute-start | bytes 393224 | tf_op jit(solution)/shard_map/ppermute | solution.py:19
  797.3 80.3 %collective-permute-start.3 = (bf16[512,128]{1,0:T(8,128)(2,1)S(1)}, bf16[512,128]{1,0:T(8,128)(2,1)}, u32[]{:S(2)}, u32[]{:S(2)}) collective-permute-start(bf16[512,128]{1,0:T(8,128)(2,1)S(1)} %bitcast.288), channel_id=1, source_target_pairs={{1,0},{2,1},{3,2},{4,3},{5,4},{6,5},{7,6},{9,8},{10,9},{11,10},{12... | collective-permute-start | bytes 393224 | tf_op jit(solution)/shard_map/ppermute | solution.py:21
  (60 other events, 1233.5 us)
Sparse Core Ops, SparseCore 0:
  128.1 39.9 all-gather.1
  228.9 62.0 reduce-scatter.2
  335.3 60.9 reduce-scatter.4
  877.2 128.1 all-reduce.2
where the time goes:
time: 1030 us; the launch traced here: 1020 us
  other arithmetic  336 us (33%)
  waiting for transfers between devices  276 us (27%)
  local copies, waits for them, and re-layouts  179 us (17%)
  blocking collectives  82.6 us (8%)
  matrix products  76.4 us (7%)
  starting transfers between devices  49.3 us (5%)
  between operations  16.8 us (2%)
    scatter-add x7, other arithmetic, block_transpose(): jax.ops.segment_sum(spread, columns.reshape(-1), num_segments=targets)  285 us
    psum x1, waiting for transfers between devices, body(): lax.psum((stack_in, stack_out, stack_bias), ('slab', 'grp'))  121 us
    dot_general x7, local copies, waits for them, and re-layouts, block_transpose(): jnp.einsum('rij,rih->rjh', blocks, pieces, preferred_element_type=jnp.flo...  63.6 us
    reduce_scatter x1, waiting for transfers between devices, body(): lax.psum_scatter(grad_ctx_two.astype(jnp.bfloat16), 'grp', scatter_dimens...  60.4 us
    reduce_scatter x1, waiting for transfers between devices, body(): lax.psum_scatter(grad_ctx_one.astype(jnp.bfloat16), 'grp', scatter_dimens...  50.3 us
    psum x1, blocking collectives, body(): lax.psum((stack_in, stack_out, stack_bias), ('slab', 'grp'))  41 us
    gather x7, local copies, waits for them, and re-layouts, block_apply(): picked = tiles[columns].reshape(block_count, span, feature)  41 us
    dot_general x7, matrix products, block_transpose(): jnp.einsum('rij,rih->rjh', blocks, pieces, preferred_element_type=jnp.flo...  33.4 us
  transfers between devices with their start and end apart: 17, of which 11 were waited for; matrix products, arithmetic and copies ran while one was open for 17% of the time, Pallas kernels for 0%

commit v1 on v0

v1 whole, which is shorter than its diff:
```python
import functools
import math

import jax
import jax.numpy as jnp
from jax import lax
from jax.experimental import pallas as pl
from jax.experimental.pallas import tpu as pltpu
from jax.sharding import PartitionSpec as P

BF = jnp.bfloat16
F32 = jnp.float32
HALO = 512
BLK = 64
CHUNK = 8
VMEM_LIMIT = 56 * 1024 * 1024

VM = pl.BlockSpec(memory_space=pltpu.VMEM)
SM = pl.BlockSpec(memory_space=pltpu.SMEM)


def params():
    return pltpu.CompilerParams(vmem_limit_bytes=VMEM_LIMIT)


def cost(flops, nbytes):
    return pl.CostEstimate(flops=int(flops), bytes_accessed=int(nbytes), transcendentals=0)


def dot(a, b):
    return jnp.dot(a, b, preferred_element_type=F32)


def dot_nt(a, b):
    return lax.dot_general(a, b, (((1,), (1,)), ((), ())), preferred_element_type=F32)


def dot_tn(a, b):
    return lax.dot_general(a, b, (((0,), (0,)), ((), ())), preferred_element_type=F32)


def iota(shape, dim):
    return lax.broadcasted_iota(jnp.int32, shape, dim)


def as_ones(mask):
    return jnp.where(mask, 1.0, 0.0).astype(BF)


def tile_at(ref, index):
    return ref[pl.ds(pl.multiple_of(index * BLK, BLK), BLK), :]


def apply_row(block, cols, r, count, ref, shift=0):
    picked = jnp.concatenate([tile_at(ref, cols[r, i] - shift) for i in range(count)], axis=0)
    return dot(block, picked)


def spread_row(block, cols, r, count, rows, acc):
    spread = dot_tn(block, rows)
    for i in range(count):
        at = pl.ds(pl.multiple_of(cols[r, i] * BLK, BLK), BLK)
        acc[at, :] += spread[i * BLK : (i + 1) * BLK]


def place_matrix(row_table, first, count):
    n = row_table.shape[1]
    return as_ones(row_table == iota((count, n), 0) + first)


def prep_kernel(count, cols, owner_ref, pool, cot, place_out, table_out, packed_out, slots_scr, *, groups, balance):
    slots = owner_ref.shape[1]
    cap = slots // groups
    k = cols.shape[1]
    for q in range(pool.shape[0]):
        slots_scr[q * BLK : (q + 1) * BLK, :] = apply_row(pool[q], cols, q, k, cot).astype(BF)
    owner = owner_ref[...]
    live = iota((1, slots), 1) < count[0]
    rows = max(16, groups)
    target = iota((rows, slots), 0)
    low = target * balance
    hit = (owner >= low) & (owner < low + balance) & live
    onehot = jnp.where(hit, 1.0, 0.0)
    upper = as_ones(iota((slots, slots), 0) <= iota((slots, slots), 1))
    running = dot(onehot.astype(BF), upper)
    rank = jnp.sum(onehot * running, axis=0, keepdims=True) - 1.0
    base = jnp.sum(jnp.where(hit, target * cap, 0).astype(F32), axis=0, keepdims=True)
    start = jnp.sum(jnp.where(hit, low, 0).astype(F32), axis=0, keepdims=True)
    place = jnp.where(live, (base + rank).astype(jnp.int32), slots)
    place_out[...] = place
    local = owner - start.astype(jnp.int32) + 1
    kind = iota((rows, slots), 0)
    parts = jnp.where(kind == 0, local >> 5, jnp.where(kind == 1, local & 31, 0)).astype(F32).astype(BF)
    step = min(256, slots)
    for p in range(0, slots, step):
        ones = place_matrix(place, p, step)
        packed_out[p : p + step, :] = dot(ones, slots_scr[...]).astype(BF)
        code = dot_nt(parts, ones)
        table_out[:, p : p + step] = (code[0:1] * 32.0 + code[1:2]).astype(jnp.int32) - 1


def prep(count, cols, owner, pool, cot, groups, balance):
    slots = owner.shape[1]
    feature = cot.shape[1]
    return pl.pallas_call(
        functools.partial(prep_kernel, groups=groups, balance=balance),
        out_shape=(
            jax.ShapeDtypeStruct((1, slots), jnp.int32),
            jax.ShapeDtypeStruct((1, slots), jnp.int32),
            jax.ShapeDtypeStruct((slots, feature), BF),
        ),
        in_specs=[SM, SM, VM, VM, VM],
        out_specs=(VM, VM, VM),
        scratch_shapes=[pltpu.VMEM((slots, feature), BF)],
        compiler_params=params(),
        cost_estimate=cost(2 * slots * slots * 256, 4e6),
        name="prep_slots",
    )(count, cols, owner, pool, cot)


def layer_rows(x, message, w_in, w_out, bias):
    pre = dot(jnp.concatenate([x, message], axis=1), w_in) + bias
    hidden = (pre * jax.nn.sigmoid(pre)).astype(BF)
    return (x.astype(F32) + dot(hidden, w_out)).astype(BF)


def fine_inner_kernel(cols, feats, adj, w_in, w_out, bias, msg_out, res_out, *, rim):
    k = cols.shape[1]
    chunk = pl.program_id(0) + 1
    for j in range(CHUNK):
        block = apply_row(adj[j], cols, chunk * CHUNK + j, k, feats, rim)
        msg_out[j * BLK : (j + 1) * BLK, :] = block.astype(BF)
    rows = CHUNK * BLK
    x = feats[pl.ds(pl.multiple_of(chunk * rows, rows), rows), :]
    res_out[...] = layer_rows(x, msg_out[...], w_in[...], w_out[...], bias[...])


def fine_edge_kernel(cols, feats, prev, after, adj, w_in, w_out, bias, _m, _r, msg_out, res_out, ctx, *, rim):
    k = cols.shape[1]
    total = feats.shape[0]
    blocks = total // BLK
    rows = CHUNK * BLK
    width = rim * BLK
    upper = pl.program_id(0) == 1

    @pl.when(pl.program_id(0) == 0)
    def _():
        ctx[0:width, :] = prev[...]
        ctx[width:, :] = feats[0 : 2 * width, :]

    @pl.when(upper)
    def _():
        ctx[0 : 2 * width, :] = feats[total - 2 * width : total, :]
        ctx[2 * width :, :] = after[...]

    first = jnp.where(upper, blocks - CHUNK, 0)
    for j in range(CHUNK):
        block = apply_row(adj[j], cols, first + j, k, ctx, first)
        msg_out[j * BLK : (j + 1) * BLK, :] = block.astype(BF)
    x = feats[pl.ds(pl.multiple_of(first * BLK, rows), rows), :]
    res_out[...] = layer_rows(x, msg_out[...], w_in[...], w_out[...], bias[...])


def fine_forward(cols, feats, prev, after, adj, w_in, w_out, bias):
    total, feature = feats.shape
    blocks, _, span = adj.shape
    chunks = blocks // CHUNK
    rows = CHUNK * BLK
    rim = HALO // BLK
    out = (jax.ShapeDtypeStruct((total, feature), BF),) * 2
    inner_map = lambda c: (c + 1, 0)
    message, result = pl.pallas_call(
        functools.partial(fine_inner_kernel, rim=rim),
        grid=(chunks - 2,),
        out_shape=out,
        in_specs=[SM, VM, pl.BlockSpec((CHUNK, BLK, span), lambda c: (c + 1, 0, 0)), VM, VM, VM],
        out_specs=(pl.BlockSpec((rows, feature), inner_map),) * 2,
        compiler_params=params(),
        cost_estimate=cost(3e9, 2e7),
        name="fine_inner",
    )(cols, feats, adj, w_in, w_out, bias)
    edge_map = lambda c: (c * (chunks - 1), 0)
    return pl.pallas_call(
        functools.partial(fine_edge_kernel, rim=rim),
        grid=(2,),
        out_shape=out,
        in_specs=[
            SM,
            VM,
            VM,
            VM,
            pl.BlockSpec((CHUNK, BLK, span), lambda c: (c * (chunks - 1), 0, 0)),
            VM,
            VM,
            VM,
            pl.BlockSpec(memory_space=pl.ANY),
            pl.BlockSpec(memory_space=pl.ANY),
        ],
        out_specs=(pl.BlockSpec((rows, feature), edge_map),) * 2,
        scratch_shapes=[pltpu.VMEM((3 * HALO, feature), BF)],
        input_output_aliases={8: 0, 9: 1},
        compiler_params=params(),
        cost_estimate=cost(4e8, 4e6),
        name="fine_edge",
    )(cols, feats, prev, after, adj, w_in, w_out, bias, message, result)


def pool_kernel(cols, place, pool, src, packed_out, slots_scr):
    k = cols.shape[1]
    for q in range(pool.shape[0]):
        slots_scr[q * BLK : (q + 1) * BLK, :] = apply_row(pool[q], cols, q, k, src).astype(BF)
    slots = place.shape[1]
    step = min(256, slots)
    for p in range(0, slots, step):
        packed_out[p : p + step, :] = dot(place_matrix(place[...], p, step), slots_scr[...]).astype(BF)


def pool_pack(cols, place, pool, src):
    slots = place.shape[1]
    feature = src.shape[1]
    return pl.pallas_call(
        pool_kernel,
        out_shape=jax.ShapeDtypeStruct((slots, feature), BF),
        in_specs=[SM, VM, VM, VM],
        out_specs=VM,
        scratch_shapes=[pltpu.VMEM((slots, feature), BF)],
        compiler_params=params(),
        cost_estimate=cost(2 * slots * slots * 128, 3.5e6),
        name="pool_one_pack",
    )(cols, place, pool, src)


def place_kernel(table, got, own_out):
    own_out[...] = dot(place_matrix(table[...], 0, own_out.shape[0]), got[...]).astype(BF)


def place_rows(table, got, balance):
    return pl.pallas_call(
        place_kernel,
        out_shape=jax.ShapeDtypeStruct((balance, got.shape[1]), BF),
        in_specs=[VM, VM],
        out_specs=VM,
        compiler_params=params(),
        cost_estimate=cost(2 * balance * got.size, 1e6),
        name="place_own_one",
    )(table, got)


def place_pool_kernel(cols, count, table, got, pool, own_out, slots_out):
    k = cols.shape[1]
    own_out[...] = dot(place_matrix(table[...], 0, own_out.shape[0]), got[...]).astype(BF)
    for q in range(pool.shape[0]):
        slots_out[q * BLK : (q + 1) * BLK, :] = apply_row(pool[q], cols, q, k, own_out).astype(BF)


def place_pool(cols, count, table, got, pool, balance):
    feature = got.shape[1]
    return pl.pallas_call(
        place_pool_kernel,
        out_shape=(
            jax.ShapeDtypeStruct((balance, feature), BF),
            jax.ShapeDtypeStruct((pool.shape[0] * BLK, feature), BF),
        ),
        in_specs=[SM, SM, VM, VM, VM],
        out_specs=(VM, VM),
        compiler_params=params(),
        cost_estimate=cost(2 * balance * got.size, 1e6),
        name="place_grad_up_one",
    )(cols, count, table, got, pool)


def one_forward_kernel(cols, pool_cols, ctx, own, adj, pool, w_in, w_out, bias, msg_out, res_out, slots_out):
    k = cols.shape[1]
    for r in range(adj.shape[0]):
        msg_out[r * BLK : (r + 1) * BLK, :] = apply_row(adj[r], cols, r, k, ctx).astype(BF)
    res_out[...] = layer_rows(own[...], msg_out[...], w_in[...], w_out[...], bias[...])
    k = pool_cols.shape[1]
    for q in range(pool.shape[0]):
        slots_out[q * BLK : (q + 1) * BLK, :] = apply_row(pool[q], pool_cols, q, k, res_out).astype(BF)


def one_forward(cols, pool_cols, ctx, own, adj, pool, w_in, w_out, bias):
    own_shape = jax.ShapeDtypeStruct(own.shape, BF)
    return pl.pallas_call(
        one_forward_kernel,
        out_shape=(own_shape, own_shape, jax.ShapeDtypeStruct((pool.shape[0] * BLK, own.shape[1]), BF)),
        in_specs=[SM, SM] + [VM] * 7,
        out_specs=(VM, VM, VM),
        compiler_params=params(),
        cost_estimate=cost(2e8, 2.5e6),
        name="level_one_forward",
    )(cols, pool_cols, ctx, own, adj, pool, w_in, w_out, bias)


def grad_pre_rows(grad_low, x, message, w_in, w_out, bias):
    joined = jnp.concatenate([x, message], axis=1)
    pre = dot(joined, w_in) + bias
    sig = jax.nn.sigmoid(pre)
    hidden = (pre * sig).astype(BF)
    grad_pre = dot_nt(grad_low, w_out) * (sig * (1.0 + pre * (1.0 - sig)))
    return joined, hidden, grad_pre


def coarse_kernel(
    me, cols_two, cols_one, pool_cols, slots_two, gslots_two, own_two, mine_two, adj_two, adj_one, pool_two,
    table_one, own_one, msg_one, res_one, gup_one,
    wi1, wo1, b1, wi2, wo2, b2,
    upsend_out, gctx_out, gx_out, dwi1, dwo1, db1, dwi2, dwo2, db2,
    both, xs, gs, ms, hs, gps, rs, ctx_acc, up_acc, gmsg, gctx_acc,
):
    feature = own_one.shape[1]
    n2 = xs.shape[0]
    n1 = own_one.shape[0]
    both[:, :feature] = slots_two[...]
    both[:, feature:] = gslots_two[...]
    table = own_two[...]
    step = min(256, n2)
    for v in range(0, n2, step):
        rows = dot(place_matrix(table, v, step), both[...]).astype(BF)
        xs[v : v + step, :] = rows[:, :feature]
        gs[v : v + step, :] = rows[:, feature:]
    k = cols_two.shape[1]
    for r in range(adj_two.shape[0]):
        ms[r * BLK : (r + 1) * BLK, :] = apply_row(adj_two[r], cols_two, r, k, xs).astype(BF)
    ctx_acc[...] = jnp.zeros_like(ctx_acc)
    for v in range(0, n2, step):
        x, m, g = xs[v : v + step, :], ms[v : v + step, :], gs[v : v + step, :]
        joined, hidden, grad_pre = grad_pre_rows(g, x, m, wi2[...], wo2[...], b2[...])
        rs[v : v + step, :feature] = (x.astype(F32) + dot(hidden, wo2[...])).astype(BF)
        hs[v : v + step, :] = hidden
        gps[v : v + step, :] = grad_pre
        grad_joined = dot_nt(grad_pre.astype(BF), wi2[...])
        ctx_acc[v : v + step, :] += g.astype(F32) + grad_joined[:, :feature]
        gm = grad_joined[:, feature:].astype(BF)
        for j in range(step // BLK):
            r = v // BLK + j
            spread_row(adj_two[r], cols_two, r, k, gm[j * BLK : (j + 1) * BLK], ctx_acc)
    rs[:, feature:] = ctx_acc[...].astype(BF)
    balance = mine_two.shape[1] // 2
    at = pl.ds(pl.multiple_of(me[0] * balance, balance), balance)
    gp_own = gps[at, :]
    joined = jnp.concatenate([xs[at, :], ms[at, :]], axis=1)
    dwi2[...] = dot_tn(joined, gp_own.astype(BF))
    dwo2[...] = dot_tn(hs[at, :], gs[at, :])
    db2[...] = jnp.sum(gp_own, axis=0, keepdims=True)
    mine = place_matrix(mine_two[...], 0, n2)
    back = dot_tn(mine, rs[...]).astype(BF)
    up_acc[:, :feature] = res_one[...].astype(F32)
    up_acc[:, feature:] = gup_one[...].astype(F32)
    k = pool_cols.shape[1]
    for q in range(pool_two.shape[0]):
        spread_row(pool_two[q], pool_cols, q, k, back[q * BLK : (q + 1) * BLK], up_acc)
    ones = place_matrix(table_one[...], 0, n1)
    upsend_out[...] = dot_tn(ones, up_acc[:, :feature].astype(BF)).astype(BF)
    grad = up_acc[:, feature:]
    grad_low = grad.astype(BF)
    joined, hidden, grad_pre = grad_pre_rows(grad_low, own_one[...], msg_one[...], wi1[...], wo1[...], b1[...])
    grad_pre_low = grad_pre.astype(BF)
    dwi1[...] = dot_tn(joined, grad_pre_low)
    dwo1[...] = dot_tn(hidden, grad_low)
    db1[...] = jnp.sum(grad_pre, axis=0, keepdims=True)
    grad_joined = dot_nt(grad_pre_low, wi1[...])
    gx_out[...] = grad + grad_joined[:, :feature]
    gmsg[...] = grad_joined[:, feature:].astype(BF)
    gctx_acc[...] = jnp.zeros_like(gctx_acc)
    k = cols_one.shape[1]
    for r in range(adj_one.shape[0]):
        spread_row(adj_one[r], cols_one, r, k, gmsg[r * BLK : (r + 1) * BLK, :], gctx_acc)
    gctx_out[...] = gctx_acc[...].astype(BF)


def coarse_levels(
    me, cols_two, cols_one, pool_cols, slots_two, gslots_two, own_two, mine_two, adj_two, adj_one, pool_two,
    table_one, own_one, msg_one, res_one, gup_one, wi1, wo1, b1, wi2, wo2, b2, groups,
):
    n1, feature = own_one.shape
    n2 = adj_two.shape[0] * BLK
    slots_one = table_one.shape[1]
    weight_shapes = (
        jax.ShapeDtypeStruct((2 * feature, feature), F32),
        jax.ShapeDtypeStruct((feature, feature), F32),
        jax.ShapeDtypeStruct((1, feature), F32),
    )
    return pl.pallas_call(
        coarse_kernel,
        out_shape=(
            jax.ShapeDtypeStruct((slots_one, feature), BF),
            jax.ShapeDtypeStruct((groups * n1, feature), BF),
            jax.ShapeDtypeStruct((n1, feature), F32),
        )
        + weight_shapes * 2,
        in_specs=[SM] * 4 + [VM] * 18,
        out_specs=(VM,) * 9,
        scratch_shapes=[
            pltpu.VMEM((slots_two.shape[0], 2 * feature), BF),
            pltpu.VMEM((n2, feature), BF),
            pltpu.VMEM((n2, feature), BF),
            pltpu.VMEM((n2, feature), BF),
            pltpu.VMEM((n2, feature), BF),
            pltpu.VMEM((n2, feature), F32),
            pltpu.VMEM((n2, 2 * feature), BF),
            pltpu.VMEM((n2, feature), F32),
            pltpu.VMEM((n1, 2 * feature), F32),
            pltpu.VMEM((n1, feature), BF),
            pltpu.VMEM((groups * n1, feature), F32),
        ],
        compiler_params=params(),
        cost_estimate=cost(4e9, 8e6),
        name="coarse_levels",
    )(
        me, cols_two, cols_one, pool_cols, slots_two, gslots_two, own_two, mine_two, adj_two, adj_one, pool_two,
        table_one, own_one, msg_one, res_one, gup_one, wi1, wo1, b1, wi2, wo2, b2,
    )


def owner_sum_kernel(table, parts, gx, send_out):
    total = gx[...]
    for d in range(parts.shape[0]):
        total += parts[d].astype(F32)
    ones = place_matrix(table[...], 0, gx.shape[0])
    send_out[...] = dot_tn(ones, total.astype(BF)).astype(BF)


def owner_sum(table, parts, gx):
    return pl.pallas_call(
        owner_sum_kernel,
        out_shape=jax.ShapeDtypeStruct((table.shape[1], gx.shape[1]), BF),
        in_specs=[VM, VM, VM],
        out_specs=VM,
        compiler_params=params(),
        cost_estimate=cost(2 * table.shape[1] * gx.size, 2e6),
        name="grad_own_one_send",
    )(table, parts, gx)


def lift(place, got, pool, cols, acc):
    rows = dot_tn(place_matrix(place[...], 0, got.shape[0]), got[...]).astype(BF)
    k = cols.shape[1]
    for q in range(pool.shape[0]):
        spread_row(pool[q], cols, q, k, rows[q * BLK : (q + 1) * BLK], acc)


def node_out_kernel(cols, place, got, pool, base, out, acc):
    rows = out.shape[0]

    @pl.when(pl.program_id(0) == 0)
    def _():
        acc[...] = jnp.zeros_like(acc)
        lift(place, got, pool, cols, acc)

    at = pl.ds(pl.multiple_of(pl.program_id(0) * rows, rows), rows)
    out[...] = (base[...].astype(F32) + acc[at, :]).astype(BF)


def node_out_rows(cols, place, got, pool, base):
    total, feature = base.shape
    rows = 1024
    spec = pl.BlockSpec((rows, feature), lambda c: (c, 0))
    return pl.pallas_call(
        node_out_kernel,
        grid=(total // rows,),
        out_shape=jax.ShapeDtypeStruct((total, feature), BF),
        in_specs=[SM, VM, VM, VM, spec],
        out_specs=spec,
        scratch_shapes=[pltpu.VMEM((total, feature), F32)],
        compiler_params=params(),
        cost_estimate=cost(5e8, 6e6),
        name="node_out",
    )(cols, place, got, pool, base)


def fine_grad_kernel(
    cols, place, got, pool, cot, feats, message, w_in, w_out, bias, gx_out, gmsg_out, dwi, dwo, db, acc
):
    rows = cot.shape[0]
    feature = cot.shape[1]

    @pl.when(pl.program_id(0) == 0)
    def _():
        acc[...] = jnp.zeros_like(acc)
        dwi[...] = jnp.zeros_like(dwi)
        dwo[...] = jnp.zeros_like(dwo)
        db[...] = jnp.zeros_like(db)
        lift(place, got, pool, cols, acc)

    at = pl.ds(pl.multiple_of(pl.program_id(0) * rows, rows), rows)
    grad = cot[...].astype(F32) + acc[at, :]
    grad_low = grad.astype(BF)
    joined, hidden, grad_pre = grad_pre_rows(grad_low, feats[...], message[...], w_in[...], w_out[...], bias[...])
    grad_pre_low = grad_pre.astype(BF)
    dwi[...] += dot_tn(joined, grad_pre_low)
    dwo[...] += dot_tn(hidden, grad_low)
    db[...] += jnp.sum(grad_pre, axis=0, keepdims=True)
    grad_joined = dot_nt(grad_pre_low, w_in[...])
    gx_out[...] = grad + grad_joined[:, :feature]
    gmsg_out[...] = grad_joined[:, feature:].astype(BF)


def fine_grad(cols, place, got, pool, cot, feats, message, w_in, w_out, bias):
    total, feature = cot.shape
    rows = 512
    spec = pl.BlockSpec((rows, feature), lambda c: (c, 0))
    return pl.pallas_call(
        fine_grad_kernel,
        grid=(total // rows,),
        out_shape=(
            jax.ShapeDtypeStruct((total, feature), F32),
            jax.ShapeDtypeStruct((total, feature), BF),
            jax.ShapeDtypeStruct((2 * feature, feature), F32),
            jax.ShapeDtypeStruct((feature, feature), F32),
            jax.ShapeDtypeStruct((1, feature), F32),
        ),
        in_specs=[SM, VM, VM, VM, spec, spec, spec, VM, VM, VM],
        out_specs=(spec, spec, VM, VM, VM),
        scratch_shapes=[pltpu.VMEM((total, feature), F32)],
        compiler_params=params(),
        cost_estimate=cost(3e9, 1.5e7),
        name="fine_layer_backward",
    )(cols, place, got, pool, cot, feats, message, w_in, w_out, bias)


def fine_spread_kernel(cols, adj, gmsg, gx, mid_out, low_out, high_out, acc, *, rim):
    k = cols.shape[1]
    step = pl.program_id(0)
    steps = pl.num_programs(0)
    width = rim * BLK
    rows = CHUNK * BLK
    total = mid_out.shape[0]

    @pl.when(step == 0)
    def _():
        acc[...] = jnp.zeros_like(acc)

    for j in range(CHUNK):
        spread_row(adj[j], cols, step * CHUNK + j, k, gmsg[j * BLK : (j + 1) * BLK, :], acc)
    at = pl.ds(pl.multiple_of(width + step * rows, rows), rows)
    acc[at, :] += gx[...]

    @pl.when(step == steps - 1)
    def _():
        mid_out[...] = acc[width : width + total, :].astype(BF)
        low_out[0:width, :] = acc[0:width, :].astype(BF)
        low_out[width:, :] = acc[width + total :, :].astype(BF)
        high_out[0:width, :] = acc[width : 2 * width, :]
        high_out[width:, :] = acc[total : total + width, :]


def fine_spread(cols, adj, gmsg, gx):
    total, feature = gx.shape
    blocks, _, span = adj.shape
    rows = CHUNK * BLK
    spec = pl.BlockSpec((rows, feature), lambda c: (c, 0))
    return pl.pallas_call(
        functools.partial(fine_spread_kernel, rim=HALO // BLK),
        grid=(blocks // CHUNK,),
        out_shape=(
            jax.ShapeDtypeStruct((total, feature), BF),
            jax.ShapeDtypeStruct((2 * HALO, feature), BF),
            jax.ShapeDtypeStruct((2 * HALO, feature), F32),
        ),
        in_specs=[SM, pl.BlockSpec((CHUNK, BLK, span), lambda c: (c, 0, 0)), spec, spec],
        out_specs=(VM, VM, VM),
        scratch_shapes=[pltpu.VMEM((total + 2 * HALO, feature), F32)],
        compiler_params=params(),
        cost_estimate=cost(2e9, 2.2e7),
        name="fine_spread",
    )(cols, adj, gmsg, gx)


def rim_add_kernel(mid_in, rims, prev, after, out):
    got = jnp.where(pl.program_id(0) == 0, prev[...].astype(F32), after[...].astype(F32))
    out[...] = (rims[...] + got).astype(BF)


def rim_add(mid, rims, prev, after):
    total, feature = mid.shape
    return pl.pallas_call(
        rim_add_kernel,
        grid=(2,),
        out_shape=jax.ShapeDtypeStruct(mid.shape, BF),
        in_specs=[
            pl.BlockSpec(memory_space=pl.ANY),
            pl.BlockSpec((HALO, feature), lambda c: (c, 0)),
            VM,
            VM,
        ],
        out_specs=pl.BlockSpec((HALO, feature), lambda c: (c * (total // HALO - 1), 0)),
        input_output_aliases={0: 0},
        compiler_params=params(),
        cost_estimate=cost(1e6, 1.5e6),
        name="rim_add",
    )(mid, rims, prev, after)


def exchange(parts):
    return lax.all_to_all(parts, "grp", split_axis=0, concat_axis=0, tiled=True)


def gather_rows(rows):
    groups = lax.axis_size("grp")
    got = exchange(jnp.broadcast_to(rows[None], (groups,) + rows.shape))
    return got.reshape((groups * rows.shape[0],) + rows.shape[1:])


def halo_pair(low, high):
    count = lax.axis_size("grp")
    prev = lax.ppermute(high, "grp", [(i, i + 1) for i in range(count - 1)])
    after = lax.ppermute(low, "grp", [(i + 1, i) for i in range(count - 1)])
    return prev, after


def total_over_devices(rows):
    groups = lax.axis_size("grp")
    height = rows.shape[0]
    part = -(-height // (8 * groups)) * 8
    padded = jnp.pad(rows, ((0, part * groups - height), (0, 0)))
    mine = jnp.sum(exchange(padded.reshape(groups, part, rows.shape[1])), axis=0)
    slabs = lax.axis_size("slab")
    hop = 1
    while hop < slabs:
        mine = mine + lax.ppermute(mine, "slab", [(i, i ^ hop) for i in range(slabs)])
        hop *= 2
    return gather_rows(mine)[:height]


def body(
    node_feats,
    cotangent,
    fine_adjacency,
    fine_columns,
    pool_one,
    pool_one_columns,
    count_one,
    owner_one,
    adjacency_one,
    columns_one,
    pool_two,
    pool_two_columns,
    count_two,
    owner_two,
    adjacency_two,
    columns_two,
    weight_in,
    weight_out,
    biases,
):
    groups = lax.axis_size("grp")
    feature = node_feats.shape[1]
    slots_one = owner_one.shape[0]
    balance_one = slots_one // 2
    slots_two = owner_two.shape[0]
    me = lax.axis_index("grp").astype(jnp.int32).reshape(1)
    bias_rows = [biases[level : level + 1] for level in range(3)]

    prev, after = halo_pair(node_feats[:HALO], node_feats[-HALO:])
    adjacency_two_all = lax.all_gather(adjacency_two, "grp", axis=0, tiled=True)
    place_one, table_sent, gslots_send = prep(
        count_one, pool_one_columns, owner_one.reshape(1, slots_one), pool_one, cotangent, groups, balance_one
    )
    mine_two = jnp.where(jnp.arange(slots_two) < count_two[0], owner_two, -1).astype(jnp.int32)
    ints_two = jnp.concatenate([mine_two, columns_two.reshape(-1)])
    ints = exchange(
        jnp.concatenate(
            [table_sent.reshape(groups, -1), jnp.broadcast_to(ints_two[None], (groups, ints_two.shape[0]))], axis=1
        )[:, None, :]
    )[:, 0, :]
    cap_one = slots_one // groups
    table_one = ints[:, :cap_one].reshape(1, slots_one)
    own_two_all = ints[:, cap_one : cap_one + slots_two].reshape(1, groups * slots_two)
    columns_two_all = ints[:, cap_one + slots_two :].reshape(-1, columns_two.shape[1])
    gslots_got = exchange(gslots_send.reshape(groups, cap_one, feature))

    message0, result0 = fine_forward(
        fine_columns, node_feats, prev, after, fine_adjacency, weight_in[0], weight_out[0], bias_rows[0]
    )
    sent_one = pool_pack(pool_one_columns, place_one, pool_one, result0)
    got_one = exchange(sent_one.reshape(groups, cap_one, feature))
    own_one = place_rows(table_one, got_one.reshape(slots_one, feature), balance_one)
    context_one = gather_rows(own_one)

    grad_up_one, gslots_two = place_pool(
        pool_two_columns, count_two, table_one, gslots_got.reshape(slots_one, feature), pool_two, balance_one
    )
    gslots_two_all = gather_rows(gslots_two)

    message_one, result1, coarse_two = one_forward(
        columns_one, pool_two_columns, context_one, own_one, adjacency_one, pool_two,
        weight_in[1], weight_out[1], bias_rows[1],
    )
    coarse_two_all = gather_rows(coarse_two)

    up_send, gctx_one, gx_one, dwi1, dwo1, db1, dwi2, dwo2, db2 = coarse_levels(
        me, columns_two_all, columns_one, pool_two_columns, coarse_two_all, gslots_two_all, own_two_all,
        mine_two.reshape(1, slots_two), adjacency_two_all, adjacency_one, pool_two,
        table_one, own_one, message_one, result1, grad_up_one,
        weight_in[1], weight_out[1], bias_rows[1], weight_in[2], weight_out[2], bias_rows[2], groups,
    )
    gctx_parts = exchange(gctx_one.reshape(groups, balance_one, feature))
    up_got = exchange(up_send.reshape(groups, cap_one, feature)).reshape(slots_one, feature)
    grad_send = owner_sum(table_one, gctx_parts, gx_one)
    grad_got = exchange(grad_send.reshape(groups, cap_one, feature)).reshape(slots_one, feature)
    node_out = node_out_rows(pool_one_columns, place_one, up_got, pool_one, result0)

    coarse_sums = total_over_devices(jnp.concatenate([dwi1, dwo1, dwi2, dwo2, db1, db2], axis=0))

    gx_zero, gmsg_zero, dwi0, dwo0, db0 = fine_grad(
        pool_one_columns, place_one, grad_got, pool_one, cotangent, node_feats, message0,
        weight_in[0], weight_out[0], bias_rows[0],
    )
    fine_sums = total_over_devices(jnp.concatenate([dwi0, dwo0, db0], axis=0))
    mid, rims_out, rims_own = fine_spread(fine_columns, fine_adjacency, gmsg_zero, gx_zero)
    from_prev, from_after = halo_pair(rims_out[:HALO], rims_out[HALO:])
    grad_feats = rim_add(mid, rims_own, from_prev, from_after)

    scale = 1.0 / math.sqrt(node_feats.shape[0] * groups * lax.axis_size("slab"))
    wide = 2 * feature
    level = wide + feature
    grad_in = jnp.stack([fine_sums[:wide], coarse_sums[:wide], coarse_sums[level : level + wide]])
    grad_out = jnp.stack([fine_sums[wide:level], coarse_sums[wide:level], coarse_sums[level + wide : 2 * level]])
    grad_bias = jnp.concatenate([fine_sums[level : level + 1], coarse_sums[2 * level : 2 * level + 2]])
    return (node_out, grad_feats, grad_in * scale, grad_out * scale, grad_bias * scale)


def solution(mesh):
    rows = P(("slab", "grp"), None)
    blocks = P(("slab", "grp"), None, None)
    flat = P(("slab", "grp"))
    placed = (
        rows, rows, blocks, rows, blocks, rows, flat, flat, blocks, rows,
        blocks, rows, flat, flat, blocks, rows, P(), P(), P(),
    )
    return jax.shard_map(
        body,
        mesh=mesh,
        in_specs=placed,
        out_specs=(rows, rows, P(), P(), P()),
        check_vma=False,
    )
```

time: 1030 us -> 337 us (0.33); the launches traced: 1020 us -> 334 us
  other arithmetic: 336 us -> 5.16 us
  waiting for transfers between devices: 276 us -> 91.3 us
  local copies, waits for them, and re-layouts: 179 us -> 19.4 us
  Pallas kernels: 0 us -> 97.7 us
  matrix products: 76.4 us -> 0 us
  blocking collectives: 82.6 us -> 43.8 us
  starting transfers between devices: 49.3 us -> 60.5 us
    scatter-add x9 -> x0, other arithmetic: 288 us -> none  [the longest x7 285 us: block_transpose(): jax.ops.segment_sum(spread, columns.reshape(-1), num_segments=targets)]
    psum x1 -> x0, waiting for transfers between devices: 121 us -> none  [body(): lax.psum((stack_in, stack_out, stack_bias), ('slab', 'grp'))]
    reduce_scatter x2 -> x0, waiting for transfers between devices: 111 us -> none  [the longest x1 60.4 us: body(): lax.psum_scatter(grad_ctx_two.astype(jnp.bfloat16), 'grp', scatter_dimens...]
    pallas_call x0 -> x13, Pallas kernels: none -> 97.7 us  [the longest x1 20.8 us: fine_spread(): pl.pallas_call(functools.partial(fine_spread_kernel, rim=HALO // BLK), gr...]
    dot_general x32 -> x0, matrix products: 76.4 us -> none  [the longest x7 33.4 us: block_transpose(): jnp.einsum('rij,rih->rjh', blocks, pieces, preferred_element_type=jnp.flo...]
    dot_general x7 -> x0, local copies, waits for them, and re-layouts: 63.6 us -> none  [block_transpose(): jnp.einsum('rij,rih->rjh', blocks, pieces, preferred_element_type=jnp.flo...]
    gather x15 -> x0, local copies, waits for them, and re-layouts: 57.4 us -> none  [the longest x7 41 us: block_apply(): picked = tiles[columns].reshape(block_count, span, feature)]
    psum x1 -> x0, blocking collectives: 41 us -> none  [body(): lax.psum((stack_in, stack_out, stack_bias), ('slab', 'grp'))]
  transfers between devices with their start and end apart: 17 -> 20, of which waited for: 11 -> 12; matrix products, arithmetic and copies ran while one was open for 17% -> 4% of each run, Pallas kernels for 0% -> 27%
where the time goes in v1:
time: 337 us; the launch traced here: 334 us
  Pallas kernels  97.7 us (29%)
  waiting for transfers between devices  91.3 us (27%)
  starting transfers between devices  60.5 us (18%)
  blocking collectives  43.8 us (13%)
  local copies, waits for them, and re-layouts  19.4 us (6%)
  between operations  15.7 us (5%)
  other arithmetic  5.16 us (2%)
    all_to_all x11, waiting for transfers between devices, exchange(): return lax.all_to_all(parts, 'grp', split_axis=0, concat_axis=0, tiled=True)  54.6 us
    all_to_all x11, starting transfers between devices, exchange(): return lax.all_to_all(parts, 'grp', split_axis=0, concat_axis=0, tiled=True)  44.6 us
    all_to_all x2, blocking collectives, exchange(): return lax.all_to_all(parts, 'grp', split_axis=0, concat_axis=0, tiled=True)  43.8 us
    all_gather x1, waiting for transfers between devices, body(): adjacency_two_all = lax.all_gather(adjacency_two, 'grp', axis=0, tiled=True)  27.4 us
    pallas_call x1, Pallas kernels, fine_spread(): pl.pallas_call(functools.partial(fine_spread_kernel, rim=HALO // BLK), gr...  20.8 us
    pallas_call x1, Pallas kernels, fine_grad(): pl.pallas_call(fine_grad_kernel, grid=(total // rows,), out_shape=(jax.Sh...  19.2 us
    pallas_call x1, Pallas kernels, fine_forward(): pl.pallas_call(functools.partial(fine_inner_kernel, rim=rim), grid=(chunk...  15.6 us
    ppermute x2, starting transfers between devices, halo_pair(): prev = lax.ppermute(high, 'grp', [(i, i + 1) for i in range(count - 1)])  10 us
  transfers between devices with their start and end apart: 20, of which 12 were waited for; matrix products, arithmetic and copies ran while one was open for 4% of the time, Pallas kernels for 27%

profile of v1, /device:TPU:0, one launch (start us, length us, event | category | flops | bytes accessed | tf_op | source)
XLA Modules:
  0.0 333.7 jit_solution(10779943076134819521)
XLA Ops:
  9.5 5.5 %collective-permute-start = (bf16[512,128]{1,0:T(8,128)(2,1)S(1)}, bf16[512,128]{1,0:T(8,128)(2,1)S(1)}, u32[]{:S(2)}, u32[]{:S(2)}) collective-permute-start(bf16[512,128]{1,0:T(8,128)(2,1)S(1)} %get-tuple-element.64), channel_id=1, source_target_pairs={{0,1},{1,2},{2,3},{3,4},{4,5},{5,6},{6,7},{8,9},{9,10},{10,11},{11... | collective-permute-start | bytes 393224 | tf_op jit(solution)/shard_map/ppermute | solution.py:607
  19.1 4.5 %prep_slots.1 = (s32[1,1024]{1,0:T(1,128)}, s32[1,1024]{1,0:T(1,128)}, bf16[1024,128]{1,0:T(8,128)(2,1)}) custom-call(s32[1]{0:T(128)S(6)} %copy.55.count, s32[16,8]{1,0:T(8,128)} %copy.45.cols, s32[1,1024]{1,0:T(1,128)} %bitcast.78, bf16[16,64,512]{2,1,0:T(8,128)(2,1)} %pool.11, bf16[8192,128]{1,0:T(8,128)(2,1)} %cot.3), custom_call_target="tpu_custom_call" | custom-call | flops 536870912 | bytes 4000000 | tf_op jit(solution)/shard_map/prep_slots/pallas_call | solution.py:105
  24.9 6.2 %all-to-all-start = ((s32[8,1,400]{2,1,0:T(1,128)}), s32[8,1,400]{2,1,0:T(1,128)S(1)}, u32[]{:S(2)}, u32[]{:S(2)}) async-start(s32[8,1,400]{2,1,0:T(1,128)} %broadcast_in_dim.20), calls=%async_computation | async-start | bytes 32768 | tf_op jit(solution)/shard_map/all_to_all | solution.py:596
  33.8 15.6 %fine_inner.1 = (bf16[8192,128]{1,0:T(8,128)(2,1)}, bf16[8192,128]{1,0:T(8,128)(2,1)}) custom-call(s32[128,12]{1,0:T(8,128)} %copy.43.cols, bf16[8192,128]{1,0:T(8,128)(2,1)} %feats.5, bf16[128,64,768]{2,1,0:T(8,128)(2,1)} %adj.7, bf16[256,128]{1,0:T(8,128)(2,1)} %get-tuple-element.72.w_in, bf16[128,128]{1,0:T(8,128)(2,1)} %get-tuple-element.75.w_out, ...), custom_call_target="tpu_custom_call" | custom-call | flops 3000000000 | bytes 20000000 | tf_op jit(solution)/shard_map/fine_inner/pallas_call | solution.py:172
  50.1 4.0 %fine_edge.1 = (bf16[8192,128]{1,0:T(8,128)(2,1)}, bf16[8192,128]{1,0:T(8,128)(2,1)}) custom-call(s32[128,12]{1,0:T(8,128)} %copy.43.cols, bf16[8192,128]{1,0:T(8,128)(2,1)} %feats.5, bf16[512,128]{1,0:T(8,128)(2,1)} %copy-done.8, bf16[512,128]{1,0:T(8,128)(2,1)} %copy-done.7, ...), custom_call_target="tpu_custom_call", output_to_operand_aliasing={{0}: (8, {}), {1}: (9, {})} | custom-call | flops 400000000 | bytes 4000000 | tf_op jit(solution)/shard_map/fine_edge/pallas_call | solution.py:183
  54.1 3.8 %pool_one_pack.1 = bf16[1024,128]{1,0:T(8,128)(2,1)} custom-call(s32[16,8]{1,0:T(8,128)} %copy.45.cols, s32[1,1024]{1,0:T(1,128)} %get-tuple-element.34.place, bf16[16,64,512]{2,1,0:T(8,128)(2,1)} %pool.11, bf16[8192,128]{1,0:T(8,128)(2,1)} %get-tuple-element.38.src.base), custom_call_target="tpu_custom_call" | custom-call | flops 268435456 | bytes 3500000 | tf_op jit(solution)/shard_map/pool_one_pack/pallas_call | solution.py:221
  57.9 14.3 %all_to_all.65 = bf16[8,128,128]{2,1,0:T(8,128)(2,1)} all-to-all(bf16[8,128,128]{2,1,0:T(8,128)(2,1)} %bitcast.62), channel_id=1, replica_groups=mesh['slab'=4,'grp'=8] {'grp'}, dimensions={0} | all-to-all | bytes 524288 | tf_op jit(solution)/shard_map/all_to_all | solution.py:596
  72.2 3.4 %all-to-all-start.4 = ((bf16[8,128,128]{2,1,0:T(8,128)(2,1)}), bf16[8,128,128]{2,1,0:T(8,128)(2,1)S(1)}, u32[]{:S(2)}, u32[]{:S(2)}) async-start(bf16[8,128,128]{2,1,0:T(8,128)(2,1)} %bitcast.13), calls=%async_computation.4 | async-start | bytes 524288 | tf_op jit(solution)/shard_map/all_to_all | solution.py:596
  78.3 5.5 %all-to-all-done.4 = bf16[8,128,128]{2,1,0:T(8,128)(2,1)S(1)} async-done(((bf16[8,128,128]{2,1,0:T(8,128)(2,1)}), bf16[8,128,128]{2,1,0:T(8,128)(2,1)S(1)}, u32[]{:S(2)}, u32[]{:S(2)}) %all-to-all-start.4) | async-done | bytes 262176 | tf_op jit(solution)/shard_map/all_to_all | solution.py:596
  85.9 3.6 %all-to-all-start.2 = ((bf16[8,512,128]{2,1,0:T(8,128)(2,1)}), bf16[8,512,128]{2,1,0:T(8,128)(2,1)S(1)}, u32[]{:S(2)}, u32[]{:S(2)}) async-start(bf16[8,512,128]{2,1,0:T(8,128)(2,1)} %broadcast_in_dim.21), calls=%async_computation.2 | async-start | bytes 2097152 | tf_op jit(solution)/shard_map/all_to_all | solution.py:596
  91.9 20.7 %all-to-all-done.2 = bf16[8,512,128]{2,1,0:T(8,128)(2,1)S(1)} async-done(((bf16[8,512,128]{2,1,0:T(8,128)(2,1)}), bf16[8,512,128]{2,1,0:T(8,128)(2,1)S(1)}, u32[]{:S(2)}, u32[]{:S(2)}) %all-to-all-start.2) | async-done | bytes 1048608 | tf_op jit(solution)/shard_map/all_to_all | solution.py:596
  114.4 3.5 %all-to-all-start.5 = ((bf16[8,256,128]{2,1,0:T(8,128)(2,1)}), bf16[8,256,128]{2,1,0:T(8,128)(2,1)S(1)}, u32[]{:S(2)}, u32[]{:S(2)}) async-start(bf16[8,256,128]{2,1,0:T(8,128)(2,1)} %broadcast_in_dim.23), calls=%async_computation.5 | async-start | bytes 1048576 | tf_op jit(solution)/shard_map/all_to_all | solution.py:596
  118.6 3.0 level_one_forward.1
  121.7 9.5 %all-to-all-done.5 = bf16[8,256,128]{2,1,0:T(8,128)(2,1)S(1)} async-done(((bf16[8,256,128]{2,1,0:T(8,128)(2,1)}), bf16[8,256,128]{2,1,0:T(8,128)(2,1)S(1)}, u32[]{:S(2)}, u32[]{:S(2)}) %all-to-all-start.5) | async-done | bytes 524320 | tf_op jit(solution)/shard_map/all_to_all | solution.py:596
  132.9 3.7 %all-to-all-start.3 = ((bf16[8,256,128]{2,1,0:T(8,128)(2,1)}), bf16[8,256,128]{2,1,0:T(8,128)(2,1)S(1)}, u32[]{:S(2)}, u32[]{:S(2)}) async-start(bf16[8,256,128]{2,1,0:T(8,128)(2,1)} %broadcast_in_dim.22), calls=%async_computation.3 | async-start | bytes 1048576 | tf_op jit(solution)/shard_map/all_to_all | solution.py:596
  137.9 27.4 %all-gather.2.cloned.1.call-done.adj_two = bf16[16,64,512]{2,1,0:T(8,128)(2,1)} async-done(((bf16[2,64,512]{2,1,0:T(8,128)(2,1)}), bf16[16,64,512]{2,1,0:T(8,128)(2,1)}) %all-gather.2.cloned.1.call-update) | async-done | bytes 1048592 | tf_op jit(solution)/shard_map/all_gather | solution.py:656
  166.1 9.1 %coarse_levels.1 = (bf16[1024,128]{1,0:T(8,128)(2,1)}, bf16[4096,128]{1,0:T(8,128)(2,1)}, f32[512,128]{1,0:T(8,128)}, f32[256,128]{1,0:T(8,128)}, f32[128,128]{1...) custom-call(s32[1]{0:T(128)} %bitcast.1.me, ...), custom_call_target="tpu_custom_call" | custom-call | flops 4000000000 | bytes 8000000 | tf_op jit(solution)/shard_map/coarse_levels/pallas_call | solution.py:384
  175.3 29.5 %all_to_all.66.parts = bf16[8,512,128]{2,1,0:T(8,128)(2,1)} all-to-all(bf16[8,512,128]{2,1,0:T(8,128)(2,1)} %bitcast.60), channel_id=1, replica_groups=mesh['slab'=4,'grp'=8] {'grp'}, dimensions={0} | all-to-all | bytes 2097152 | tf_op jit(solution)/shard_map/all_to_all | solution.py:596
  204.7 3.5 %all-to-all-start.6 = ((bf16[8,128,128]{2,1,0:T(8,128)(2,1)}), bf16[8,128,128]{2,1,0:T(8,128)(2,1)S(1)}, u32[]{:S(2)}, u32[]{:S(2)}) async-start(bf16[8,128,128]{2,1,0:T(8,128)(2,1)} %bitcast.19), calls=%async_computation.6 | async-start | bytes 524288 | tf_op jit(solution)/shard_map/all_to_all | solution.py:596
  210.9 5.9 %all-to-all-done.6 = bf16[8,128,128]{2,1,0:T(8,128)(2,1)S(1)} async-done(((bf16[8,128,128]{2,1,0:T(8,128)(2,1)}), bf16[8,128,128]{2,1,0:T(8,128)(2,1)S(1)}, u32[]{:S(2)}, u32[]{:S(2)}) %all-to-all-start.6) | async-done | bytes 262176 | tf_op jit(solution)/shard_map/all_to_all | solution.py:596
  216.8 3.5 %all-to-all-start.8 = ((bf16[8,128,128]{2,1,0:T(8,128)(2,1)}), bf16[8,128,128]{2,1,0:T(8,128)(2,1)S(1)}, u32[]{:S(2)}, u32[]{:S(2)}) async-start(bf16[8,128,128]{2,1,0:T(8,128)(2,1)} %bitcast.61), calls=%async_computation.8 | async-start | bytes 524288 | tf_op jit(solution)/shard_map/all_to_all | solution.py:596
  221.2 7.6 %all-to-all-done.8 = bf16[8,128,128]{2,1,0:T(8,128)(2,1)S(1)} async-done(((bf16[8,128,128]{2,1,0:T(8,128)(2,1)}), bf16[8,128,128]{2,1,0:T(8,128)(2,1)S(1)}, u32[]{:S(2)}, u32[]{:S(2)}) %all-to-all-start.8) | async-done | bytes 262176 | tf_op jit(solution)/shard_map/all_to_all | solution.py:596
  228.8 3.5 %all-to-all-start.11 = ((f32[8,104,128]{2,1,0:T(8,128)}), f32[8,104,128]{2,1,0:T(8,128)S(1)}, u32[]{:S(2)}, u32[]{:S(2)}) async-start(f32[8,104,128]{2,1,0:T(8,128)} %bitcast.27), calls=%async_computation.11 | async-start | bytes 851968 | tf_op jit(solution)/shard_map/all_to_all | solution.py:596
  232.3 19.2 %fine_layer_backward.1 = (f32[8192,128]{1,0:T(8,128)}, bf16[8192,128]{1,0:T(8,128)(2,1)}, f32[256,128]{1,0:T(8,128)}, f32[128,128]{1,0:T(8,128)}, f32[1,128]{1,0:T(1,128)}) custom-call(s32[16,8]{1,0:T(8,128)} %copy.45.cols, s32[1,1024]{1,0:T(1,128)} %get-tuple-element.34.place, bf16[1024,128]{1,0:T(8,128)(2,1)} %bitcast.68, bf16[16,64,512]{2,1,0:T(8,128)(2,1)} %pool.11, ...), custom_call_target="tpu_custom_call" | custom-call | flops 3000000000 | bytes 15000000 | tf_op jit(solution)/shard_map/fine_layer_backward/pallas_call | solution.py:503
  253.2 6.0 %all-to-all-start.9 = ((f32[8,56,128]{2,1,0:T(8,128)}), f32[8,56,128]{2,1,0:T(8,128)S(1)}, u32[]{:S(2)}, u32[]{:S(2)}) async-start(f32[8,56,128]{2,1,0:T(8,128)} %bitcast.24), calls=%async_computation.9 | async-start | bytes 458752 | tf_op jit(solution)/shard_map/all_to_all | solution.py:596
  268.0 3.7 %all-to-all-start.12 = ((f32[8,104,128]{2,1,0:T(8,128)}), f32[8,104,128]{2,1,0:T(8,128)S(1)}, u32[]{:S(2)}, u32[]{:S(2)}) async-start(f32[8,104,128]{2,1,0:T(8,128)} %broadcast_in_dim.25), calls=%async_computation.12 | async-start | bytes 851968 | tf_op jit(solution)/shard_map/all_to_all | solution.py:596
  271.7 8.8 %node_out.1 = bf16[8192,128]{1,0:T(8,128)(2,1)} custom-call(s32[16,8]{1,0:T(8,128)} %copy.45.cols, s32[1,1024]{1,0:T(1,128)} %get-tuple-element.34.place, bf16[1024,128]{1,0:T(8,128)(2,1)} %bitcast.58, bf16[16,64,512]{2,1,0:T(8,128)(2,1)} %pool.11, bf16[8192,128]{1,0:T(8,128)(2,1)} %get-tuple-element.38.src.base), custom_call_target="tpu_custom_call" | custom-call | flops 500000000 | bytes 6000000 | tf_op jit(solution)/shard_map/node_out/pallas_call | solution.py:459
  280.5 2.9 all-to-all-done.12
  285.0 20.8 %fine_spread.1 = (bf16[8192,128]{1,0:T(8,128)(2,1)}, bf16[1024,128]{1,0:T(8,128)(2,1)}, f32[1024,128]{1,0:T(8,128)}) custom-call(s32[128,12]{1,0:T(8,128)} %copy.43.cols, bf16[128,64,768]{2,1,0:T(8,128)(2,1)} %adj.7, bf16[8192,128]{1,0:T(8,128)(2,1)} %get-tuple-element.49.gmsg, f32[8192,128]{1,0:T(8,128)} %get-tuple-element.50.gx), custom_call_target="tpu_custom_call" | custom-call | flops 2000000000 | bytes 22000000 | tf_op jit(solution)/shard_map/fine_spread/pallas_call | solution.py:553
  306.5 4.1 %all-to-all-start.10 = ((f32[8,56,128]{2,1,0:T(8,128)}), f32[8,56,128]{2,1,0:T(8,128)S(1)}, u32[]{:S(2)}, u32[]{:S(2)}) async-start(f32[8,56,128]{2,1,0:T(8,128)} %broadcast_in_dim.24), calls=%async_computation.10 | async-start | bytes 458752 | tf_op jit(solution)/shard_map/all_to_all | solution.py:596
  312.8 4.6 %collective-permute-start.2 = (bf16[512,128]{1,0:T(8,128)(2,1)S(1)}, bf16[512,128]{1,0:T(8,128)(2,1)S(1)}, u32[]{:S(2)}, u32[]{:S(2)}) collective-permute-start(bf16[512,128]{1,0:T(8,128)(2,1)S(1)} %get-tuple-element.70), channel_id=1, source_target_pairs={{0,1},{1,2},{2,3},{3,4},{4,5},{5,6},{6,7},{8,9},{9,10},{10,11},{11... | collective-permute-start | bytes 393224 | tf_op jit(solution)/shard_map/ppermute | solution.py:607
  319.6 2.7 collective-permute-done.2.prev
  (108 shorter events, 48.6 us)
Async XLA Ops:
  7.2 24.6 %copy-start.16 = (s32[128,12]{0,1:T(8,128)S(1)}, s32[128,12]{0,1:T(8,128)}, u32[]{:S(2)}) copy-start(s32[128,12]{0,1:T(8,128)} %param.22) | copy-start | bytes 18436
  7.2 25.3 %copy-start.13 = (bf16[3,128,128]{2,1,0:T(8,128)(2,1)S(1)}, bf16[3,128,128]{2,1,0:T(8,128)(2,1)}, u32[]{:S(2)}) copy-start(bf16[3,128,128]{2,1,0:T(8,128)(2,1)} %param.36) | copy-start | bytes 294916
  7.2 25.9 %copy-start.6 = (bf16[3,256,128]{2,1,0:T(8,128)(2,1)S(1)}, bf16[3,256,128]{2,1,0:T(8,128)(2,1)}, u32[]{:S(2)}) copy-start(bf16[3,256,128]{2,1,0:T(8,128)(2,1)} %param.35) | copy-start | bytes 589828
  8.2 41.1 %collective-permute-start.1 = (bf16[512,128]{1,0:T(8,128)(2,1)S(1)}, bf16[512,128]{1,0:T(8,128)(2,1)S(1)}, u32[]{:S(2)}, u32[]{:S(2)}) collective-permute-start(bf16[512,128]{1,0:T(8,128)(2,1)S(1)} %get-tuple-element.63), channel_id=1, source_target_pairs={{1,0},{2,1},{3,2},{4,3},{5,4},{6,5},{7,6},{9,8},{10,9},{11,10},{12... | collective-permute-start | bytes 393224 | tf_op jit(solution)/shard_map/ppermute | solution.py:608
  9.5 39.9 %collective-permute-start = (bf16[512,128]{1,0:T(8,128)(2,1)S(1)}, bf16[512,128]{1,0:T(8,128)(2,1)S(1)}, u32[]{:S(2)}, u32[]{:S(2)}) collective-permute-start(bf16[512,128]{1,0:T(8,128)(2,1)S(1)} %get-tuple-element.64), channel_id=1, source_target_pairs={{0,1},{1,2},{2,3},{3,4},{4,5},{5,6},{6,7},{8,9},{9,10},{10,11},{11... | collective-permute-start | bytes 393224 | tf_op jit(solution)/shard_map/ppermute | solution.py:607
  19.1 30.3 %copy-start.17 = (s32[256]{0:T(256)}, s32[256]{0:T(256)S(1)}, u32[]{:S(2)}) copy-start(s32[256]{0:T(256)S(1)} %compare_select_fusion) | copy-start | bytes 3076
  24.9 32.9 %all-to-all-start = ((s32[8,1,400]{2,1,0:T(1,128)}), s32[8,1,400]{2,1,0:T(1,128)S(1)}, u32[]{:S(2)}, u32[]{:S(2)}) async-start(s32[8,1,400]{2,1,0:T(1,128)} %broadcast_in_dim.20), calls=%async_computation | async-start | bytes 32768 | tf_op jit(solution)/shard_map/all_to_all | solution.py:596
  72.2 11.6 %all-to-all-start.4 = ((bf16[8,128,128]{2,1,0:T(8,128)(2,1)}), bf16[8,128,128]{2,1,0:T(8,128)(2,1)S(1)}, u32[]{:S(2)}, u32[]{:S(2)}) async-start(bf16[8,128,128]{2,1,0:T(8,128)(2,1)} %bitcast.13), calls=%async_computation.4 | async-start | bytes 524288 | tf_op jit(solution)/shard_map/all_to_all | solution.py:596
  85.9 26.7 %all-to-all-start.2 = ((bf16[8,512,128]{2,1,0:T(8,128)(2,1)}), bf16[8,512,128]{2,1,0:T(8,128)(2,1)S(1)}, u32[]{:S(2)}, u32[]{:S(2)}) async-start(bf16[8,512,128]{2,1,0:T(8,128)(2,1)} %broadcast_in_dim.21), calls=%async_computation.2 | async-start | bytes 2097152 | tf_op jit(solution)/shard_map/all_to_all | solution.py:596
  114.4 16.8 %all-to-all-start.5 = ((bf16[8,256,128]{2,1,0:T(8,128)(2,1)}), bf16[8,256,128]{2,1,0:T(8,128)(2,1)S(1)}, u32[]{:S(2)}, u32[]{:S(2)}) async-start(bf16[8,256,128]{2,1,0:T(8,128)(2,1)} %broadcast_in_dim.23), calls=%async_computation.5 | async-start | bytes 1048576 | tf_op jit(solution)/shard_map/all_to_all | solution.py:596
  117.9 47.4 %all-gather.2.cloned.1.call-start = ((), (), s32[]{:S(2)}) async-start(), calls=%async_computation.13 | async-start | bytes 1179648 | tf_op jit(solution)/shard_map/all_gather | solution.py:656
  131.2 34.1 %copy-start.3 = (bf16[8,256,128]{2,1,0:T(8,128)(2,1)}, bf16[8,256,128]{2,1,0:T(8,128)(2,1)S(1)}, u32[]{:S(2)}) copy-start(bf16[8,256,128]{2,1,0:T(8,128)(2,1)S(1)} %all-to-all-done.5) | copy-start | bytes 1572868
  132.9 32.3 %all-to-all-start.3 = ((bf16[8,256,128]{2,1,0:T(8,128)(2,1)}), bf16[8,256,128]{2,1,0:T(8,128)(2,1)S(1)}, u32[]{:S(2)}, u32[]{:S(2)}) async-start(bf16[8,256,128]{2,1,0:T(8,128)(2,1)} %broadcast_in_dim.22), calls=%async_computation.3 | async-start | bytes 1048576 | tf_op jit(solution)/shard_map/all_to_all | solution.py:596
  175.2 45.1 %copy-start.11 = (f32[256,128]{1,0:T(8,128)S(1)}, f32[256,128]{1,0:T(8,128)}, u32[]{:S(2)}) copy-start(f32[256,128]{1,0:T(8,128)} %get-tuple-element.57) | copy-start | bytes 393220
  175.2 45.1 %copy-start.12 = (f32[256,128]{1,0:T(8,128)S(1)}, f32[256,128]{1,0:T(8,128)}, u32[]{:S(2)}) copy-start(f32[256,128]{1,0:T(8,128)} %get-tuple-element.59) | copy-start | bytes 393220
  175.2 45.1 %copy-start.14 = (f32[128,128]{1,0:T(8,128)S(1)}, f32[128,128]{1,0:T(8,128)}, u32[]{:S(2)}) copy-start(f32[128,128]{1,0:T(8,128)} %get-tuple-element.58) | copy-start | bytes 196612
  175.2 45.1 %copy-start.15 = (f32[128,128]{1,0:T(8,128)S(1)}, f32[128,128]{1,0:T(8,128)}, u32[]{:S(2)}) copy-start(f32[128,128]{1,0:T(8,128)} %get-tuple-element.60) | copy-start | bytes 196612
  175.2 45.1 %copy-start.19 = (f32[1,128]{1,0:T(1,128)S(1)}, f32[1,128]{1,0:T(1,128)}, u32[]{:S(2)}) copy-start(f32[1,128]{1,0:T(1,128)} %get-tuple-element.61) | copy-start | bytes 1540
  175.3 45.1 %copy-start.20 = (f32[1,128]{1,0:T(1,128)S(1)}, f32[1,128]{1,0:T(1,128)}, u32[]{:S(2)}) copy-start(f32[1,128]{1,0:T(1,128)} %get-tuple-element.62) | copy-start | bytes 1540
  204.7 12.1 %all-to-all-start.6 = ((bf16[8,128,128]{2,1,0:T(8,128)(2,1)}), bf16[8,128,128]{2,1,0:T(8,128)(2,1)S(1)}, u32[]{:S(2)}, u32[]{:S(2)}) async-start(bf16[8,128,128]{2,1,0:T(8,128)(2,1)} %bitcast.19), calls=%async_computation.6 | async-start | bytes 524288 | tf_op jit(solution)/shard_map/all_to_all | solution.py:596
  216.8 34.8 %copy-start.1 = (bf16[8,128,128]{2,1,0:T(8,128)(2,1)}, bf16[8,128,128]{2,1,0:T(8,128)(2,1)S(1)}, u32[]{:S(2)}) copy-start(bf16[8,128,128]{2,1,0:T(8,128)(2,1)S(1)} %all-to-all-done.6) | copy-start | bytes 786436
  216.8 12.0 %all-to-all-start.8 = ((bf16[8,128,128]{2,1,0:T(8,128)(2,1)}), bf16[8,128,128]{2,1,0:T(8,128)(2,1)S(1)}, u32[]{:S(2)}, u32[]{:S(2)}) async-start(bf16[8,128,128]{2,1,0:T(8,128)(2,1)} %bitcast.61), calls=%async_computation.8 | async-start | bytes 524288 | tf_op jit(solution)/shard_map/all_to_all | solution.py:596
  228.8 24.4 %all-to-all-start.11 = ((f32[8,104,128]{2,1,0:T(8,128)}), f32[8,104,128]{2,1,0:T(8,128)S(1)}, u32[]{:S(2)}, u32[]{:S(2)}) async-start(f32[8,104,128]{2,1,0:T(8,128)} %bitcast.27), calls=%async_computation.11 | async-start | bytes 851968 | tf_op jit(solution)/shard_map/all_to_all | solution.py:596
  253.2 14.0 %all-to-all-start.9 = ((f32[8,56,128]{2,1,0:T(8,128)}), f32[8,56,128]{2,1,0:T(8,128)S(1)}, u32[]{:S(2)}, u32[]{:S(2)}) async-start(f32[8,56,128]{2,1,0:T(8,128)} %bitcast.24), calls=%async_computation.9 | async-start | bytes 458752 | tf_op jit(solution)/shard_map/all_to_all | solution.py:596
  259.2 1.3 collective-permute-start.6
  260.5 4.2 %collective-permute-start.7 = (f32[104,128]{1,0:T(8,128)S(1)}, f32[104,128]{1,0:T(8,128)S(1)}, u32[]{:S(2)}, u32[]{:S(2)}) collective-permute-start(f32[104,128]{1,0:T(8,128)S(1)} %add.18), channel_id=1, source_target_pairs={{0,16},{8,24},{16,0},{24,8},{1,17},{9,25},{17,1},{25,9},{2,18},{10... | collective-permute-start | bytes 159752 | tf_op jit(solution)/shard_map/ppermute | solution.py:621
  268.0 15.4 %all-to-all-start.12 = ((f32[8,104,128]{2,1,0:T(8,128)}), f32[8,104,128]{2,1,0:T(8,128)S(1)}, u32[]{:S(2)}, u32[]{:S(2)}) async-start(f32[8,104,128]{2,1,0:T(8,128)} %broadcast_in_dim.25), calls=%async_computation.12 | async-start | bytes 851968 | tf_op jit(solution)/shard_map/all_to_all | solution.py:596
  280.5 3.0 collective-permute-start.4
  283.5 22.3 %collective-permute-start.5 = (f32[56,128]{1,0:T(8,128)S(1)}, f32[56,128]{1,0:T(8,128)S(1)}, u32[]{:S(2)}, u32[]{:S(2)}) collective-permute-start(f32[56,128]{1,0:T(8,128)S(1)} %add.16), channel_id=1, source_target_pairs={{0,16},{8,24},{16,0},{24,8},{1,17},{9,25},{17,1},{25,9},{2,18},{10... | collective-permute-start | bytes 86024 | tf_op jit(solution)/shard_map/ppermute | solution.py:621
  306.5 18.2 %all-to-all-start.10 = ((f32[8,56,128]{2,1,0:T(8,128)}), f32[8,56,128]{2,1,0:T(8,128)S(1)}, u32[]{:S(2)}, u32[]{:S(2)}) async-start(f32[8,56,128]{2,1,0:T(8,128)} %broadcast_in_dim.24), calls=%async_computation.10 | async-start | bytes 458752 | tf_op jit(solution)/shard_map/all_to_all | solution.py:596
  311.5 8.0 %collective-permute-start.3 = (bf16[512,128]{1,0:T(8,128)(2,1)S(1)}, bf16[512,128]{1,0:T(8,128)(2,1)S(1)}, u32[]{:S(2)}, u32[]{:S(2)}) collective-permute-start(bf16[512,128]{1,0:T(8,128)(2,1)S(1)} %get-tuple-element.69), channel_id=1, source_target_pairs={{1,0},{2,1},{3,2},{4,3},{5,4},{6,5},{7,6},{9,8},{10,9},{11,10},{12... | collective-permute-start | bytes 393224 | tf_op jit(solution)/shard_map/ppermute | solution.py:608
  312.8 9.4 %collective-permute-start.2 = (bf16[512,128]{1,0:T(8,128)(2,1)S(1)}, bf16[512,128]{1,0:T(8,128)(2,1)S(1)}, u32[]{:S(2)}, u32[]{:S(2)}) collective-permute-start(bf16[512,128]{1,0:T(8,128)(2,1)S(1)} %get-tuple-element.70), channel_id=1, source_target_pairs={{0,1},{1,2},{2,3},{3,4},{4,5},{5,6},{6,7},{8,9},{9,10},{10,11},{11... | collective-permute-start | bytes 393224 | tf_op jit(solution)/shard_map/ppermute | solution.py:607
  (9 other events, 44.6 us)
Sparse Core Ops, SparseCore 0:
  120.8 44.4 all-gather.1

commit v2 on v1

v2 whole, which is shorter than its diff:
```python
import functools
import math

import jax
import jax.numpy as jnp
from jax import lax
from jax.experimental import pallas as pl
from jax.experimental.pallas import tpu as pltpu
from jax.sharding import PartitionSpec as P

BF = jnp.bfloat16
F32 = jnp.float32
HALO = 512
BLK = 64
CHUNK = 8
EXTRA = 16
VMEM_LIMIT = 56 * 1024 * 1024

VM = pl.BlockSpec(memory_space=pltpu.VMEM)
SM = pl.BlockSpec(memory_space=pltpu.SMEM)


def params():
    return pltpu.CompilerParams(vmem_limit_bytes=VMEM_LIMIT)


def takes(microseconds):
    return pl.CostEstimate(flops=0, bytes_accessed=int(3 * microseconds * 3.69e6), transcendentals=0)


def dot(a, b):
    return jnp.dot(a, b, preferred_element_type=F32)


def dot_nt(a, b):
    return lax.dot_general(a, b, (((1,), (1,)), ((), ())), preferred_element_type=F32)


def dot_tn(a, b):
    return lax.dot_general(a, b, (((0,), (0,)), ((), ())), preferred_element_type=F32)


def iota(shape, dim):
    return lax.broadcasted_iota(jnp.int32, shape, dim)


def as_ones(mask):
    return jnp.where(mask, 1.0, 0.0).astype(BF)


def tile_at(ref, index):
    return ref[pl.ds(pl.multiple_of(index * BLK, BLK), BLK), :]


def apply_row(block, cols, r, count, ref, shift=0):
    picked = jnp.concatenate([tile_at(ref, cols[r, i] - shift) for i in range(count)], axis=0)
    return dot(block, picked)


def spread_row(block, cols, r, count, rows, acc, shift=0):
    spread = dot_tn(block, rows)
    for i in range(count):
        at = pl.ds(pl.multiple_of((cols[r, i] - shift) * BLK, BLK), BLK)
        acc[at, :] += spread[i * BLK : (i + 1) * BLK]


def place_matrix(row_table, first, count):
    n = row_table.shape[1]
    return as_ones(row_table == iota((count, n), 0) + first)


def digits(values):
    shifted = values + 1
    return (shifted >> 6).astype(F32), (shifted & 63).astype(F32)


def from_digits(high, low):
    return (high.astype(F32) * 64.0 + low.astype(F32)).astype(jnp.int32) - 1


def lane_rows(values):
    n = values.shape[1]
    rows = []
    for at in range(0, n, 128):
        row = values[:, at : min(at + 128, n)]
        if row.shape[1] < 128:
            row = jnp.concatenate([row, jnp.zeros((1, 128 - row.shape[1]), F32)], axis=1)
        rows.append(row)
    return rows


def prep_kernel(
    count, cols, count_two, owner_ref, two_ref, cols_two, pool, cot, adj_two, place_out, mine_out, send_out, slots_scr,
    *, groups, balance,
):
    slots = owner_ref.shape[1]
    cap = slots // groups
    k = cols.shape[1]
    for q in range(pool.shape[0]):
        slots_scr[q * BLK : (q + 1) * BLK, :] = apply_row(pool[q], cols, q, k, cot).astype(BF)
    owner = owner_ref[...]
    live = iota((1, slots), 1) < count[0]
    rows = max(16, groups)
    target = iota((rows, slots), 0)
    low = target * balance
    hit = (owner >= low) & (owner < low + balance) & live
    onehot = jnp.where(hit, 1.0, 0.0)
    upper = as_ones(iota((slots, slots), 0) <= iota((slots, slots), 1))
    running = dot(onehot.astype(BF), upper)
    rank = jnp.sum(onehot * running, axis=0, keepdims=True) - 1.0
    base = jnp.sum(jnp.where(hit, target * cap, 0).astype(F32), axis=0, keepdims=True)
    start = jnp.sum(jnp.where(hit, low, 0).astype(F32), axis=0, keepdims=True)
    place = jnp.where(live, (base + rank).astype(jnp.int32), slots)
    place_out[...] = place
    two = two_ref[...]
    two = jnp.where(iota(two.shape, 1) < count_two[0], two, -1)
    mine_out[...] = two
    two_high, two_low = digits(two)
    shared = lane_rows(two_high) + lane_rows(two_low) + lane_rows(cols_two[...].astype(F32))
    local_high, local_low = digits(owner - start.astype(jnp.int32))
    kind = iota((rows, slots), 0)
    parts = jnp.where(kind == 0, local_high, jnp.where(kind == 1, local_low, 0.0)).astype(BF)
    for d in range(groups):
        ones = place_matrix(place, d * cap, cap)
        send_out[d, 0:cap, :] = dot(ones, slots_scr[...]).astype(BF)
        code = dot_nt(parts, ones)
        if cap < 128:
            code = jnp.concatenate([code, jnp.zeros((rows, 128 - cap), F32)], axis=1)
        tail = [code[0:1], code[1:2]] + shared
        tail = jnp.concatenate(tail + [jnp.zeros((EXTRA - len(tail), 128), F32)], axis=0)
        send_out[d, cap : cap + EXTRA, :] = tail.astype(BF)
        at = cap + EXTRA
        for r in range(adj_two.shape[0]):
            for c in range(0, adj_two.shape[2], 128):
                send_out[d, at : at + BLK, :] = adj_two[r, :, c : c + 128]
                at += BLK


def prep(count, cols, count_two, owner, two, cols_two, pool, cot, adj_two, groups, balance):
    slots = owner.shape[1]
    feature = cot.shape[1]
    height = slots // groups + EXTRA + adj_two.size // 128
    return pl.pallas_call(
        functools.partial(prep_kernel, groups=groups, balance=balance),
        out_shape=(
            jax.ShapeDtypeStruct((1, slots), jnp.int32),
            jax.ShapeDtypeStruct(two.shape, jnp.int32),
            jax.ShapeDtypeStruct((groups, height, feature), BF),
        ),
        in_specs=[SM, SM, SM, VM, VM, VM, VM, VM, VM],
        out_specs=(VM, VM, VM),
        scratch_shapes=[pltpu.VMEM((slots, feature), BF)],
        compiler_params=params(),
        cost_estimate=takes(5),
        name="prep_slots",
    )(count, cols, count_two, owner, two, cols_two, pool, cot, adj_two)


def layer_rows(x, message, w_in, w_out, bias):
    pre = dot(jnp.concatenate([x, message], axis=1), w_in) + bias
    hidden = (pre * jax.nn.sigmoid(pre)).astype(BF)
    return (x.astype(F32) + dot(hidden, w_out)).astype(BF)


def fine_inner_kernel(cols, feats_hbm, adj_hbm, w_in, w_out, bias, *refs, rim, first, last):
    msg_out, res_out, feats, adj, feats_sem, adj_sem = refs[-6:]
    k = cols.shape[1]
    step = pl.program_id(0)
    chunk = step + first
    rows = CHUNK * BLK

    def feats_copy(c):
        at = pl.ds(pl.multiple_of(c * rows, rows), rows)
        return pltpu.make_async_copy(feats_hbm.at[at, :], feats.at[at, :], feats_sem.at[c - first + 1])

    def adj_copy(c):
        source = adj_hbm.at[pl.ds(c * CHUNK, CHUNK)]
        return pltpu.make_async_copy(source, adj.at[pl.ds((c - first) * CHUNK, CHUNK)], adj_sem.at[c - first])

    @pl.when(step == 0)
    def _():
        for c in (first - 1, first, first + 1):
            feats_copy(c).start()
        for c in range(first, last):
            adj_copy(c).start()
            if c + 2 <= last:
                feats_copy(c + 2).start()
        feats_copy(first - 1).wait()
        feats_copy(first).wait()

    feats_copy(chunk + 1).wait()
    adj_copy(chunk).wait()
    for j in range(CHUNK):
        block = apply_row(adj[step * CHUNK + j], cols, chunk * CHUNK + j, k, feats, rim)
        msg_out[j * BLK : (j + 1) * BLK, :] = block.astype(BF)
    x = feats[pl.ds(pl.multiple_of(chunk * rows, rows), rows), :]
    res_out[...] = layer_rows(x, msg_out[...], w_in[...], w_out[...], bias[...])


def fine_inner(cols, feats, adj, w_in, w_out, bias, first, last, done):
    total, feature = feats.shape
    rows = CHUNK * BLK
    steps = last - first
    hbm = pl.BlockSpec(memory_space=pl.ANY)
    return pl.pallas_call(
        functools.partial(fine_inner_kernel, rim=HALO // BLK, first=first, last=last),
        grid=(steps,),
        out_shape=(jax.ShapeDtypeStruct((total, feature), BF),) * 2,
        in_specs=[SM, hbm, hbm, VM, VM, VM] + [hbm] * len(done),
        out_specs=(pl.BlockSpec((rows, feature), lambda c: (c + first, 0)),) * 2,
        scratch_shapes=[
            pltpu.VMEM((total, feature), BF),
            pltpu.VMEM((steps * CHUNK,) + adj.shape[1:], BF),
            pltpu.SemaphoreType.DMA((steps + 2,)),
            pltpu.SemaphoreType.DMA((steps,)),
        ],
        input_output_aliases={6 + i: i for i in range(len(done))},
        compiler_params=params(),
        cost_estimate=takes(1.1 * steps),
        name="fine_inner",
    )(cols, feats, adj, w_in, w_out, bias, *done)


def fine_edge_kernel(me, cols, feats, prev, after, adj, w_in, w_out, bias, _m, _r, msg_out, res_out, ctx, *, blocks, groups):
    k = cols.shape[1]
    rows = CHUNK * BLK
    width = prev.shape[0]
    upper = pl.program_id(0) == 1

    @pl.when(pl.program_id(0) == 0)
    def _():
        ctx[0:width, :] = jnp.where(me[0] > 0, prev[...], jnp.zeros_like(prev))
        ctx[width:, :] = feats[...]

    @pl.when(upper)
    def _():
        ctx[0 : 2 * width, :] = feats[...]
        ctx[2 * width :, :] = jnp.where(me[0] < groups - 1, after[...], jnp.zeros_like(after))

    first = jnp.where(upper, blocks - CHUNK, 0)
    for j in range(CHUNK):
        block = apply_row(adj[j], cols, first + j, k, ctx, first)
        msg_out[j * BLK : (j + 1) * BLK, :] = block.astype(BF)
    x = ctx[width : width + rows, :]
    res_out[...] = layer_rows(x, msg_out[...], w_in[...], w_out[...], bias[...])


def fine_edge(me, groups, cols, feats, prev, after, adj, w_in, w_out, bias, message, result):
    total, feature = feats.shape
    blocks, _, span = adj.shape
    chunks = blocks // CHUNK
    rows = CHUNK * BLK
    out = (jax.ShapeDtypeStruct((total, feature), BF),) * 2
    edge_map = lambda c: (c * (chunks - 1), 0)
    return pl.pallas_call(
        functools.partial(fine_edge_kernel, blocks=blocks, groups=groups),
        grid=(2,),
        out_shape=out,
        in_specs=[
            SM,
            SM,
            pl.BlockSpec((2 * HALO, feature), lambda c: (c * (total // (2 * HALO) - 1), 0)),
            VM,
            VM,
            pl.BlockSpec((CHUNK, BLK, span), lambda c: (c * (chunks - 1), 0, 0)),
            VM,
            VM,
            VM,
            pl.BlockSpec(memory_space=pl.ANY),
            pl.BlockSpec(memory_space=pl.ANY),
        ],
        out_specs=(pl.BlockSpec((rows, feature), edge_map),) * 2,
        scratch_shapes=[pltpu.VMEM((3 * HALO, feature), BF)],
        input_output_aliases={9: 0, 10: 1},
        compiler_params=params(),
        cost_estimate=takes(4),
        name="fine_edge",
    )(me, cols, feats, prev, after, adj, w_in, w_out, bias, message, result)


def pool_kernel(cols, place, pool, src, packed_out, slots_scr):
    k = cols.shape[1]
    for q in range(pool.shape[0]):
        slots_scr[q * BLK : (q + 1) * BLK, :] = apply_row(pool[q], cols, q, k, src).astype(BF)
    slots = place.shape[1]
    step = min(256, slots)
    for p in range(0, slots, step):
        packed_out[p : p + step, :] = dot(place_matrix(place[...], p, step), slots_scr[...]).astype(BF)


def pool_pack(cols, place, pool, src):
    slots = place.shape[1]
    feature = src.shape[1]
    return pl.pallas_call(
        pool_kernel,
        out_shape=jax.ShapeDtypeStruct((slots, feature), BF),
        in_specs=[SM, VM, VM, VM],
        out_specs=VM,
        scratch_shapes=[pltpu.VMEM((slots, feature), BF)],
        compiler_params=params(),
        cost_estimate=takes(4),
        name="pool_one_pack",
    )(cols, place, pool, src)


def place_all(tables, got, n, cap):
    own = jnp.zeros((n, got.shape[2]), F32)
    for d in range(got.shape[0]):
        own += dot(place_matrix(tables[d], 0, n), got[d, 0:cap, :])
    return own.astype(BF)


def tables_from(first, cap):
    return [
        from_digits(first[d, cap : cap + 1, :], first[d, cap + 1 : cap + 2, :])[:, :cap]
        for d in range(first.shape[0])
    ]


def place_kernel(first, got, own_out):
    cap = got.shape[1]
    own_out[...] = place_all(tables_from(first, cap), got, own_out.shape[0], cap)


def place_rows(first, got, balance):
    groups, cap, feature = got.shape
    return pl.pallas_call(
        place_kernel,
        grid=(1,),
        out_shape=jax.ShapeDtypeStruct((balance, feature), BF),
        in_specs=[pl.BlockSpec((groups, cap + EXTRA, feature), lambda c: (0, 0, 0)), VM],
        out_specs=VM,
        compiler_params=params(),
        cost_estimate=takes(3),
        name="place_own_one",
    )(first, got)


def place_pool_kernel(cols, first, pool, own_out, slots_out, table_out):
    k = cols.shape[1]
    cap = table_out.shape[1]
    tables = tables_from(first, cap)
    own_out[...] = place_all(tables, first, own_out.shape[0], cap)
    for d in range(first.shape[0]):
        table_out[d : d + 1, :] = tables[d]
    for q in range(pool.shape[0]):
        slots_out[q * BLK : (q + 1) * BLK, :] = apply_row(pool[q], cols, q, k, own_out).astype(BF)


def place_pool(cols, first, pool, balance, cap):
    groups, _, feature = first.shape
    return pl.pallas_call(
        place_pool_kernel,
        grid=(1,),
        out_shape=(
            jax.ShapeDtypeStruct((balance, feature), BF),
            jax.ShapeDtypeStruct((pool.shape[0] * BLK, feature), BF),
            jax.ShapeDtypeStruct((groups, cap), jnp.int32),
        ),
        in_specs=[SM, pl.BlockSpec((groups, cap + EXTRA, feature), lambda c: (0, 0, 0)), VM],
        out_specs=(VM, VM, VM),
        compiler_params=params(),
        cost_estimate=takes(3),
        name="place_grad_up_one",
    )(cols, first, pool)


def one_forward_kernel(me, cols, pool_cols, *refs):
    pieces = refs[:-10]
    gslots, adj, pool, w_in, w_out, bias, msg_out, res_out, slots_out, ctx = refs[-10:]
    own = pieces[0]
    n = own.shape[0]
    for hop, piece in enumerate(pieces):
        ctx[pl.ds(pl.multiple_of((me[0] ^ hop) * n, n), n), :] = piece[...]
    k = cols.shape[1]
    for r in range(adj.shape[0]):
        msg_out[r * BLK : (r + 1) * BLK, :] = apply_row(adj[r], cols, r, k, ctx).astype(BF)
    res_out[...] = layer_rows(own[...], msg_out[...], w_in[...], w_out[...], bias[...])
    k = pool_cols.shape[1]
    for q in range(pool.shape[0]):
        rows = apply_row(pool[q], pool_cols, q, k, res_out).astype(BF)
        slots_out[q * BLK : (q + 1) * BLK, 0 : rows.shape[1]] = rows
    slots_out[:, own.shape[1] :] = gslots[...]


def one_forward(me, cols, pool_cols, pieces, gslots, adj, pool, w_in, w_out, bias):
    own = pieces[0]
    own_shape = jax.ShapeDtypeStruct(own.shape, BF)
    return pl.pallas_call(
        one_forward_kernel,
        out_shape=(own_shape, own_shape, jax.ShapeDtypeStruct((pool.shape[0] * BLK, 2 * own.shape[1]), BF)),
        in_specs=[SM, SM, SM] + [VM] * (len(pieces) + 6),
        out_specs=(VM, VM, VM),
        scratch_shapes=[pltpu.VMEM((len(pieces) * own.shape[0], own.shape[1]), BF)],
        compiler_params=params(),
        cost_estimate=takes(3),
        name="level_one_forward",
    )(me, cols, pool_cols, *pieces, gslots, adj, pool, w_in, w_out, bias)


def grad_pre_rows(grad_low, x, message, w_in, w_out, bias):
    joined = jnp.concatenate([x, message], axis=1)
    pre = dot(joined, w_in) + bias
    sig = jax.nn.sigmoid(pre)
    hidden = (pre * sig).astype(BF)
    grad_pre = dot_nt(grad_low, w_out) * (sig * (1.0 + pre * (1.0 - sig)))
    return joined, hidden, grad_pre


def coarse_kernel(groups, me, cols_two, cols_one, pool_cols, *refs):
    slots_two, refs = refs[:groups], refs[groups:]
    (
        mine_two, first, adj_one, pool_two, table_one, own_one, msg_one, res_one, gup_one,
        wi1, wo1, b1, wi2, wo2, b2, up_out, gx_out, sums_out,
    ) = refs[:18]
    part_outs, refs = refs[18 : 18 + groups - 1], refs[18 + groups - 1 :]
    both, xs, gs, ms, hs, gps, rs, ctx_acc, up_acc, gmsg, gctx_acc = refs
    feature = own_one.shape[1]
    n2 = xs.shape[0]
    n1 = own_one.shape[0]
    slots = mine_two.shape[1]
    for hop in range(groups):
        both[pl.ds(pl.multiple_of((me[0] ^ hop) * slots, slots), slots), :] = slots_two[hop][...]
    cap = table_one.shape[1]
    lanes = slots // 128
    at = cap + 2
    table = jnp.concatenate(
        [
            from_digits(first[d, at + c : at + c + 1, :], first[d, at + lanes + c : at + lanes + c + 1, :])
            for d in range(first.shape[0])
            for c in range(lanes)
        ],
        axis=1,
    )
    step = min(256, n2)
    for v in range(0, n2, step):
        rows = dot(place_matrix(table, v, step), both[...]).astype(BF)
        xs[v : v + step, :] = rows[:, :feature]
        gs[v : v + step, :] = rows[:, feature:]
    k = cols_two.shape[1]
    wide = k * BLK // 128

    def adj(r):
        per = n2 // (BLK * groups)
        at = cap + EXTRA + (r % per) * wide * BLK
        return jnp.concatenate(
            [first[r // per, at + c * BLK : at + (c + 1) * BLK, :] for c in range(wide)], axis=1
        )

    for r in range(n2 // BLK):
        ms[r * BLK : (r + 1) * BLK, :] = apply_row(adj(r), cols_two, r, k, xs).astype(BF)
    ctx_acc[...] = jnp.zeros_like(ctx_acc)
    for v in range(0, n2, step):
        x, m, g = xs[v : v + step, :], ms[v : v + step, :], gs[v : v + step, :]
        joined, hidden, grad_pre = grad_pre_rows(g, x, m, wi2[...], wo2[...], b2[...])
        rs[v : v + step, :feature] = (x.astype(F32) + dot(hidden, wo2[...])).astype(BF)
        hs[v : v + step, :] = hidden
        gps[v : v + step, :] = grad_pre
        grad_joined = dot_nt(grad_pre.astype(BF), wi2[...])
        ctx_acc[v : v + step, :] += g.astype(F32) + grad_joined[:, :feature]
        gm = grad_joined[:, feature:].astype(BF)
        for j in range(step // BLK):
            r = v // BLK + j
            spread_row(adj(r), cols_two, r, k, gm[j * BLK : (j + 1) * BLK], ctx_acc)
    rs[:, feature:] = ctx_acc[...].astype(BF)
    balance = slots // 2
    at = pl.ds(pl.multiple_of(me[0] * balance, balance), balance)
    gp_own = gps[at, :]
    joined = jnp.concatenate([xs[at, :], ms[at, :]], axis=1)
    level = 3 * feature
    sums_out[level : level + 2 * feature, :] = dot_tn(joined, gp_own.astype(BF))
    sums_out[level + 2 * feature : 2 * level, :] = dot_tn(hs[at, :], gs[at, :])
    bias_two = jnp.sum(gp_own, axis=0, keepdims=True)
    mine = place_matrix(mine_two[...], 0, n2)
    back = dot_tn(mine, rs[...]).astype(BF)
    up_acc[:, :feature] = res_one[...].astype(F32)
    up_acc[:, feature:] = gup_one[...].astype(F32)
    k = pool_cols.shape[1]
    for q in range(pool_two.shape[0]):
        spread_row(pool_two[q], pool_cols, q, k, back[q * BLK : (q + 1) * BLK], up_acc)
    up_low = up_acc[:, :feature].astype(BF)
    for d in range(table_one.shape[0]):
        up_out[d] = dot_tn(place_matrix(table_one[d : d + 1, :], 0, n1), up_low).astype(BF)
    grad = up_acc[:, feature:]
    grad_low = grad.astype(BF)
    joined, hidden, grad_pre = grad_pre_rows(grad_low, own_one[...], msg_one[...], wi1[...], wo1[...], b1[...])
    grad_pre_low = grad_pre.astype(BF)
    sums_out[0 : 2 * feature, :] = dot_tn(joined, grad_pre_low)
    sums_out[2 * feature : level, :] = dot_tn(hidden, grad_low)
    bias_one = jnp.sum(grad_pre, axis=0, keepdims=True)
    rest = sums_out.shape[0] - 2 * level
    row = iota((rest, feature), 0)
    sums_out[2 * level :, :] = jnp.where(row == 0, bias_one, jnp.where(row == 1, bias_two, 0.0))
    grad_joined = dot_nt(grad_pre_low, wi1[...])
    gmsg[...] = grad_joined[:, feature:].astype(BF)
    gctx_acc[...] = jnp.zeros_like(gctx_acc)
    k = cols_one.shape[1]
    for r in range(adj_one.shape[0]):
        spread_row(adj_one[r], cols_one, r, k, gmsg[r * BLK : (r + 1) * BLK, :], gctx_acc)
    own_at = pl.ds(pl.multiple_of(me[0] * n1, n1), n1)
    gx_out[...] = grad + grad_joined[:, :feature] + gctx_acc[own_at, :]
    for hop in range(1, groups):
        at = pl.ds(pl.multiple_of((me[0] ^ hop) * n1, n1), n1)
        part_outs[hop - 1][...] = gctx_acc[at, :].astype(BF)


def coarse_levels(
    me, cols_two, cols_one, pool_cols, slots_two, mine_two, first, adj_one, pool_two,
    table_one, own_one, msg_one, res_one, gup_one, wi1, wo1, b1, wi2, wo2, b2, sum_rows,
):
    groups = len(slots_two)
    n1, feature = own_one.shape
    n2 = mine_two.shape[1] // 2 * groups
    cap = table_one.shape[1]
    return pl.pallas_call(
        functools.partial(coarse_kernel, groups),
        out_shape=(
            jax.ShapeDtypeStruct((groups, cap, feature), BF),
            jax.ShapeDtypeStruct((n1, feature), F32),
            jax.ShapeDtypeStruct((sum_rows, feature), F32),
        )
        + (jax.ShapeDtypeStruct((n1, feature), BF),) * (groups - 1),
        in_specs=[SM] * 4 + [VM] * (15 + groups),
        out_specs=(VM,) * (2 + groups),
        scratch_shapes=[
            pltpu.VMEM((groups * slots_two[0].shape[0], 2 * feature), BF),
            pltpu.VMEM((n2, feature), BF),
            pltpu.VMEM((n2, feature), BF),
            pltpu.VMEM((n2, feature), BF),
            pltpu.VMEM((n2, feature), BF),
            pltpu.VMEM((n2, feature), F32),
            pltpu.VMEM((n2, 2 * feature), BF),
            pltpu.VMEM((n2, feature), F32),
            pltpu.VMEM((n1, 2 * feature), F32),
            pltpu.VMEM((n1, feature), BF),
            pltpu.VMEM((groups * n1, feature), F32),
        ],
        compiler_params=params(),
        cost_estimate=takes(9),
        name="coarse_levels",
    )(
        me, cols_two, cols_one, pool_cols, *slots_two, mine_two, first, adj_one, pool_two,
        table_one, own_one, msg_one, res_one, gup_one, wi1, wo1, b1, wi2, wo2, b2,
    )


def owner_sum_kernel(table, gx, *refs):
    send_out = refs[-1]
    total = gx[...]
    for part in refs[:-1]:
        total += part[...].astype(F32)
    low = total.astype(BF)
    for d in range(table.shape[0]):
        send_out[d] = dot_tn(place_matrix(table[d : d + 1, :], 0, gx.shape[0]), low).astype(BF)


def owner_sum(table, gx, parts):
    return pl.pallas_call(
        owner_sum_kernel,
        out_shape=jax.ShapeDtypeStruct(table.shape + (gx.shape[1],), BF),
        in_specs=[VM] * (2 + len(parts)),
        out_specs=VM,
        compiler_params=params(),
        cost_estimate=takes(3),
        name="grad_own_one_send",
    )(table, gx, *parts)


def lift(place, got, pool, cols, acc):
    groups, height, _ = got.shape
    cap = place.shape[1] // groups
    packed = jnp.concatenate([got[d, height - cap :, :] for d in range(groups)], axis=0)
    rows = dot_tn(place_matrix(place[...], 0, packed.shape[0]), packed).astype(BF)
    k = cols.shape[1]
    for q in range(pool.shape[0]):
        spread_row(pool[q], cols, q, k, rows[q * BLK : (q + 1) * BLK], acc)


def node_out_kernel(cols, place, got, pool, base, out, acc):
    rows = out.shape[0]

    @pl.when(pl.program_id(0) == 0)
    def _():
        acc[...] = jnp.zeros_like(acc)
        lift(place, got, pool, cols, acc)

    at = pl.ds(pl.multiple_of(pl.program_id(0) * rows, rows), rows)
    out[...] = (base[...].astype(F32) + acc[at, :]).astype(BF)


def node_out_rows(cols, place, got, pool, base):
    total, feature = base.shape
    rows = 1024
    spec = pl.BlockSpec((rows, feature), lambda c: (c, 0))
    return pl.pallas_call(
        node_out_kernel,
        grid=(total // rows,),
        out_shape=jax.ShapeDtypeStruct((total, feature), BF),
        in_specs=[SM, VM, VM, VM, spec],
        out_specs=spec,
        scratch_shapes=[pltpu.VMEM((total, feature), F32)],
        compiler_params=params(),
        cost_estimate=takes(9),
        name="node_out",
    )(cols, place, got, pool, base)


def fine_grad_kernel(
    cols, place, got, pool, cot, feats, message, w_in, w_out, bias, gx_out, gmsg_out, sums, acc
):
    rows = cot.shape[0]
    feature = cot.shape[1]

    @pl.when(pl.program_id(0) == 0)
    def _():
        acc[...] = jnp.zeros_like(acc)
        sums[...] = jnp.zeros_like(sums)
        lift(place, got, pool, cols, acc)

    at = pl.ds(pl.multiple_of(pl.program_id(0) * rows, rows), rows)
    grad = cot[...].astype(F32) + acc[at, :]
    grad_low = grad.astype(BF)
    joined, hidden, grad_pre = grad_pre_rows(grad_low, feats[...], message[...], w_in[...], w_out[...], bias[...])
    grad_pre_low = grad_pre.astype(BF)
    level = 3 * feature
    sums[0 : 2 * feature, :] += dot_tn(joined, grad_pre_low)
    sums[2 * feature : level, :] += dot_tn(hidden, grad_low)
    sums[level : level + 1, :] += jnp.sum(grad_pre, axis=0, keepdims=True)
    grad_joined = dot_nt(grad_pre_low, w_in[...])
    gx_out[...] = grad + grad_joined[:, :feature]
    gmsg_out[...] = grad_joined[:, feature:].astype(BF)


def fine_grad(cols, place, got, pool, cot, feats, message, w_in, w_out, bias, sum_rows):
    total, feature = cot.shape
    rows = 1024
    spec = pl.BlockSpec((rows, feature), lambda c: (c, 0))
    return pl.pallas_call(
        fine_grad_kernel,
        grid=(total // rows,),
        out_shape=(
            jax.ShapeDtypeStruct((total, feature), F32),
            jax.ShapeDtypeStruct((total, feature), BF),
            jax.ShapeDtypeStruct((sum_rows, feature), F32),
        ),
        in_specs=[SM, VM, VM, VM, spec, spec, spec, VM, VM, VM],
        out_specs=(spec, spec, VM),
        scratch_shapes=[pltpu.VMEM((total, feature), F32)],
        compiler_params=params(),
        cost_estimate=takes(19),
        name="fine_layer_backward",
    )(cols, place, got, pool, cot, feats, message, w_in, w_out, bias)


def spread_edge_kernel(cols, adj, gmsg, gx, rims_out, carry_out, acc, *, blocks):
    k = cols.shape[1]
    upper = pl.program_id(0) == 1
    width = rims_out.shape[0]
    first = jnp.where(upper, blocks - CHUNK, 0)
    acc[0:width, :] = jnp.zeros_like(gx)
    acc[width : 2 * width, :] = gx[...]
    acc[2 * width :, :] = jnp.zeros_like(gx)
    for j in range(CHUNK):
        spread_row(adj[j], cols, first + j, k, gmsg[j * BLK : (j + 1) * BLK, :], acc, first)

    @pl.when(jnp.logical_not(upper))
    def _():
        rims_out[...] = acc[0:width, :].astype(BF)
        carry_out[...] = acc[width:, :]

    @pl.when(upper)
    def _():
        rims_out[...] = acc[2 * width :, :].astype(BF)
        carry_out[...] = acc[0 : 2 * width, :]


def spread_edge(cols, adj, gmsg, gx):
    blocks, _, span = adj.shape
    feature = gmsg.shape[1]
    chunks = blocks // CHUNK
    return pl.pallas_call(
        functools.partial(spread_edge_kernel, blocks=blocks),
        grid=(2,),
        out_shape=(
            jax.ShapeDtypeStruct((2 * HALO, feature), BF),
            jax.ShapeDtypeStruct((4 * HALO, feature), F32),
        ),
        in_specs=[
            SM,
            pl.BlockSpec((CHUNK, BLK, span), lambda c: (c * (chunks - 1), 0, 0)),
            pl.BlockSpec((CHUNK * BLK, feature), lambda c: (c * (chunks - 1), 0)),
            pl.BlockSpec((CHUNK * BLK, feature), lambda c: (c * (chunks - 1), 0)),
        ],
        out_specs=(
            pl.BlockSpec((HALO, feature), lambda c: (c, 0)),
            pl.BlockSpec((2 * HALO, feature), lambda c: (c, 0)),
        ),
        scratch_shapes=[pltpu.VMEM((3 * HALO, feature), F32)],
        compiler_params=params(),
        cost_estimate=takes(3),
        name="spread_edge",
    )(cols, adj, gmsg, gx)


def spread_inner_kernel(cols, adj_a, adj_b, gmsg_a, gmsg_b, gx_a, gx_b, carry, mid_out, rims_out, acc, *, rim):
    k = cols.shape[1]
    step = pl.program_id(0)
    steps = pl.num_programs(0)
    width = rim * BLK
    total = mid_out.shape[0]

    @pl.when(step == 0)
    def _():
        acc[0 : 2 * width, :] = carry[0 : 2 * width, :]
        acc[2 * width : total - 2 * width, :] = jnp.zeros((total - 4 * width, acc.shape[1]), F32)
        acc[total - 2 * width :, :] = carry[2 * width :, :]

    for half, (adj, gmsg, gx) in enumerate(((adj_a, gmsg_a, gx_a), (adj_b, gmsg_b, gx_b))):
        chunk = 2 * step + 1 + half
        for j in range(CHUNK):
            spread_row(adj[j], cols, chunk * CHUNK + j, k, gmsg[j * BLK : (j + 1) * BLK, :], acc, rim)
        rows = gx.shape[0]
        acc[pl.ds(pl.multiple_of(chunk * rows, rows), rows), :] += gx[...]

    @pl.when(step == steps - 1)
    def _():
        mid_out[...] = acc[...].astype(BF)
        rims_out[0:width, :] = acc[0:width, :]
        rims_out[width:, :] = acc[total - width :, :]


def spread_inner(cols, adj, gmsg, gx, carry):
    total, feature = gx.shape
    blocks, _, span = adj.shape
    rows = CHUNK * BLK
    return pl.pallas_call(
        functools.partial(spread_inner_kernel, rim=HALO // BLK),
        grid=(blocks // CHUNK // 2 - 1,),
        out_shape=(
            jax.ShapeDtypeStruct((total, feature), BF),
            jax.ShapeDtypeStruct((2 * HALO, feature), F32),
        ),
        in_specs=[
            SM,
            pl.BlockSpec((CHUNK, BLK, span), lambda c: (2 * c + 1, 0, 0)),
            pl.BlockSpec((CHUNK, BLK, span), lambda c: (2 * c + 2, 0, 0)),
            pl.BlockSpec((rows, feature), lambda c: (2 * c + 1, 0)),
            pl.BlockSpec((rows, feature), lambda c: (2 * c + 2, 0)),
            pl.BlockSpec((rows, feature), lambda c: (2 * c + 1, 0)),
            pl.BlockSpec((rows, feature), lambda c: (2 * c + 2, 0)),
            VM,
        ],
        out_specs=(VM, VM),
        scratch_shapes=[pltpu.VMEM((total, feature), F32)],
        compiler_params=params(),
        cost_estimate=takes(18),
        name="spread_inner",
    )(cols, adj, adj, gmsg, gmsg, gx, gx, carry)


def rim_add_kernel(me, mid_in, rims, prev, after, out, *, groups):
    low = jnp.where(me[0] > 0, prev[...].astype(F32), 0.0)
    high = jnp.where(me[0] < groups - 1, after[...].astype(F32), 0.0)
    out[...] = (rims[...] + jnp.where(pl.program_id(0) == 0, low, high)).astype(BF)


def rim_add(me, groups, mid, rims, prev, after):
    total, feature = mid.shape
    return pl.pallas_call(
        functools.partial(rim_add_kernel, groups=groups),
        grid=(2,),
        out_shape=jax.ShapeDtypeStruct(mid.shape, BF),
        in_specs=[
            SM,
            pl.BlockSpec(memory_space=pl.ANY),
            pl.BlockSpec((HALO, feature), lambda c: (c, 0)),
            VM,
            VM,
        ],
        out_specs=pl.BlockSpec((HALO, feature), lambda c: (c * (total // HALO - 1), 0)),
        input_output_aliases={1: 0},
        compiler_params=params(),
        cost_estimate=takes(2),
        name="rim_add",
    )(me, mid, rims, prev, after)


def after_all(value, *others):
    return lax.optimization_barrier((value,) + others)[0]


def exchange(parts):
    return lax.all_to_all(parts, "grp", split_axis=0, concat_axis=0, tiled=True)


def gather_rows(rows):
    groups = lax.axis_size("grp")
    got = exchange(jnp.broadcast_to(rows[None], (groups,) + rows.shape))
    return got.reshape((groups * rows.shape[0],) + rows.shape[1:])


def halo_pair(low, high):
    count = lax.axis_size("grp")
    prev = lax.ppermute(high, "grp", [(i, (i + 1) % count) for i in range(count)])
    after = lax.ppermute(low, "grp", [((i + 1) % count, i) for i in range(count)])
    return prev, after


def hop_by(rows, axis, hop):
    return lax.ppermute(rows, axis, [(i, i ^ hop) for i in range(lax.axis_size(axis))])


def gather_hops(rows):
    groups = lax.axis_size("grp")
    if groups != 8:
        return [rows] + [hop_by(rows, "grp", hop) for hop in range(1, groups)]
    got = {hop: hop_by(rows, "grp", hop) for hop in (4, 2, 1)}
    got[5] = hop_by(got[4], "grp", 1)
    got[6] = hop_by(got[4], "grp", 2)
    got[3] = hop_by(got[2], "grp", 1)
    got[7] = hop_by(got[5], "grp", 2)
    return [rows] + [got[hop] for hop in range(1, 8)]


def add_low(*parts):
    return sum(part.astype(F32) for part in parts).astype(BF)


def scatter_hops(parts):
    groups = lax.axis_size("grp")
    if groups != 8:
        return [hop_by(parts[hop - 1], "grp", hop) for hop in range(1, groups)]
    far = hop_by(parts[6], "grp", 7)
    six = hop_by(parts[5], "grp", 2)
    five = hop_by(parts[4], "grp", 1)
    three = hop_by(parts[2], "grp", 1)
    return [
        hop_by(add_low(parts[3], five, six), "grp", 4),
        hop_by(add_low(parts[1], three), "grp", 2),
        hop_by(parts[0], "grp", 1),
        far,
    ]


ALL = ("slab", "grp")


def padded_rows(height):
    part = 8 * lax.axis_size(ALL)
    return -(-height // part) * part


def send_shares(rows):
    count = lax.axis_size(ALL)
    shares = rows.reshape(count, rows.shape[0] // count, rows.shape[1])
    return lax.all_to_all(shares, ALL, split_axis=0, concat_axis=0, tiled=True)


def share_sums(rows):
    count = lax.axis_size(ALL)
    return lax.all_to_all(
        jnp.broadcast_to(rows[None], (count,) + rows.shape), ALL, split_axis=0, concat_axis=0, tiled=True
    )


def body(
    node_feats,
    cotangent,
    fine_adjacency,
    fine_columns,
    pool_one,
    pool_one_columns,
    count_one,
    owner_one,
    adjacency_one,
    columns_one,
    pool_two,
    pool_two_columns,
    count_two,
    owner_two,
    adjacency_two,
    columns_two,
    weight_in,
    weight_out,
    biases,
):
    groups = lax.axis_size("grp")
    feature = node_feats.shape[1]
    slots_one = owner_one.shape[0]
    balance_one = slots_one // 2
    slots_two = owner_two.shape[0]
    me = lax.axis_index("grp").astype(jnp.int32).reshape(1)
    bias_rows = [biases[level : level + 1] for level in range(3)]

    cap_one = slots_one // groups
    place_one, mine_two, send = prep(
        count_one, pool_one_columns, count_two, owner_one.reshape(1, slots_one), owner_two.reshape(1, slots_two),
        columns_two.reshape(1, -1), pool_one, cotangent, adjacency_two, groups, balance_one,
    )
    prev, after = halo_pair(node_feats[:HALO], node_feats[-HALO:])
    first = exchange(send)
    chunks = fine_adjacency.shape[0] // CHUNK
    fine_weights = (fine_adjacency, weight_in[0], weight_out[0], bias_rows[0])
    done = fine_inner(after_all(fine_columns, send), node_feats, *fine_weights, 1, chunks - 1, ())
    message0, result0 = fine_edge(me, groups, fine_columns, node_feats, prev, after, *fine_weights, *done)
    sent_one = pool_pack(pool_one_columns, place_one, pool_one, result0)
    sent_one, first = lax.optimization_barrier((sent_one, first))
    got_one = exchange(sent_one.reshape(groups, cap_one, feature))
    own_one = place_rows(first, got_one, balance_one)
    grad_up_one, gslots_two, table_one = place_pool(
        pool_two_columns, after_all(first, own_one), pool_two, balance_one, cap_one
    )
    at = cap_one + 2 + 2 * slots_two // 128
    columns_two_all = first[:, at, : columns_two.size].astype(jnp.int32).reshape(-1, columns_two.shape[1])
    message_one, result1, slots_two_mine = one_forward(
        me, columns_one, pool_two_columns, gather_hops(own_one), gslots_two, adjacency_one, pool_two,
        weight_in[1], weight_out[1], bias_rows[1],
    )
    level = 3 * feature
    up_send, gx_one, coarse_sums, *parts_back = coarse_levels(
        me, columns_two_all, columns_one, pool_two_columns, gather_hops(slots_two_mine), mine_two, first,
        adjacency_one, pool_two, table_one, own_one, message_one, result1, grad_up_one,
        weight_in[1], weight_out[1], bias_rows[1], weight_in[2], weight_out[2], bias_rows[2],
        padded_rows(2 * level + 2),
    )
    up_got = exchange(up_send)
    grad_send = owner_sum(table_one, gx_one, scatter_hops(parts_back))
    grad_send, up_got = lax.optimization_barrier((grad_send, up_got))
    grad_got = exchange(grad_send)
    node_out = node_out_rows(pool_one_columns, place_one, up_got, pool_one, result0)
    grad_got, node_out = lax.optimization_barrier((grad_got, node_out))

    coarse_shares = send_shares(after_all(coarse_sums, grad_got))
    gx_zero, gmsg_zero, fine_sums = fine_grad(
        pool_one_columns, place_one, grad_got, pool_one, cotangent, node_feats, message0,
        weight_in[0], weight_out[0], bias_rows[0], padded_rows(level + 1),
    )
    coarse_shares, gmsg_zero, fine_sums = lax.optimization_barrier((coarse_shares, gmsg_zero, fine_sums))
    fine_shares = send_shares(fine_sums)
    rims_out, carry = spread_edge(fine_columns, fine_adjacency, gmsg_zero, gx_zero)
    fine_shares, carry = lax.optimization_barrier((fine_shares, carry))
    mine = jnp.concatenate([jnp.sum(fine_shares, axis=0), jnp.sum(coarse_shares, axis=0)], axis=0).astype(BF)
    sums = share_sums(mine).astype(F32)
    from_prev, from_after = halo_pair(rims_out[:HALO], rims_out[HALO:])
    mid, rims_own = spread_inner(fine_columns, fine_adjacency, gmsg_zero, gx_zero, after_all(carry, mine))
    grad_feats = rim_add(me, groups, mid, rims_own, from_prev, from_after)
    cut = fine_shares.shape[1]
    fine_sums = sums[:, :cut].reshape(-1, feature)
    coarse_sums = sums[:, cut:].reshape(-1, feature)

    scale = 1.0 / math.sqrt(node_feats.shape[0] * groups * lax.axis_size("slab"))
    wide = 2 * feature
    grad_in = jnp.stack([fine_sums[:wide], coarse_sums[:wide], coarse_sums[level : level + wide]])
    grad_out = jnp.stack([fine_sums[wide:level], coarse_sums[wide:level], coarse_sums[level + wide : 2 * level]])
    grad_bias = jnp.concatenate([fine_sums[level : level + 1], coarse_sums[2 * level : 2 * level + 2]])
    return (node_out, grad_feats, grad_in * scale, grad_out * scale, grad_bias * scale)


def solution(mesh):
    rows = P(("slab", "grp"), None)
    blocks = P(("slab", "grp"), None, None)
    flat = P(("slab", "grp"))
    placed = (
        rows, rows, blocks, rows, blocks, rows, flat, flat, blocks, rows,
        blocks, rows, flat, flat, blocks, rows, P(), P(), P(),
    )
    return jax.shard_map(
        body,
        mesh=mesh,
        in_specs=placed,
        out_specs=(rows, rows, P(), P(), P()),
        check_vma=False,
    )
```

time: 337 us -> 229 us (0.68)
  waiting for transfers between devices: 91.3 us -> 39 us
  blocking collectives: 43.8 us -> 17.7 us
  between operations: 15.7 us -> 2.25 us
  local copies, waits for them, and re-layouts: 19.4 us -> 12.8 us
  Pallas kernels: 97.7 us -> 92.3 us
    all_to_all x11 -> x3, waiting for transfers between devices: 54.6 us -> 0.01 us  [exchange(): return lax.all_to_all(parts, 'grp', split_axis=0, concat_axis=0, tiled=True)]
    all_to_all x11 -> x3, starting transfers between devices: 44.6 us -> 16 us  [exchange(): return lax.all_to_all(parts, 'grp', split_axis=0, concat_axis=0, tiled=True)]
    all_gather x1 -> x0, waiting for transfers between devices: 27.4 us -> none  [body(): adjacency_two_all = lax.all_gather(adjacency_two, 'grp', axis=0, tiled=True)]
    all_to_all x2 -> x1, blocking collectives: 43.8 us -> 17.7 us  [exchange(): return lax.all_to_all(parts, 'grp', split_axis=0, concat_axis=0, tiled=True)]
    ppermute x8 -> x25, waiting for transfers between devices: 8.69 us -> 31.1 us  [the longest x21 25.2 us: hop_by(): lax.ppermute(rows, axis, [(i, i ^ hop) for i in range(lax.axis_size(axis))])]
    ppermute x8 -> x25, starting transfers between devices: 15.8 us -> 29.8 us  [the longest x21 20.4 us: hop_by(): lax.ppermute(rows, axis, [(i, i ^ hop) for i in range(lax.axis_size(axis))])]
    all_to_all x0 -> x3, starting transfers between devices: none -> 12.6 us  [the longest x2 9.99 us: send_shares(): return lax.all_to_all(shares, ALL, split_axis=0, concat_axis=0, tiled=True)]
    all_to_all x0 -> x3, waiting for transfers between devices: none -> 7.91 us  [the longest x2 7.91 us: send_shares(): return lax.all_to_all(shares, ALL, split_axis=0, concat_axis=0, tiled=True)]
  transfers between devices with their start and end apart: 20 -> 31, of which waited for: 12 -> 14; matrix products, arithmetic and copies ran while one was open for 4% -> 4% of each run, Pallas kernels for 27% -> 32%
where the time goes in v2:
time: 229 us; the launch traced here: 227 us
  Pallas kernels  92.3 us (40%)
  starting transfers between devices  58.3 us (25%)
  waiting for transfers between devices  39 us (17%)
  blocking collectives  17.7 us (8%)
  local copies, waits for them, and re-layouts  12.8 us (6%)
  other arithmetic  4.81 us (2%)
    ppermute x21, waiting for transfers between devices, hop_by(): lax.ppermute(rows, axis, [(i, i ^ hop) for i in range(lax.axis_size(axis))])  25.2 us
    ppermute x21, starting transfers between devices, hop_by(): lax.ppermute(rows, axis, [(i, i ^ hop) for i in range(lax.axis_size(axis))])  20.4 us
    all_to_all x1, blocking collectives, exchange(): return lax.all_to_all(parts, 'grp', split_axis=0, concat_axis=0, tiled=True)  17.7 us
    all_to_all x3, starting transfers between devices, exchange(): return lax.all_to_all(parts, 'grp', split_axis=0, concat_axis=0, tiled=True)  16 us
    pallas_call x1, Pallas kernels, spread_inner(): pl.pallas_call(functools.partial(spread_inner_kernel, rim=HALO // BLK), g...  15.7 us
    pallas_call x1, Pallas kernels, fine_inner(): pl.pallas_call(functools.partial(fine_inner_kernel, rim=HALO // BLK, firs...  14.5 us
    pallas_call x1, Pallas kernels, fine_grad(): pl.pallas_call(fine_grad_kernel, grid=(total // rows,), out_shape=(jax.Sh...  14.4 us
    all_to_all x2, starting transfers between devices, send_shares(): return lax.all_to_all(shares, ALL, split_axis=0, concat_axis=0, tiled=True)  9.99 us
  transfers between devices with their start and end apart: 31, of which 14 were waited for; matrix products, arithmetic and copies ran while one was open for 4% of the time, Pallas kernels for 32%

profile of v2, /device:TPU:0, one launch (start us, length us, event | category | flops | bytes accessed | tf_op | source)
XLA Modules:
  0.0 227.2 jit_solution(7645831679282272600)
XLA Ops:
  4.5 5.0 %prep_slots.1 = (s32[1,1024]{1,0:T(1,128)}, s32[1,256]{1,0:T(1,128)}, bf16[8,656,128]{2,1,0:T(8,128)(2,1)}) custom-call(s32[1]{0:T(128)S(6)} %copy.46.count, s32[16,8]{1,0:T(8,128)} %copy.38.cols, s32[1]{0:T(128)S(6)} %copy.47.count_two, s32[1,1024]{1,0:T(1,128)} %bitcast.36, s32[1,256]{1,0:T(1,128)} %bitcast.37, s32[1,16]{1,0:T(1,128)} %reshape.70.cols_two, ...), custom_call_target="tpu_custom_call" | custom-call | bytes 55350000 | tf_op jit(solution)/shard_map/prep_slots/pallas_call | solution.py:143
  9.5 7.4 %all-to-all-start = ((bf16[8,656,128]{2,1,0:T(8,128)(2,1)}), bf16[8,656,128]{2,1,0:T(8,128)(2,1)S(1)}, u32[]{:S(2)}, u32[]{:S(2)}) async-start(bf16[8,656,128]{2,1,0:T(8,128)(2,1)} %get-tuple-element.50), calls=%async_computation | async-start | bytes 2686976 | tf_op jit(solution)/shard_map/all_to_all | solution.py:793
  17.9 4.8 %collective-permute-start.1 = (bf16[512,128]{1,0:T(8,128)(2,1)S(1)}, bf16[512,128]{1,0:T(8,128)(2,1)S(1)}, u32[]{:S(2)}, u32[]{:S(2)}) collective-permute-start(bf16[512,128]{1,0:T(8,128)(2,1)S(1)} %get-tuple-element.93), channel_id=1, source_target_pairs={{1,0},{2,1},{3,2},{4,3},{5,4},{6,5},{7,6},{0,7},{9,8},{10,9},{11,1... | collective-permute-start | bytes 393224 | tf_op jit(solution)/shard_map/ppermute | solution.py:805
  26.0 14.5 %fine_inner.1 = (bf16[8192,128]{1,0:T(8,128)(2,1)}, bf16[8192,128]{1,0:T(8,128)(2,1)}) custom-call(s32[128,12]{1,0:T(8,128)} %copy.36.cols, bf16[8192,128]{1,0:T(8,128)(2,1)} %feats.3, bf16[128,64,768]{2,1,0:T(8,128)(2,1)} %adj_b.1, bf16[256,128]{1,0:T(8,128)(2,1)} %get-tuple-element.102.w_in, bf16[128,128]{1,0:T(8,128)(2,1)} %get-tuple-element.105.w_out, ...), custom_call_target="tpu_custom_call" | custom-call | bytes 170478000 | tf_op jit(solution)/shard_map/fine_inner/pallas_call | solution.py:205
  42.1 4.5 %collective-permute-done.prev = bf16[512,128]{1,0:T(8,128)(2,1)S(1)} collective-permute-done((bf16[512,128]{1,0:T(8,128)(2,1)S(1)}, bf16[512,128]{1,0:T(8,128)(2,1)S(1)}, u32[]{:S(2)}, u32[]{:S(2)}) %collective-permute-start) | collective-permute-done | bytes 131104 | tf_op jit(solution)/shard_map/ppermute | solution.py:804
  47.2 4.0 %fine_edge.1 = (bf16[8192,128]{1,0:T(8,128)(2,1)}, bf16[8192,128]{1,0:T(8,128)(2,1)}) custom-call(s32[1]{0:T(128)} %bitcast.2.me, s32[128,12]{1,0:T(8,128)} %copy.37.cols, bf16[8192,128]{1,0:T(8,128)(2,1)} %feats.3, bf16[512,128]{1,0:T(8,128)(2,1)} %copy-done.5, bf16[512,128]{1,0:T(8,128)(2,1)} %copy-done.4, ...), custom_call_target="tpu_custom_call", output_to_operand_aliasing={{0}: (9, {}), {1}: (10, {})} | custom-call | bytes 44280000 | tf_op jit(solution)/shard_map/fine_edge/pallas_call | solution.py:255
  51.2 3.8 %pool_one_pack.1 = bf16[1024,128]{1,0:T(8,128)(2,1)} custom-call(s32[16,8]{1,0:T(8,128)} %copy.38.cols, s32[1,1024]{1,0:T(1,128)} %get-tuple-element.49.place, bf16[16,64,512]{2,1,0:T(8,128)(2,1)} %pool.9, bf16[8192,128]{1,0:T(8,128)(2,1)} %get-tuple-element.54.src.base), custom_call_target="tpu_custom_call" | custom-call | bytes 44280000 | tf_op jit(solution)/shard_map/pool_one_pack/pallas_call | solution.py:294
  55.0 17.7 %all_to_all.35.got = bf16[8,128,128]{2,1,0:T(8,128)(2,1)} all-to-all(bf16[8,128,128]{2,1,0:T(8,128)(2,1)} %bitcast.26), channel_id=1, replica_groups=mesh['slab'=4,'grp'=8] {'grp'}, dimensions={0} | all-to-all | bytes 524288 | tf_op jit(solution)/shard_map/all_to_all | solution.py:793
  72.7 2.1 place_own_one.1.refs_0_.refs_13_
  76.1 6.3 %collective-permute-done.5.refs_4_ = bf16[512,128]{1,0:T(8,128)(2,1)S(1)} collective-permute-done((bf16[512,128]{1,0:T(8,128)(2,1)}, bf16[512,128]{1,0:T(8,128)(2,1)S(1)}, u32[]{:S(2)}, u32[]{:S(2)}) %collective-permute-start.5) | collective-permute-done | bytes 131104 | tf_op jit(solution)/shard_map/ppermute | solution.py:810
  85.2 2.1 collective-permute-done.6.refs_5_
  87.8 2.4 %place_grad_up_one.1 = (bf16[512,128]{1,0:T(8,128)(2,1)}, bf16[256,128]{1,0:T(8,128)(2,1)}, s32[8,128]{1,0:T(8,128)}) custom-call(s32[4,8]{1,0:T(4,128)} %pool_cols.3, bf16[8,656,128]{2,1,0:T(8,128)(2,1)} %copy-done, bf16[4,64,512]{2,1,0:T(8,128)(2,1)} %refs_11_.1), custom_call_target="tpu_custom_call" | custom-call | bytes 33210000 | tf_op jit(solution)/shard_map/place_grad_up_one/pallas_call | solution.py:352
  90.2 2.1 collective-permute-done.8.refs_7_
  93.0 3.1 %level_one_forward.1 = (bf16[512,128]{1,0:T(8,128)(2,1)}, bf16[512,128]{1,0:T(8,128)(2,1)}, bf16[256,256]{1,0:T(8,128)(2,1)}) custom-call(s32[1]{0:T(128)} %bitcast.2.me, s32[8,8]{1,0:T(8,128)} %cols_one.1, s32[4,8]{1,0:T(4,128)} %pool_cols.3, bf16[512,128]{1,0:T(8,128)(2,1)} %place_own_one.1.refs_0_.refs_13_, bf16[512,128]{1,0:T(8,128)(2,1)} %copy-done.16, ...), custom_call_target="tpu_custom_call" | custom-call | bytes 33210000 | tf_op jit(solution)/shard_map/level_one_forward/pallas_call | solution.py:389
  99.9 3.8 %collective-permute-done.12.refs_4_ = bf16[256,256]{1,0:T(8,128)(2,1)S(1)} collective-permute-done((bf16[256,256]{1,0:T(8,128)(2,1)}, bf16[256,256]{1,0:T(8,128)(2,1)S(1)}, u32[]{:S(2)}, u32[]{:S(2)}) %collective-permute-start.12) | collective-permute-done | bytes 131104 | tf_op jit(solution)/shard_map/ppermute | solution.py:810
  106.6 2.0 collective-permute-done.13.refs_5_
  111.5 2.2 collective-permute-done.15.refs_7_
  114.3 9.5 %coarse_levels.1 = (bf16[8,128,128]{2,1,0:T(8,128)(2,1)}, f32[512,128]{1,0:T(8,128)}, f32[1024,128]{1,0:T(8,128)}, bf16[512,128]{1,0:T(8,128)(2,1)}, bf16[512,12...) custom-call(s32[1]{0:T(128)} %bitcast.2.me, ...), custom_call_target="tpu_custom_call" | custom-call | bytes 99630000 | tf_op jit(solution)/shard_map/coarse_levels/pallas_call | solution.py:515
  125.0 4.8 %all-to-all-start.2 = ((bf16[8,128,128]{2,1,0:T(8,128)(2,1)}), bf16[8,128,128]{2,1,0:T(8,128)(2,1)S(1)}, u32[]{:S(2)}, u32[]{:S(2)}) async-start(bf16[8,128,128]{2,1,0:T(8,128)(2,1)} %get-tuple-element.73), calls=%async_computation.2 | async-start | bytes 524288 | tf_op jit(solution)/shard_map/all_to_all | solution.py:793
  131.9 4.7 %collective-permute-start.22 = (bf16[512,128]{1,0:T(8,128)(2,1)}, bf16[512,128]{1,0:T(8,128)(2,1)S(1)}, u32[]{:S(2)}, u32[]{:S(2)}) collective-permute-start(bf16[512,128]{1,0:T(8,128)(2,1)} %get-tuple-element.72), channel_id=1, source_target_pairs={{0,7},{1,6},{2,5},{3,4},{4,3},{5,2},{6,1},{7,0},{8,15},{9,14},{10,... | collective-permute-start | bytes 393224 | tf_op jit(solution)/shard_map/ppermute | solution.py:810
  139.8 4.3 %collective-permute-done.18.refs_0_ = bf16[512,128]{1,0:T(8,128)(2,1)S(1)} collective-permute-done((bf16[512,128]{1,0:T(8,128)(2,1)S(1)}, bf16[512,128]{1,0:T(8,128)(2,1)S(1)}, u32[]{:S(2)}, u32[]{:S(2)}) %collective-permute-start.18) | collective-permute-done | bytes 131104 | tf_op jit(solution)/shard_map/ppermute | solution.py:810
  145.7 2.4 %grad_own_one_send.1 = bf16[8,128,128]{2,1,0:T(8,128)(2,1)} custom-call(s32[8,128]{1,0:T(8,128)} %get-tuple-element.58.refs_12_.table, f32[512,128]{1,0:T(8,128)} %get-tuple-element.65.gx, bf16[512,128]{1,0:T(8,128)(2,1)} %copy-done.24, bf16[512,128]{1,0:T(8,128)(2,1)} %copy-done.25, bf16[512,128]{1,0:T(8,128)(2,1)} %copy-done.22, bf16[512,128]{1,0:T(8,128)(2,1)} %copy-done.23), custom_call_target="tpu_custom_call" | custom-call | bytes 33210000 | tf_op jit(solution)/shard_map/grad_own_one_send/pallas_call | solution.py:558
  148.1 3.8 %all-to-all-start.3 = ((bf16[8,128,128]{2,1,0:T(8,128)(2,1)}), bf16[8,128,128]{2,1,0:T(8,128)(2,1)S(1)}, u32[]{:S(2)}, u32[]{:S(2)}) async-start(bf16[8,128,128]{2,1,0:T(8,128)(2,1)} %grad_own_one_send.1), calls=%async_computation.3 | async-start | bytes 524288 | tf_op jit(solution)/shard_map/all_to_all | solution.py:793
  151.9 8.8 %node_out.1 = bf16[8192,128]{1,0:T(8,128)(2,1)} custom-call(s32[16,8]{1,0:T(8,128)} %copy.38.cols, s32[1,1024]{1,0:T(1,128)} %get-tuple-element.49.place, bf16[8,128,128]{2,1,0:T(8,128)(2,1)} %copy-done.1, bf16[16,64,512]{2,1,0:T(8,128)(2,1)} %pool.9, bf16[8192,128]{1,0:T(8,128)(2,1)} %get-tuple-element.54.src.base), custom_call_target="tpu_custom_call" | custom-call | bytes 99630000 | tf_op jit(solution)/shard_map/node_out/pallas_call | solution.py:595
  160.6 6.1 %all-to-all-start.4 = ((f32[32,32,128]{2,1,0:T(8,128)}), f32[32,32,128]{2,1,0:T(8,128)S(1)}, u32[]{:S(2)}, u32[]{:S(2)}) async-start(f32[32,32,128]{2,1,0:T(8,128)} %bitcast.10), calls=%async_computation.4 | async-start | bytes 1048576 | tf_op jit(solution)/shard_map/all_to_all | solution.py:856
  166.7 14.4 %fine_layer_backward.1 = (f32[8192,128]{1,0:T(8,128)}, bf16[8192,128]{1,0:T(8,128)(2,1)}, f32[512,128]{1,0:T(8,128)}) custom-call(s32[16,8]{1,0:T(8,128)} %copy.38.cols, s32[1,1024]{1,0:T(1,128)} %get-tuple-element.49.place, bf16[8,128,128]{2,1,0:T(8,128)(2,1)} %copy-done.2, bf16[16,64,512]{2,1,0:T(8,128)(2,1)} %pool.9, bf16[8192,128]{1,0:T(8,128)(2,1)} %cot.3, ...), custom_call_target="tpu_custom_call" | custom-call | bytes 210330000 | tf_op jit(solution)/shard_map/fine_layer_backward/pallas_call | solution.py:638
  183.1 3.9 %all-to-all-start.5 = ((f32[32,16,128]{2,1,0:T(8,128)}), f32[32,16,128]{2,1,0:T(8,128)S(1)}, u32[]{:S(2)}, u32[]{:S(2)}) async-start(f32[32,16,128]{2,1,0:T(8,128)} %bitcast.31), calls=%async_computation.5 | async-start | bytes 524288 | tf_op jit(solution)/shard_map/all_to_all | solution.py:856
  187.0 4.6 %spread_edge.1 = (bf16[1024,128]{1,0:T(8,128)(2,1)}, f32[2048,128]{1,0:T(8,128)}) custom-call(s32[128,12]{1,0:T(8,128)} %copy.37.cols, bf16[128,64,768]{2,1,0:T(8,128)(2,1)} %adj_b.1, bf16[8192,128]{1,0:T(8,128)(2,1)} %get-tuple-element.83.gmsg.gmsg_a.gmsg_b, f32[8192,128]{1,0:T(8,128)} %get-tuple-element.84.gx.gx_a.gx_b), custom_call_target="tpu_custom_call" | custom-call | bytes 33210000 | tf_op jit(solution)/shard_map/spread_edge/pallas_call | solution.py:681
  191.6 6.0 %all-to-all-done.5 = f32[32,16,128]{2,1,0:T(8,128)S(1)} async-done(((f32[32,16,128]{2,1,0:T(8,128)}), f32[32,16,128]{2,1,0:T(8,128)S(1)}, u32[]{:S(2)}, u32[]{:S(2)}) %all-to-all-start.5) | async-done | bytes 262176 | tf_op jit(solution)/shard_map/all_to_all | solution.py:856
  198.5 2.6 %all-to-all-start.6 = ((bf16[32,48,128]{2,1,0:T(8,128)(2,1)}), bf16[32,48,128]{2,1,0:T(8,128)(2,1)S(1)}, u32[]{:S(2)}, u32[]{:S(2)}) async-start(bf16[32,48,128]{2,1,0:T(8,128)(2,1)} %broadcast_in_dim.2), calls=%async_computation.6 | async-start | bytes 786432 | tf_op jit(solution)/shard_map/all_to_all | solution.py:861
  202.1 4.6 %collective-permute-start.24 = (bf16[512,128]{1,0:T(8,128)(2,1)S(1)}, bf16[512,128]{1,0:T(8,128)(2,1)S(1)}, u32[]{:S(2)}, u32[]{:S(2)}) collective-permute-start(bf16[512,128]{1,0:T(8,128)(2,1)S(1)} %get-tuple-element.99), channel_id=1, source_target_pairs={{1,0},{2,1},{3,2},{4,3},{5,4},{6,5},{7,6},{0,7},{9,8},{10,9},{11,1... | collective-permute-start | bytes 393224 | tf_op jit(solution)/shard_map/ppermute | solution.py:805
  206.7 15.7 %spread_inner.1 = (bf16[8192,128]{1,0:T(8,128)(2,1)}, f32[1024,128]{1,0:T(8,128)}) custom-call(s32[128,12]{1,0:T(8,128)} %copy.37.cols, bf16[128,64,768]{2,1,0:T(8,128)(2,1)} %adj_b.1, bf16[128,64,768]{2,1,0:T(8,128)(2,1)} %adj_b.1, bf16[8192,128]{1,0:T(8,128)(2,1)} %get-tuple-element.83.gmsg.gmsg_a.gmsg_b, ...), custom_call_target="tpu_custom_call" | custom-call | bytes 199260000 | tf_op jit(solution)/shard_map/spread_inner/pallas_call | solution.py:736
  (131 shorter events, 40.9 us)
Async XLA Ops:
  9.5 45.4 %all-to-all-start = ((bf16[8,656,128]{2,1,0:T(8,128)(2,1)}), bf16[8,656,128]{2,1,0:T(8,128)(2,1)S(1)}, u32[]{:S(2)}, u32[]{:S(2)}) async-start(bf16[8,656,128]{2,1,0:T(8,128)(2,1)} %get-tuple-element.50), calls=%async_computation | async-start | bytes 2686976 | tf_op jit(solution)/shard_map/all_to_all | solution.py:793
  17.9 24.1 %collective-permute-start.1 = (bf16[512,128]{1,0:T(8,128)(2,1)S(1)}, bf16[512,128]{1,0:T(8,128)(2,1)S(1)}, u32[]{:S(2)}, u32[]{:S(2)}) collective-permute-start(bf16[512,128]{1,0:T(8,128)(2,1)S(1)} %get-tuple-element.93), channel_id=1, source_target_pairs={{1,0},{2,1},{3,2},{4,3},{5,4},{6,5},{7,6},{0,7},{9,8},{10,9},{11,1... | collective-permute-start | bytes 393224 | tf_op jit(solution)/shard_map/ppermute | solution.py:805
  22.7 23.8 %collective-permute-start = (bf16[512,128]{1,0:T(8,128)(2,1)S(1)}, bf16[512,128]{1,0:T(8,128)(2,1)S(1)}, u32[]{:S(2)}, u32[]{:S(2)}) collective-permute-start(bf16[512,128]{1,0:T(8,128)(2,1)S(1)} %get-tuple-element.94), channel_id=1, source_target_pairs={{0,1},{1,2},{2,3},{3,4},{4,5},{5,6},{6,7},{7,0},{8,9},{9,10},{10,1... | collective-permute-start | bytes 393224 | tf_op jit(solution)/shard_map/ppermute | solution.py:804
  55.0 17.7 %copy-start = (bf16[8,656,128]{2,1,0:T(8,128)(2,1)}, bf16[8,656,128]{2,1,0:T(8,128)(2,1)S(1)}, u32[]{:S(2)}) copy-start(bf16[8,656,128]{2,1,0:T(8,128)(2,1)S(1)} %all-to-all-done.first.refs_9_) | copy-start | bytes 4030468
  74.8 7.6 %collective-permute-start.5 = (bf16[512,128]{1,0:T(8,128)(2,1)}, bf16[512,128]{1,0:T(8,128)(2,1)S(1)}, u32[]{:S(2)}, u32[]{:S(2)}) collective-permute-start(bf16[512,128]{1,0:T(8,128)(2,1)} %place_own_one.1.refs_0_.refs_13_), channel_id=1, source_target_pairs={{0,4},{1,5},{2,6},{3,7},{4,0},{5,1},{6,2},{7,3},{8,12},{9,13},{10,... | collective-permute-start | bytes 393224 | tf_op jit(solution)/shard_map/ppermute | solution.py:810
  75.4 9.0 %collective-permute-start.3 = (bf16[512,128]{1,0:T(8,128)(2,1)}, bf16[512,128]{1,0:T(8,128)(2,1)S(1)}, u32[]{:S(2)}, u32[]{:S(2)}) collective-permute-start(bf16[512,128]{1,0:T(8,128)(2,1)} %place_own_one.1.refs_0_.refs_13_), channel_id=1, source_target_pairs={{0,2},{1,3},{2,0},{3,1},{4,6},{5,7},{6,4},{7,5},{8,10},{9,11},{10,... | collective-permute-start | bytes 393224 | tf_op jit(solution)/shard_map/ppermute | solution.py:810
  82.4 5.0 %collective-permute-start.6 = (bf16[512,128]{1,0:T(8,128)(2,1)S(1)}, bf16[512,128]{1,0:T(8,128)(2,1)S(1)}, u32[]{:S(2)}, u32[]{:S(2)}) collective-permute-start(bf16[512,128]{1,0:T(8,128)(2,1)S(1)} %collective-permute-done.5.refs_4_), channel_id=1, source_target_pairs={{0,1},{1,0},{2,3},{3,2},{4,5},{5,4},{6,7},{7,6},{8,9},{9,8},{10,11... | collective-permute-start | bytes 393224 | tf_op jit(solution)/shard_map/ppermute | solution.py:810
  83.1 7.1 %collective-permute-start.2 = (bf16[512,128]{1,0:T(8,128)(2,1)}, bf16[512,128]{1,0:T(8,128)(2,1)S(1)}, u32[]{:S(2)}, u32[]{:S(2)}) collective-permute-start(bf16[512,128]{1,0:T(8,128)(2,1)} %place_own_one.1.refs_0_.refs_13_), channel_id=1, source_target_pairs={{0,1},{1,0},{2,3},{3,2},{4,5},{5,4},{6,7},{7,6},{8,9},{9,8},{10,11... | collective-permute-start | bytes 393224 | tf_op jit(solution)/shard_map/ppermute | solution.py:810
  84.4 5.8 %collective-permute-start.7 = (bf16[512,128]{1,0:T(8,128)(2,1)S(1)}, bf16[512,128]{1,0:T(8,128)(2,1)S(1)}, u32[]{:S(2)}, u32[]{:S(2)}) collective-permute-start(bf16[512,128]{1,0:T(8,128)(2,1)S(1)} %collective-permute-done.5.refs_4_), channel_id=1, source_target_pairs={{0,2},{1,3},{2,0},{3,1},{4,6},{5,7},{6,4},{7,5},{8,10},{9,11},{10,... | collective-permute-start | bytes 393224 | tf_op jit(solution)/shard_map/ppermute | solution.py:810
  84.4 5.8 %collective-permute-start.4 = (bf16[512,128]{1,0:T(8,128)(2,1)S(1)}, bf16[512,128]{1,0:T(8,128)(2,1)S(1)}, u32[]{:S(2)}, u32[]{:S(2)}) collective-permute-start(bf16[512,128]{1,0:T(8,128)(2,1)S(1)} %collective-permute-done.3.refs_2_), channel_id=1, source_target_pairs={{0,1},{1,0},{2,3},{3,2},{4,5},{5,4},{6,7},{7,6},{8,9},{9,8},{10,11... | collective-permute-start | bytes 393224 | tf_op jit(solution)/shard_map/ppermute | solution.py:810
  87.3 5.0 %collective-permute-start.8 = (bf16[512,128]{1,0:T(8,128)(2,1)S(1)}, bf16[512,128]{1,0:T(8,128)(2,1)S(1)}, u32[]{:S(2)}, u32[]{:S(2)}) collective-permute-start(bf16[512,128]{1,0:T(8,128)(2,1)S(1)} %collective-permute-done.6.refs_5_), channel_id=1, source_target_pairs={{0,2},{1,3},{2,0},{3,1},{4,6},{5,7},{6,4},{7,5},{8,10},{9,11},{10,... | collective-permute-start | bytes 393224 | tf_op jit(solution)/shard_map/ppermute | solution.py:810
  96.1 7.6 %collective-permute-start.12 = (bf16[256,256]{1,0:T(8,128)(2,1)}, bf16[256,256]{1,0:T(8,128)(2,1)S(1)}, u32[]{:S(2)}, u32[]{:S(2)}) collective-permute-start(bf16[256,256]{1,0:T(8,128)(2,1)} %get-tuple-element.60.refs_0_), channel_id=1, source_target_pairs={{0,4},{1,5},{2,6},{3,7},{4,0},{5,1},{6,2},{7,3},{8,12},{9,13},{10,... | collective-permute-start | bytes 393224 | tf_op jit(solution)/shard_map/ppermute | solution.py:810
  97.9 7.9 %collective-permute-start.10 = (bf16[256,256]{1,0:T(8,128)(2,1)}, bf16[256,256]{1,0:T(8,128)(2,1)S(1)}, u32[]{:S(2)}, u32[]{:S(2)}) collective-permute-start(bf16[256,256]{1,0:T(8,128)(2,1)} %get-tuple-element.60.refs_0_), channel_id=1, source_target_pairs={{0,2},{1,3},{2,0},{3,1},{4,6},{5,7},{6,4},{7,5},{8,10},{9,11},{10,... | collective-permute-start | bytes 393224 | tf_op jit(solution)/shard_map/ppermute | solution.py:810
  103.7 5.0 %collective-permute-start.13 = (bf16[256,256]{1,0:T(8,128)(2,1)S(1)}, bf16[256,256]{1,0:T(8,128)(2,1)S(1)}, u32[]{:S(2)}, u32[]{:S(2)}) collective-permute-start(bf16[256,256]{1,0:T(8,128)(2,1)S(1)} %collective-permute-done.12.refs_4_), channel_id=1, source_target_pairs={{0,1},{1,0},{2,3},{3,2},{4,5},{5,4},{6,7},{7,6},{8,9},{9,8},{10,11... | collective-permute-start | bytes 393224 | tf_op jit(solution)/shard_map/ppermute | solution.py:810
  104.5 5.6 %collective-permute-start.9 = (bf16[256,256]{1,0:T(8,128)(2,1)}, bf16[256,256]{1,0:T(8,128)(2,1)S(1)}, u32[]{:S(2)}, u32[]{:S(2)}) collective-permute-start(bf16[256,256]{1,0:T(8,128)(2,1)} %get-tuple-element.60.refs_0_), channel_id=1, source_target_pairs={{0,1},{1,0},{2,3},{3,2},{4,5},{5,4},{6,7},{7,6},{8,9},{9,8},{10,11... | collective-permute-start | bytes 393224 | tf_op jit(solution)/shard_map/ppermute | solution.py:810
  105.7 5.0 %collective-permute-start.14 = (bf16[256,256]{1,0:T(8,128)(2,1)S(1)}, bf16[256,256]{1,0:T(8,128)(2,1)S(1)}, u32[]{:S(2)}, u32[]{:S(2)}) collective-permute-start(bf16[256,256]{1,0:T(8,128)(2,1)S(1)} %collective-permute-done.12.refs_4_), channel_id=1, source_target_pairs={{0,2},{1,3},{2,0},{3,1},{4,6},{5,7},{6,4},{7,5},{8,10},{9,11},{10,... | collective-permute-start | bytes 393224 | tf_op jit(solution)/shard_map/ppermute | solution.py:810
  105.7 5.7 %collective-permute-start.11 = (bf16[256,256]{1,0:T(8,128)(2,1)S(1)}, bf16[256,256]{1,0:T(8,128)(2,1)S(1)}, u32[]{:S(2)}, u32[]{:S(2)}) collective-permute-start(bf16[256,256]{1,0:T(8,128)(2,1)S(1)} %collective-permute-done.10.refs_2_), channel_id=1, source_target_pairs={{0,1},{1,0},{2,3},{3,2},{4,5},{5,4},{6,7},{7,6},{8,9},{9,8},{10,11... | collective-permute-start | bytes 393224 | tf_op jit(solution)/shard_map/ppermute | solution.py:810
  108.7 5.0 %collective-permute-start.15 = (bf16[256,256]{1,0:T(8,128)(2,1)S(1)}, bf16[256,256]{1,0:T(8,128)(2,1)S(1)}, u32[]{:S(2)}, u32[]{:S(2)}) collective-permute-start(bf16[256,256]{1,0:T(8,128)(2,1)S(1)} %collective-permute-done.13.refs_5_), channel_id=1, source_target_pairs={{0,2},{1,3},{2,0},{3,1},{4,6},{5,7},{6,4},{7,5},{8,10},{9,11},{10,... | collective-permute-start | bytes 393224 | tf_op jit(solution)/shard_map/ppermute | solution.py:810
  123.8 12.8 %collective-permute-start.16 = (bf16[512,128]{1,0:T(8,128)(2,1)}, bf16[512,128]{1,0:T(8,128)(2,1)S(1)}, u32[]{:S(2)}, u32[]{:S(2)}) collective-permute-start(bf16[512,128]{1,0:T(8,128)(2,1)} %get-tuple-element.67), channel_id=1, source_target_pairs={{0,1},{1,0},{2,3},{3,2},{4,5},{5,4},{6,7},{7,6},{8,9},{9,8},{10,11... | collective-permute-start | bytes 393224 | tf_op jit(solution)/shard_map/ppermute | solution.py:810
  124.7 11.9 %collective-permute-start.17 = (bf16[512,128]{1,0:T(8,128)(2,1)}, bf16[512,128]{1,0:T(8,128)(2,1)S(1)}, u32[]{:S(2)}, u32[]{:S(2)}) collective-permute-start(bf16[512,128]{1,0:T(8,128)(2,1)} %get-tuple-element.68), channel_id=1, source_target_pairs={{0,2},{1,3},{2,0},{3,1},{4,6},{5,7},{6,4},{7,5},{8,10},{9,11},{10,... | collective-permute-start | bytes 393224 | tf_op jit(solution)/shard_map/ppermute | solution.py:810
  125.0 23.1 %all-to-all-start.2 = ((bf16[8,128,128]{2,1,0:T(8,128)(2,1)}), bf16[8,128,128]{2,1,0:T(8,128)(2,1)S(1)}, u32[]{:S(2)}, u32[]{:S(2)}) async-start(bf16[8,128,128]{2,1,0:T(8,128)(2,1)} %get-tuple-element.73), calls=%async_computation.2 | async-start | bytes 524288 | tf_op jit(solution)/shard_map/all_to_all | solution.py:793
  129.9 7.8 %collective-permute-start.19 = (bf16[512,128]{1,0:T(8,128)(2,1)}, bf16[512,128]{1,0:T(8,128)(2,1)S(1)}, u32[]{:S(2)}, u32[]{:S(2)}) collective-permute-start(bf16[512,128]{1,0:T(8,128)(2,1)} %get-tuple-element.70), channel_id=1, source_target_pairs={{0,1},{1,0},{2,3},{3,2},{4,5},{5,4},{6,7},{7,6},{8,9},{9,8},{10,11... | collective-permute-start | bytes 393224 | tf_op jit(solution)/shard_map/ppermute | solution.py:810
  131.9 7.9 %collective-permute-start.21 = (bf16[512,128]{1,0:T(8,128)(2,1)}, bf16[512,128]{1,0:T(8,128)(2,1)S(1)}, u32[]{:S(2)}, u32[]{:S(2)}) collective-permute-start(bf16[512,128]{1,0:T(8,128)(2,1)} %get-tuple-element.71), channel_id=1, source_target_pairs={{0,1},{1,0},{2,3},{3,2},{4,5},{5,4},{6,7},{7,6},{8,9},{9,8},{10,11... | collective-permute-start | bytes 393224 | tf_op jit(solution)/shard_map/ppermute | solution.py:810
  131.9 7.9 %collective-permute-start.22 = (bf16[512,128]{1,0:T(8,128)(2,1)}, bf16[512,128]{1,0:T(8,128)(2,1)S(1)}, u32[]{:S(2)}, u32[]{:S(2)}) collective-permute-start(bf16[512,128]{1,0:T(8,128)(2,1)} %get-tuple-element.72), channel_id=1, source_target_pairs={{0,7},{1,6},{2,5},{3,4},{4,3},{5,2},{6,1},{7,0},{8,15},{9,14},{10,... | collective-permute-start | bytes 393224 | tf_op jit(solution)/shard_map/ppermute | solution.py:810
  137.6 6.5 %collective-permute-start.18 = (bf16[512,128]{1,0:T(8,128)(2,1)S(1)}, bf16[512,128]{1,0:T(8,128)(2,1)S(1)}, u32[]{:S(2)}, u32[]{:S(2)}) collective-permute-start(bf16[512,128]{1,0:T(8,128)(2,1)S(1)} %add_convert_fusion.1), channel_id=1, source_target_pairs={{0,4},{1,5},{2,6},{3,7},{4,0},{5,1},{6,2},{7,3},{8,12},{9,13},{10,... | collective-permute-start | bytes 393224 | tf_op jit(solution)/shard_map/ppermute | solution.py:810
  138.6 6.4 %collective-permute-start.20 = (bf16[512,128]{1,0:T(8,128)(2,1)S(1)}, bf16[512,128]{1,0:T(8,128)(2,1)S(1)}, u32[]{:S(2)}, u32[]{:S(2)}) collective-permute-start(bf16[512,128]{1,0:T(8,128)(2,1)S(1)} %add_convert_fusion), channel_id=1, source_target_pairs={{0,2},{1,3},{2,0},{3,1},{4,6},{5,7},{6,4},{7,5},{8,10},{9,11},{10,... | collective-permute-start | bytes 393224 | tf_op jit(solution)/shard_map/ppermute | solution.py:810
  148.1 12.5 %all-to-all-start.3 = ((bf16[8,128,128]{2,1,0:T(8,128)(2,1)}), bf16[8,128,128]{2,1,0:T(8,128)(2,1)S(1)}, u32[]{:S(2)}, u32[]{:S(2)}) async-start(bf16[8,128,128]{2,1,0:T(8,128)(2,1)} %grad_own_one_send.1), calls=%async_computation.3 | async-start | bytes 524288 | tf_op jit(solution)/shard_map/all_to_all | solution.py:793
  160.6 22.4 %all-to-all-start.4 = ((f32[32,32,128]{2,1,0:T(8,128)}), f32[32,32,128]{2,1,0:T(8,128)S(1)}, u32[]{:S(2)}, u32[]{:S(2)}) async-start(f32[32,32,128]{2,1,0:T(8,128)} %bitcast.10), calls=%async_computation.4 | async-start | bytes 1048576 | tf_op jit(solution)/shard_map/all_to_all | solution.py:856
  183.1 14.6 %all-to-all-start.5 = ((f32[32,16,128]{2,1,0:T(8,128)}), f32[32,16,128]{2,1,0:T(8,128)S(1)}, u32[]{:S(2)}, u32[]{:S(2)}) async-start(f32[32,16,128]{2,1,0:T(8,128)} %bitcast.31), calls=%async_computation.5 | async-start | bytes 524288 | tf_op jit(solution)/shard_map/all_to_all | solution.py:856
  198.5 26.5 %all-to-all-start.6 = ((bf16[32,48,128]{2,1,0:T(8,128)(2,1)}), bf16[32,48,128]{2,1,0:T(8,128)(2,1)S(1)}, u32[]{:S(2)}, u32[]{:S(2)}) async-start(bf16[32,48,128]{2,1,0:T(8,128)(2,1)} %broadcast_in_dim.2), calls=%async_computation.6 | async-start | bytes 786432 | tf_op jit(solution)/shard_map/all_to_all | solution.py:861
  202.1 20.3 %collective-permute-start.24 = (bf16[512,128]{1,0:T(8,128)(2,1)S(1)}, bf16[512,128]{1,0:T(8,128)(2,1)S(1)}, u32[]{:S(2)}, u32[]{:S(2)}) collective-permute-start(bf16[512,128]{1,0:T(8,128)(2,1)S(1)} %get-tuple-element.99), channel_id=1, source_target_pairs={{1,0},{2,1},{3,2},{4,3},{5,4},{6,5},{7,6},{0,7},{9,8},{10,9},{11,1... | collective-permute-start | bytes 393224 | tf_op jit(solution)/shard_map/ppermute | solution.py:805
  206.7 15.8 %collective-permute-start.23 = (bf16[512,128]{1,0:T(8,128)(2,1)S(1)}, bf16[512,128]{1,0:T(8,128)(2,1)S(1)}, u32[]{:S(2)}, u32[]{:S(2)}) collective-permute-start(bf16[512,128]{1,0:T(8,128)(2,1)S(1)} %get-tuple-element.100), channel_id=1, source_target_pairs={{0,1},{1,2},{2,3},{3,4},{4,5},{5,6},{6,7},{7,0},{8,9},{9,10},{10,1... | collective-permute-start | bytes 393224 | tf_op jit(solution)/shard_map/ppermute | solution.py:804
  (28 other events, 149.6 us)

commit v3 on v2

v3 whole, which is shorter than its diff:
```python
import functools
import math

import jax
import jax.numpy as jnp
from jax import lax
from jax.experimental import pallas as pl
from jax.experimental.pallas import tpu as pltpu
from jax.sharding import PartitionSpec as P

BF = jnp.bfloat16
F32 = jnp.float32
HALO = 512
BLK = 64
CHUNK = 8
EXTRA = 16
VMEM_LIMIT = 56 * 1024 * 1024

VM = pl.BlockSpec(memory_space=pltpu.VMEM)
SM = pl.BlockSpec(memory_space=pltpu.SMEM)


def params():
    return pltpu.CompilerParams(vmem_limit_bytes=VMEM_LIMIT)


def takes(microseconds):
    return pl.CostEstimate(flops=0, bytes_accessed=int(3 * microseconds * 3.69e6), transcendentals=0)


def dot(a, b):
    return jnp.dot(a, b, preferred_element_type=F32)


def dot_nt(a, b):
    return lax.dot_general(a, b, (((1,), (1,)), ((), ())), preferred_element_type=F32)


def dot_tn(a, b):
    return lax.dot_general(a, b, (((0,), (0,)), ((), ())), preferred_element_type=F32)


def iota(shape, dim):
    return lax.broadcasted_iota(jnp.int32, shape, dim)


def as_ones(mask):
    return jnp.where(mask, 1.0, 0.0).astype(BF)


def tile_at(ref, index):
    return ref[pl.ds(pl.multiple_of(index * BLK, BLK), BLK), :]


def apply_row(block, cols, r, count, ref, shift=0):
    picked = jnp.concatenate([tile_at(ref, cols[r, i] - shift) for i in range(count)], axis=0)
    return dot(block, picked)


def spread_row(block, cols, r, count, rows, acc, shift=0):
    spread = dot_tn(block, rows)
    for i in range(count):
        at = pl.ds(pl.multiple_of((cols[r, i] - shift) * BLK, BLK), BLK)
        acc[at, :] += spread[i * BLK : (i + 1) * BLK]


def place_matrix(row_table, first, count):
    n = row_table.shape[1]
    return as_ones(row_table == iota((count, n), 0) + first)


def digits(values):
    shifted = values + 1
    return (shifted >> 6).astype(F32), (shifted & 63).astype(F32)


def from_digits(high, low):
    return (high.astype(F32) * 64.0 + low.astype(F32)).astype(jnp.int32) - 1


def lane_rows(values):
    n = values.shape[1]
    rows = []
    for at in range(0, n, 128):
        row = values[:, at : min(at + 128, n)]
        if row.shape[1] < 128:
            row = jnp.concatenate([row, jnp.zeros((1, 128 - row.shape[1]), F32)], axis=1)
        rows.append(row)
    return rows


def pack_slots(
    count, count_two, owner_ref, two_ref, cols_two, rows_ref, place_cols_out, mine_out, send_out, groups, balance
):
    slots = owner_ref.shape[1]
    cap = slots // groups
    feature = rows_ref.shape[1] // 2
    owner = owner_ref[...]
    live = iota((1, slots), 1) < count[0]
    rows = max(16, groups)
    target = iota((rows, slots), 0)
    low = target * balance
    hit = (owner >= low) & (owner < low + balance) & live
    onehot = jnp.where(hit, 1.0, 0.0)
    upper = as_ones(iota((slots, slots), 0) <= iota((slots, slots), 1))
    running = dot(onehot.astype(BF), upper)
    rank = jnp.sum(onehot * running, axis=0, keepdims=True) - 1.0
    base = jnp.sum(jnp.where(hit, target * cap, 0).astype(F32), axis=0, keepdims=True)
    start = jnp.sum(jnp.where(hit, low, 0).astype(F32), axis=0, keepdims=True)
    place = jnp.where(live, (base + rank).astype(jnp.int32), slots)
    place_cols_out[...] = jnp.broadcast_to(place.astype(F32), (128, slots)).T
    two = two_ref[...]
    two = jnp.where(iota(two.shape, 1) < count_two[0], two, -1)
    mine_out[...] = two
    two_high, two_low = digits(two)
    shared = lane_rows(two_high) + lane_rows(two_low)
    for r in range(cols_two.shape[0]):
        shared = shared + lane_rows(cols_two[r : r + 1, :].astype(F32))
    local_high, local_low = digits(owner - start.astype(jnp.int32))
    kind = iota((rows, slots), 0)
    parts = jnp.where(kind == 0, local_high, jnp.where(kind == 1, local_low, 0.0)).astype(BF)
    for d in range(groups):
        ones = place_matrix(place, d * cap, cap)
        packed = dot(ones, rows_ref[...]).astype(BF)
        send_out[d, 0:cap, :] = packed[:, :feature]
        send_out[d, cap : 2 * cap, :] = packed[:, feature:]
        code = dot_nt(parts, ones)
        if cap < 128:
            code = jnp.concatenate([code, jnp.zeros((rows, 128 - cap), F32)], axis=1)
        tail = [code[0:1], code[1:2]] + shared
        tail = jnp.concatenate(tail + [jnp.zeros((EXTRA - len(tail), 128), F32)], axis=0)
        send_out[d, 2 * cap :, :] = tail.astype(BF)


def level_of(level, w_in, w_out, bias):
    return w_in.at[level], w_out.at[level], bias.at[pl.ds(level, 1), :]


def layer_rows(x, message, w_in, w_out, bias):
    pre = dot(jnp.concatenate([x, message], axis=1), w_in) + bias
    hidden = (pre * jax.nn.sigmoid(pre)).astype(BF)
    return (x.astype(F32) + dot(hidden, w_out)).astype(BF)


def fine_kernel(
    me, cols, pool_cols, count, count_two, prev, after, owner, two, cols_two, feats_hbm, adj_hbm, pool_hbm, cot_hbm,
    w_in, w_out, bias, msg_out, res_out, send_out, place_cols_out, mine_out,
    ext, adj, res, pool, cot, slots_scr, feats_sem, adj_sem, pool_sem, cot_sem, *, groups, balance,
):
    w_in, w_out, bias = level_of(0, w_in, w_out, bias)
    k = cols.shape[1]
    chunk = pl.program_id(0)
    rows = CHUNK * BLK
    width = prev.shape[0]
    chunks = adj.shape[0] // CHUNK

    def feats_copy(c):
        at = pl.multiple_of(c * rows, rows)
        return pltpu.make_async_copy(
            feats_hbm.at[pl.ds(at, rows), :], ext.at[pl.ds(width + at, rows), :], feats_sem.at[c]
        )

    def adj_copy(c):
        at = pl.ds(c * CHUNK, CHUNK)
        return pltpu.make_async_copy(adj_hbm.at[at], adj.at[at], adj_sem.at[c])

    def pool_copy():
        return pltpu.make_async_copy(pool_hbm, pool, pool_sem)

    def cot_copy():
        return pltpu.make_async_copy(cot_hbm, cot, cot_sem)

    @pl.when(chunk == 0)
    def _():
        feats_copy(0).start()
        for c in range(chunks):
            if c + 1 < chunks:
                feats_copy(c + 1).start()
            adj_copy(c).start()
        pool_copy().start()
        cot_copy().start()
        ext[0:width, :] = jnp.where(me[0] > 0, prev[...], jnp.zeros_like(prev))
        ext[width + chunks * rows :, :] = jnp.where(me[0] < groups - 1, after[...], jnp.zeros_like(after))
        feats_copy(0).wait()

    @pl.when(chunk + 1 < chunks)
    def _():
        feats_copy(chunk + 1).wait()

    @pl.when(chunk < chunks)
    def _():
        adj_copy(chunk).wait()
        for j in range(CHUNK):
            block = apply_row(adj[chunk * CHUNK + j], cols, chunk * CHUNK + j, k, ext)
            msg_out[j * BLK : (j + 1) * BLK, :] = block.astype(BF)
        x = ext[pl.ds(pl.multiple_of(width + chunk * rows, rows), rows), :]
        result = layer_rows(x, msg_out[...], w_in[...], w_out[...], bias[...])
        res_out[...] = result
        res[pl.ds(pl.multiple_of(chunk * rows, rows), rows), :] = result

    @pl.when(chunk == chunks)
    def _():
        pool_copy().wait()
        cot_copy().wait()
        k = pool_cols.shape[1]
        for q in range(pool.shape[0]):
            picked = [
                jnp.concatenate([tile_at(ref, pool_cols[q, i]) for i in range(k)], axis=0) for ref in (res, cot)
            ]
            slots_scr[q * BLK : (q + 1) * BLK, :] = dot(pool[q], jnp.concatenate(picked, axis=1)).astype(BF)
        pack_slots(
            count, count_two, owner, two, cols_two, slots_scr, place_cols_out, mine_out, send_out, groups, balance
        )


def fine_forward(
    me, cols, pool_cols, count, count_two, prev, after, owner, two, cols_two, feats, adj, pool, cot, w_in, w_out, bias,
    groups, balance,
):
    total, feature = feats.shape
    slots = owner.shape[1]
    rows = CHUNK * BLK
    chunks = total // rows
    hbm = pl.BlockSpec(memory_space=pl.ANY)
    spec = pl.BlockSpec((rows, feature), lambda c: (jnp.minimum(c, chunks - 1), 0))
    return pl.pallas_call(
        functools.partial(fine_kernel, groups=groups, balance=balance),
        grid=(chunks + 1,),
        out_shape=(
            jax.ShapeDtypeStruct((total, feature), BF),
            jax.ShapeDtypeStruct((total, feature), BF),
            jax.ShapeDtypeStruct((groups, 2 * (slots // groups) + EXTRA, feature), BF),
            jax.ShapeDtypeStruct((slots, 128), F32),
            jax.ShapeDtypeStruct(two.shape, jnp.int32),
        ),
        in_specs=[SM] * 5 + [VM] * 5 + [hbm] * 4 + [VM] * 3,
        out_specs=(spec, spec, VM, VM, VM),
        scratch_shapes=[
            pltpu.VMEM((total + 2 * HALO, feature), BF),
            pltpu.VMEM(adj.shape, BF),
            pltpu.VMEM((total, feature), BF),
            pltpu.VMEM(pool.shape, BF),
            pltpu.VMEM((total, feature), BF),
            pltpu.VMEM((slots, 2 * feature), BF),
            pltpu.SemaphoreType.DMA((chunks,)),
            pltpu.SemaphoreType.DMA((chunks,)),
            pltpu.SemaphoreType.DMA,
            pltpu.SemaphoreType.DMA,
        ],
        compiler_params=params(),
        cost_estimate=takes(20),
        name="fine_forward",
    )(
        me, cols, pool_cols, count, count_two, prev, after, owner, two, cols_two, feats, adj, pool, cot,
        w_in, w_out, bias,
    )


def place_all(tables, got, n, offset):
    cap = tables[0].shape[1]
    own = jnp.zeros((n, got.shape[2]), F32)
    for d in range(got.shape[0]):
        own += dot(place_matrix(tables[d], 0, n), got[d, offset : offset + cap, :])
    return own.astype(BF)


def tables_from(got, cap):
    at = 2 * cap
    return [from_digits(got[d, at : at + 1, :], got[d, at + 1 : at + 2, :])[:, :cap] for d in range(got.shape[0])]


def place_kernel(got, own_out):
    cap = (got.shape[1] - EXTRA) // 2
    own_out[...] = place_all(tables_from(got, cap), got, own_out.shape[0], 0)


def place_rows(got, balance):
    return pl.pallas_call(
        place_kernel,
        out_shape=jax.ShapeDtypeStruct((balance, got.shape[2]), BF),
        in_specs=[VM],
        out_specs=VM,
        compiler_params=params(),
        cost_estimate=takes(3),
        name="place_own_one",
    )(got)


def place_pool_kernel(cols, got, pool, own_out, slots_out, table_out):
    k = cols.shape[1]
    cap = table_out.shape[1]
    tables = tables_from(got, cap)
    own_out[...] = place_all(tables, got, own_out.shape[0], cap)
    for d in range(got.shape[0]):
        table_out[d : d + 1, :] = tables[d]
    for q in range(pool.shape[0]):
        slots_out[q * BLK : (q + 1) * BLK, :] = apply_row(pool[q], cols, q, k, own_out).astype(BF)


def place_pool(cols, got, pool, balance, cap):
    groups, _, feature = got.shape
    return pl.pallas_call(
        place_pool_kernel,
        out_shape=(
            jax.ShapeDtypeStruct((balance, feature), BF),
            jax.ShapeDtypeStruct((pool.shape[0] * BLK, feature), BF),
            jax.ShapeDtypeStruct((groups, cap), jnp.int32),
        ),
        in_specs=[SM, VM, VM],
        out_specs=(VM, VM, VM),
        compiler_params=params(),
        cost_estimate=takes(3),
        name="place_grad_up_one",
    )(cols, got, pool)


def one_forward_kernel(me, cols, pool_cols, *refs):
    pieces = refs[:-10]
    gslots, adj, pool, w_in, w_out, bias, msg_out, res_out, slots_out, ctx = refs[-10:]
    w_in, w_out, bias = level_of(1, w_in, w_out, bias)
    own = pieces[0]
    n = own.shape[0]
    for hop, piece in enumerate(pieces):
        ctx[pl.ds(pl.multiple_of((me[0] ^ hop) * n, n), n), :] = piece[...]
    k = cols.shape[1]
    for r in range(adj.shape[0]):
        msg_out[r * BLK : (r + 1) * BLK, :] = apply_row(adj[r], cols, r, k, ctx).astype(BF)
    res_out[...] = layer_rows(own[...], msg_out[...], w_in[...], w_out[...], bias[...])
    k = pool_cols.shape[1]
    for q in range(pool.shape[0]):
        rows = apply_row(pool[q], pool_cols, q, k, res_out).astype(BF)
        slots_out[q * BLK : (q + 1) * BLK, 0 : rows.shape[1]] = rows
    slots_out[:, own.shape[1] :] = gslots[...]


def one_forward(me, cols, pool_cols, pieces, gslots, adj, pool, w_in, w_out, bias):
    own = pieces[0]
    own_shape = jax.ShapeDtypeStruct(own.shape, BF)
    return pl.pallas_call(
        one_forward_kernel,
        out_shape=(own_shape, own_shape, jax.ShapeDtypeStruct((gslots.shape[0], 2 * own.shape[1]), BF)),
        in_specs=[SM, SM, SM] + [VM] * (len(pieces) + 6),
        out_specs=(VM, VM, VM),
        scratch_shapes=[pltpu.VMEM((len(pieces) * own.shape[0], own.shape[1]), BF)],
        compiler_params=params(),
        cost_estimate=takes(3),
        name="level_one_forward",
    )(me, cols, pool_cols, *pieces, gslots, adj, pool, w_in, w_out, bias)


def grad_pre_rows(grad_low, x, message, w_in, w_out, bias):
    joined = jnp.concatenate([x, message], axis=1)
    pre = dot(joined, w_in) + bias
    sig = jax.nn.sigmoid(pre)
    hidden = (pre * sig).astype(BF)
    grad_pre = dot_nt(grad_low, w_out) * (sig * (1.0 + pre * (1.0 - sig)))
    return joined, hidden, grad_pre


def coarse_kernel(groups, me, cols_two, cols_one, pool_cols, *refs):
    slots_two, refs = refs[:groups], refs[groups:]
    adj_pieces, refs = refs[:groups], refs[groups:]
    (
        mine_two, first, adj_one, pool_two, table_one, own_one, msg_one, res_one, gup_one,
        w_in, w_out, bias, up_out, gx_out, sums_out,
    ) = refs[:15]
    part_outs, refs = refs[15 : 15 + groups - 1], refs[15 + groups - 1 :]
    both, adj_two, xs, gs, ms, hs, gps, rs, ctx_acc, up_acc, gmsg, gctx_acc = refs
    wi1, wo1, b1 = level_of(1, w_in, w_out, bias)
    wi2, wo2, b2 = level_of(2, w_in, w_out, bias)
    feature = own_one.shape[1]
    n2 = xs.shape[0]
    n1 = own_one.shape[0]
    slots = mine_two.shape[1]
    per = adj_two.shape[0] // groups
    for hop in range(groups):
        source = me[0] ^ hop
        both[pl.ds(pl.multiple_of(source * slots, slots), slots), :] = slots_two[hop][...]
        adj_two[pl.ds(source * per, per)] = adj_pieces[hop][...]
    cap = table_one.shape[1]
    lanes = slots // 128
    at = 2 * cap + 2
    table = jnp.concatenate(
        [
            from_digits(first[d, at + c : at + c + 1, :], first[d, at + lanes + c : at + lanes + c + 1, :])
            for d in range(first.shape[0])
            for c in range(lanes)
        ],
        axis=1,
    )
    step = min(256, n2)
    for v in range(0, n2, step):
        rows = dot(place_matrix(table, v, step), both[...]).astype(BF)
        xs[v : v + step, :] = rows[:, :feature]
        gs[v : v + step, :] = rows[:, feature:]
    k = cols_two.shape[1]
    for r in range(n2 // BLK):
        ms[r * BLK : (r + 1) * BLK, :] = apply_row(adj_two[r], cols_two, r, k, xs).astype(BF)
    ctx_acc[...] = jnp.zeros_like(ctx_acc)
    for v in range(0, n2, step):
        x, m, g = xs[v : v + step, :], ms[v : v + step, :], gs[v : v + step, :]
        joined, hidden, grad_pre = grad_pre_rows(g, x, m, wi2[...], wo2[...], b2[...])
        rs[v : v + step, :feature] = (x.astype(F32) + dot(hidden, wo2[...])).astype(BF)
        hs[v : v + step, :] = hidden
        gps[v : v + step, :] = grad_pre
        grad_joined = dot_nt(grad_pre.astype(BF), wi2[...])
        ctx_acc[v : v + step, :] += g.astype(F32) + grad_joined[:, :feature]
        gm = grad_joined[:, feature:].astype(BF)
        for j in range(step // BLK):
            r = v // BLK + j
            spread_row(adj_two[r], cols_two, r, k, gm[j * BLK : (j + 1) * BLK], ctx_acc)
    rs[:, feature:] = ctx_acc[...].astype(BF)
    balance = slots // 2
    at = pl.ds(pl.multiple_of(me[0] * balance, balance), balance)
    gp_own = gps[at, :]
    joined = jnp.concatenate([xs[at, :], ms[at, :]], axis=1)
    level = 3 * feature
    sums_out[level : level + 2 * feature, :] = dot_tn(joined, gp_own.astype(BF))
    sums_out[level + 2 * feature : 2 * level, :] = dot_tn(hs[at, :], gs[at, :])
    bias_two = jnp.sum(gp_own, axis=0, keepdims=True)
    mine = place_matrix(mine_two[...], 0, n2)
    back = dot_tn(mine, rs[...]).astype(BF)
    up_acc[:, :feature] = res_one[...].astype(F32)
    up_acc[:, feature:] = gup_one[...].astype(F32)
    k = pool_cols.shape[1]
    for q in range(pool_two.shape[0]):
        spread_row(pool_two[q], pool_cols, q, k, back[q * BLK : (q + 1) * BLK], up_acc)
    up_low = up_acc[:, :feature].astype(BF)
    for d in range(table_one.shape[0]):
        up_out[d] = dot_tn(place_matrix(table_one[d : d + 1, :], 0, n1), up_low).astype(BF)
    grad = up_acc[:, feature:]
    grad_low = grad.astype(BF)
    joined, hidden, grad_pre = grad_pre_rows(grad_low, own_one[...], msg_one[...], wi1[...], wo1[...], b1[...])
    grad_pre_low = grad_pre.astype(BF)
    sums_out[0 : 2 * feature, :] = dot_tn(joined, grad_pre_low)
    sums_out[2 * feature : level, :] = dot_tn(hidden, grad_low)
    bias_one = jnp.sum(grad_pre, axis=0, keepdims=True)
    rest = sums_out.shape[0] - 2 * level
    row = iota((rest, feature), 0)
    sums_out[2 * level :, :] = jnp.where(row == 0, bias_one, jnp.where(row == 1, bias_two, 0.0))
    grad_joined = dot_nt(grad_pre_low, wi1[...])
    gmsg[...] = grad_joined[:, feature:].astype(BF)
    gctx_acc[...] = jnp.zeros_like(gctx_acc)
    k = cols_one.shape[1]
    for r in range(adj_one.shape[0]):
        spread_row(adj_one[r], cols_one, r, k, gmsg[r * BLK : (r + 1) * BLK, :], gctx_acc)
    own_at = pl.ds(pl.multiple_of(me[0] * n1, n1), n1)
    gx_out[...] = grad + grad_joined[:, :feature] + gctx_acc[own_at, :]
    for hop in range(1, groups):
        at = pl.ds(pl.multiple_of((me[0] ^ hop) * n1, n1), n1)
        part_outs[hop - 1][...] = gctx_acc[at, :].astype(BF)


def coarse_levels(
    me, cols_two, cols_one, pool_cols, slots_two, adj_two, mine_two, first, adj_one, pool_two,
    table_one, own_one, msg_one, res_one, gup_one, w_in, w_out, bias, sum_rows,
):
    groups = len(slots_two)
    n1, feature = own_one.shape
    n2 = mine_two.shape[1] // 2 * groups
    cap = table_one.shape[1]
    return pl.pallas_call(
        functools.partial(coarse_kernel, groups),
        out_shape=(
            jax.ShapeDtypeStruct((groups, cap, feature), BF),
            jax.ShapeDtypeStruct((n1, feature), F32),
            jax.ShapeDtypeStruct((sum_rows, feature), F32),
        )
        + (jax.ShapeDtypeStruct((n1, feature), BF),) * (groups - 1),
        in_specs=[SM] * 4 + [VM] * (12 + 2 * groups),
        out_specs=(VM,) * (2 + groups),
        scratch_shapes=[
            pltpu.VMEM((groups * mine_two.shape[1], 2 * feature), BF),
            pltpu.VMEM((n2 // BLK, BLK, cols_two.shape[1] * BLK), BF),
            pltpu.VMEM((n2, feature), BF),
            pltpu.VMEM((n2, feature), BF),
            pltpu.VMEM((n2, feature), BF),
            pltpu.VMEM((n2, feature), BF),
            pltpu.VMEM((n2, feature), F32),
            pltpu.VMEM((n2, 2 * feature), BF),
            pltpu.VMEM((n2, feature), F32),
            pltpu.VMEM((n1, 2 * feature), F32),
            pltpu.VMEM((n1, feature), BF),
            pltpu.VMEM((groups * n1, feature), F32),
        ],
        compiler_params=params(),
        cost_estimate=takes(9),
        name="coarse_levels",
    )(
        me, cols_two, cols_one, pool_cols, *slots_two, *adj_two, mine_two, first, adj_one, pool_two,
        table_one, own_one, msg_one, res_one, gup_one, w_in, w_out, bias,
    )


def owner_sum_kernel(table, gx, *refs):
    send_out = refs[-1]
    total = gx[...]
    for part in refs[:-1]:
        total += part[...].astype(F32)
    low = total.astype(BF)
    for d in range(table.shape[0]):
        send_out[d] = dot_tn(place_matrix(table[d : d + 1, :], 0, gx.shape[0]), low).astype(BF)


def owner_sum(table, gx, parts):
    return pl.pallas_call(
        owner_sum_kernel,
        out_shape=jax.ShapeDtypeStruct(table.shape + (gx.shape[1],), BF),
        in_specs=[VM] * (2 + len(parts)),
        out_specs=VM,
        compiler_params=params(),
        cost_estimate=takes(3),
        name="grad_own_one_send",
    )(table, gx, *parts)


def lift(place, got, pool, cols, acc):
    groups, height, _ = got.shape
    cap = place.shape[0] // groups
    packed = jnp.concatenate([got[d, height - cap :, :] for d in range(groups)], axis=0)
    count = packed.shape[0]
    ones = as_ones(place[:, 0:1].astype(jnp.int32) == iota((place.shape[0], count), 1))
    rows = dot(ones, packed).astype(BF)
    k = cols.shape[1]
    for q in range(pool.shape[0]):
        spread_row(pool[q], cols, q, k, rows[q * BLK : (q + 1) * BLK], acc)


def node_out_kernel(cols, place, got, pool, base, out, acc):
    rows = out.shape[0]

    @pl.when(pl.program_id(0) == 0)
    def _():
        acc[...] = jnp.zeros_like(acc)
        lift(place, got, pool, cols, acc)

    at = pl.ds(pl.multiple_of(pl.program_id(0) * rows, rows), rows)
    out[...] = (base[...].astype(F32) + acc[at, :]).astype(BF)


def node_out_rows(cols, place, got, pool, base):
    total, feature = base.shape
    rows = 1024
    spec = pl.BlockSpec((rows, feature), lambda c: (c, 0))
    return pl.pallas_call(
        node_out_kernel,
        grid=(total // rows,),
        out_shape=jax.ShapeDtypeStruct((total, feature), BF),
        in_specs=[SM, VM, VM, VM, spec],
        out_specs=spec,
        scratch_shapes=[pltpu.VMEM((total, feature), F32)],
        compiler_params=params(),
        cost_estimate=takes(9),
        name="node_out",
    )(cols, place, got, pool, base)


def fine_grad_kernel(
    cols, place, got, pool, coarse, cot, feats, message, w_in, w_out, bias, gx_out, gmsg_out, send_out, sums, acc
):
    w_in, w_out, bias = level_of(0, w_in, w_out, bias)
    rows = cot.shape[0]
    feature = cot.shape[1]

    @pl.when(pl.program_id(0) == 0)
    def _():
        acc[...] = jnp.zeros_like(acc)
        sums[...] = jnp.zeros_like(sums)
        lift(place, got, pool, cols, acc)

    at = pl.ds(pl.multiple_of(pl.program_id(0) * rows, rows), rows)
    grad = cot[...].astype(F32) + acc[at, :]
    grad_low = grad.astype(BF)
    joined, hidden, grad_pre = grad_pre_rows(grad_low, feats[...], message[...], w_in[...], w_out[...], bias[...])
    grad_pre_low = grad_pre.astype(BF)
    level = 3 * feature
    sums[0 : 2 * feature, :] += dot_tn(joined, grad_pre_low)
    sums[2 * feature : level, :] += dot_tn(hidden, grad_low)
    sums[level : level + 1, :] += jnp.sum(grad_pre, axis=0, keepdims=True)
    grad_joined = dot_nt(grad_pre_low, w_in[...])
    gx_out[...] = grad + grad_joined[:, :feature]
    gmsg_out[...] = grad_joined[:, feature:].astype(BF)

    @pl.when(pl.program_id(0) == pl.num_programs(0) - 1)
    def _():
        count = send_out.shape[0]
        cut = sums.shape[0] // count
        send_out[:, :cut, :] = sums[...].astype(BF).reshape(count, cut, feature)
        send_out[:, cut:, :] = coarse[...].astype(BF).reshape(count, coarse.shape[0] // count, feature)


def fine_grad(cols, place, got, pool, coarse, cot, feats, message, w_in, w_out, bias, sum_rows, count):
    total, feature = cot.shape
    rows = 1024
    spec = pl.BlockSpec((rows, feature), lambda c: (c, 0))
    return pl.pallas_call(
        fine_grad_kernel,
        grid=(total // rows,),
        out_shape=(
            jax.ShapeDtypeStruct((total, feature), F32),
            jax.ShapeDtypeStruct((total, feature), BF),
            jax.ShapeDtypeStruct((count, (sum_rows + coarse.shape[0]) // count, feature), BF),
        ),
        in_specs=[SM, VM, VM, VM, VM, spec, spec, spec, VM, VM, VM],
        out_specs=(spec, spec, VM),
        scratch_shapes=[pltpu.VMEM((sum_rows, feature), F32), pltpu.VMEM((total, feature), F32)],
        compiler_params=params(),
        cost_estimate=takes(19),
        name="fine_layer_backward",
    )(cols, place, got, pool, coarse, cot, feats, message, w_in, w_out, bias)


def spread_edge_kernel(cols, adj, gmsg, gx, low_out, high_out, carry_out, acc, *, blocks):
    k = cols.shape[1]
    upper = pl.program_id(0) == 1
    width = low_out.shape[0]
    first = jnp.where(upper, blocks - CHUNK, 0)
    acc[0:width, :] = jnp.zeros_like(gx)
    acc[width : 2 * width, :] = gx[...]
    acc[2 * width :, :] = jnp.zeros_like(gx)
    for j in range(CHUNK):
        spread_row(adj[j], cols, first + j, k, gmsg[j * BLK : (j + 1) * BLK, :], acc, first)

    @pl.when(jnp.logical_not(upper))
    def _():
        low_out[...] = acc[0:width, :].astype(BF)
        carry_out[...] = acc[width:, :]

    @pl.when(upper)
    def _():
        high_out[...] = acc[2 * width :, :].astype(BF)
        carry_out[...] = acc[0 : 2 * width, :]


def spread_edge(cols, adj, gmsg, gx):
    blocks, _, span = adj.shape
    feature = gmsg.shape[1]
    chunks = blocks // CHUNK
    return pl.pallas_call(
        functools.partial(spread_edge_kernel, blocks=blocks),
        grid=(2,),
        out_shape=(
            jax.ShapeDtypeStruct((HALO, feature), BF),
            jax.ShapeDtypeStruct((HALO, feature), BF),
            jax.ShapeDtypeStruct((4 * HALO, feature), F32),
        ),
        in_specs=[
            SM,
            pl.BlockSpec((CHUNK, BLK, span), lambda c: (c * (chunks - 1), 0, 0)),
            pl.BlockSpec((CHUNK * BLK, feature), lambda c: (c * (chunks - 1), 0)),
            pl.BlockSpec((CHUNK * BLK, feature), lambda c: (c * (chunks - 1), 0)),
        ],
        out_specs=(
            VM,
            VM,
            pl.BlockSpec((2 * HALO, feature), lambda c: (c, 0)),
        ),
        scratch_shapes=[pltpu.VMEM((3 * HALO, feature), F32)],
        compiler_params=params(),
        cost_estimate=takes(3),
        name="spread_edge",
    )(cols, adj, gmsg, gx)


def spread_inner_kernel(
    me, cols, adj_a, adj_b, gmsg_a, gmsg_b, gx_a, gx_b, carry, prev, after, mid_out, acc, *, rim, groups
):
    k = cols.shape[1]
    step = pl.program_id(0)
    steps = pl.num_programs(0)
    width = rim * BLK
    total = mid_out.shape[0]

    @pl.when(step == 0)
    def _():
        acc[0 : 2 * width, :] = carry[0 : 2 * width, :]
        acc[2 * width : total - 2 * width, :] = jnp.zeros((total - 4 * width, acc.shape[1]), F32)
        acc[total - 2 * width :, :] = carry[2 * width :, :]
        acc[0:width, :] += jnp.where(me[0] > 0, prev[...].astype(F32), 0.0)
        acc[total - width :, :] += jnp.where(me[0] < groups - 1, after[...].astype(F32), 0.0)

    for half, (adj, gmsg, gx) in enumerate(((adj_a, gmsg_a, gx_a), (adj_b, gmsg_b, gx_b))):
        chunk = 2 * step + 1 + half
        for j in range(CHUNK):
            spread_row(adj[j], cols, chunk * CHUNK + j, k, gmsg[j * BLK : (j + 1) * BLK, :], acc, rim)
        rows = gx.shape[0]
        acc[pl.ds(pl.multiple_of(chunk * rows, rows), rows), :] += gx[...]

    @pl.when(step == steps - 1)
    def _():
        mid_out[...] = acc[...].astype(BF)


def spread_inner(me, groups, cols, adj, gmsg, gx, carry, prev, after):
    total, feature = gx.shape
    blocks, _, span = adj.shape
    rows = CHUNK * BLK
    return pl.pallas_call(
        functools.partial(spread_inner_kernel, rim=HALO // BLK, groups=groups),
        grid=(blocks // CHUNK // 2 - 1,),
        out_shape=jax.ShapeDtypeStruct((total, feature), BF),
        in_specs=[
            SM,
            SM,
            pl.BlockSpec((CHUNK, BLK, span), lambda c: (2 * c + 1, 0, 0)),
            pl.BlockSpec((CHUNK, BLK, span), lambda c: (2 * c + 2, 0, 0)),
            pl.BlockSpec((rows, feature), lambda c: (2 * c + 1, 0)),
            pl.BlockSpec((rows, feature), lambda c: (2 * c + 2, 0)),
            pl.BlockSpec((rows, feature), lambda c: (2 * c + 1, 0)),
            pl.BlockSpec((rows, feature), lambda c: (2 * c + 2, 0)),
            VM,
            VM,
            VM,
        ],
        out_specs=VM,
        scratch_shapes=[pltpu.VMEM((total, feature), F32)],
        compiler_params=params(),
        cost_estimate=takes(18),
        name="spread_inner",
    )(me, cols, adj, adj, gmsg, gmsg, gx, gx, carry, prev, after)


def scale_kernel(sums, in_out, out_out, bias_out, *, cut, scale):
    count, height, feature = sums.shape
    level = 3 * feature
    fine = sums[:, :cut, :].reshape(count * cut, feature).astype(F32) * scale
    coarse = sums[:, cut:, :].reshape(count * (height - cut), feature).astype(F32) * scale
    for at, rows in enumerate((fine, coarse, coarse[level:])):
        in_out[at] = rows[: 2 * feature]
        out_out[at] = rows[2 * feature : level]
    bias_out[0:1, :] = fine[level : level + 1]
    bias_out[1:3, :] = coarse[2 * level : 2 * level + 2]


def scaled_sums(sums, cut, scale):
    feature = sums.shape[2]
    return pl.pallas_call(
        functools.partial(scale_kernel, cut=cut, scale=scale),
        out_shape=(
            jax.ShapeDtypeStruct((3, 2 * feature, feature), F32),
            jax.ShapeDtypeStruct((3, feature, feature), F32),
            jax.ShapeDtypeStruct((3, feature), F32),
        ),
        in_specs=[VM],
        out_specs=(VM, VM, VM),
        compiler_params=params(),
        cost_estimate=takes(1),
        name="scaled_sums",
    )(sums)


def after_all(value, *others):
    return lax.optimization_barrier((value,) + others)[0]


def exchange(parts):
    return lax.all_to_all(parts, "grp", split_axis=0, concat_axis=0, tiled=True)


def gather_rows(rows):
    groups = lax.axis_size("grp")
    got = exchange(jnp.broadcast_to(rows[None], (groups,) + rows.shape))
    return got.reshape((groups * rows.shape[0],) + rows.shape[1:])


def halo_pair(low, high):
    count = lax.axis_size("grp")
    prev = lax.ppermute(high, "grp", [(i, (i + 1) % count) for i in range(count)])
    after = lax.ppermute(low, "grp", [((i + 1) % count, i) for i in range(count)])
    return prev, after


def hop_by(rows, axis, hop):
    return lax.ppermute(rows, axis, [(i, i ^ hop) for i in range(lax.axis_size(axis))])


def gather_near(rows):
    groups = lax.axis_size("grp")
    hops = (4, 2, 1) if groups == 8 else range(1, groups)
    return {hop: hop_by(rows, "grp", hop) for hop in hops}


def gather_far(rows, near):
    groups = lax.axis_size("grp")
    got = dict(near)
    if groups == 8:
        got[5] = hop_by(got[4], "grp", 1)
        got[6] = hop_by(got[4], "grp", 2)
        got[3] = hop_by(got[2], "grp", 1)
        got[7] = hop_by(got[5], "grp", 2)
    return [rows] + [got[hop] for hop in range(1, groups)]


def gather_hops(rows):
    return gather_far(rows, gather_near(rows))


def add_low(*parts):
    return sum(part.astype(F32) for part in parts).astype(BF)


def scatter_hops(parts):
    groups = lax.axis_size("grp")
    if groups != 8:
        return [hop_by(parts[hop - 1], "grp", hop) for hop in range(1, groups)]
    far = hop_by(parts[6], "grp", 7)
    six = hop_by(parts[5], "grp", 2)
    five = hop_by(parts[4], "grp", 1)
    three = hop_by(parts[2], "grp", 1)
    return [
        hop_by(add_low(parts[3], five, six), "grp", 4),
        hop_by(add_low(parts[1], three), "grp", 2),
        hop_by(parts[0], "grp", 1),
        far,
    ]


ALL = ("slab", "grp")


def padded_rows(height):
    part = 16 * lax.axis_size(ALL)
    return -(-height // part) * part


def send_shares(shares):
    return lax.all_to_all(shares, ALL, split_axis=0, concat_axis=0, tiled=True)


def share_sums(rows):
    count = lax.axis_size(ALL)
    return lax.all_to_all(
        jnp.broadcast_to(rows[None], (count,) + rows.shape), ALL, split_axis=0, concat_axis=0, tiled=True
    )


def body(
    node_feats,
    cotangent,
    fine_adjacency,
    fine_columns,
    pool_one,
    pool_one_columns,
    count_one,
    owner_one,
    adjacency_one,
    columns_one,
    pool_two,
    pool_two_columns,
    count_two,
    owner_two,
    adjacency_two,
    columns_two,
    weight_in,
    weight_out,
    biases,
):
    groups = lax.axis_size("grp")
    feature = node_feats.shape[1]
    slots_one = owner_one.shape[0]
    balance_one = slots_one // 2
    slots_two = owner_two.shape[0]
    me = lax.axis_index("grp").astype(jnp.int32).reshape(1)
    weights = (weight_in, weight_out, biases)

    cap_one = slots_one // groups
    prev, after = halo_pair(node_feats[:HALO], node_feats[-HALO:])
    near_two = gather_near(adjacency_two)
    message0, result0, sent_one, place_cols, mine_two = fine_forward(
        me, fine_columns, pool_one_columns, count_one, count_two, prev, after, owner_one.reshape(1, slots_one),
        owner_two.reshape(1, slots_two), columns_two, node_feats, fine_adjacency, pool_one, cotangent, *weights,
        groups, balance_one,
    )
    hops = sorted(near_two)
    sent_one, *near_two = lax.optimization_barrier((sent_one, *[near_two[hop] for hop in hops]))
    adj_two = gather_far(adjacency_two, dict(zip(hops, near_two)))
    first = exchange(sent_one)
    own_one = place_rows(first, balance_one)
    grad_up_one, gslots_two, table_one = place_pool(
        pool_two_columns, after_all(first, own_one), pool_two, balance_one, cap_one
    )
    at = 2 * cap_one + 2 + 2 * slots_two // 128
    columns_two_all = first[:, at : at + columns_two.shape[0], : columns_two.shape[1]].astype(jnp.int32)
    columns_two_all = columns_two_all.reshape(-1, columns_two.shape[1])
    message_one, result1, slots_two_mine = one_forward(
        me, columns_one, pool_two_columns, gather_hops(own_one), gslots_two, adjacency_one, pool_two,
        *weights,
    )
    level = 3 * feature
    up_send, gx_one, coarse_sums, *parts_back = coarse_levels(
        me, columns_two_all, columns_one, pool_two_columns, gather_hops(slots_two_mine), adj_two, mine_two, first,
        adjacency_one, pool_two, table_one, own_one, message_one, result1, grad_up_one,
        *weights, padded_rows(2 * level + 2),
    )
    up_got = exchange(up_send)
    grad_send = owner_sum(table_one, gx_one, scatter_hops(parts_back))
    grad_send, up_got = lax.optimization_barrier((grad_send, up_got))
    grad_got = exchange(grad_send)
    node_out = node_out_rows(pool_one_columns, place_cols, up_got, pool_one, result0)
    grad_got, node_out = lax.optimization_barrier((grad_got, node_out))

    sum_rows = padded_rows(level + 1)
    gx_zero, gmsg_zero, sums_send = fine_grad(
        pool_one_columns, place_cols, grad_got, pool_one, coarse_sums, cotangent, node_feats, message0, *weights,
        sum_rows, lax.axis_size(ALL),
    )
    shares = send_shares(sums_send)
    rim_low, rim_high, carry = spread_edge(fine_columns, fine_adjacency, gmsg_zero, gx_zero)
    from_prev, from_after = halo_pair(rim_low, rim_high)
    shares, from_prev, from_after = lax.optimization_barrier((shares, from_prev, from_after))
    mine = jnp.sum(shares.astype(F32), axis=0).astype(BF)
    sums = share_sums(mine)
    from_prev = after_all(from_prev, mine)
    grad_feats = spread_inner(
        me, groups, fine_columns, fine_adjacency, gmsg_zero, gx_zero, carry, from_prev, from_after
    )
    scale = 1.0 / math.sqrt(node_feats.shape[0] * groups * lax.axis_size("slab"))
    return (node_out, grad_feats, *scaled_sums(sums, sum_rows // lax.axis_size(ALL), scale))


def solution(mesh):
    rows = P(("slab", "grp"), None)
    blocks = P(("slab", "grp"), None, None)
    flat = P(("slab", "grp"))
    placed = (
        rows, rows, blocks, rows, blocks, rows, flat, flat, blocks, rows,
        blocks, rows, flat, flat, blocks, rows, P(), P(), P(),
    )
    return jax.shard_map(
        body,
        mesh=mesh,
        in_specs=placed,
        out_specs=(rows, rows, P(), P(), P()),
        check_vma=False,
    )
```

time: 229 us -> 211 us (0.921)
  waiting for transfers between devices: 39 us -> 28.2 us
  Pallas kernels: 92.3 us -> 84.8 us
  starting transfers between devices: 58.3 us -> 63.7 us
  local copies, waits for them, and re-layouts: 12.8 us -> 9.41 us
    ppermute x21 -> x28, starting transfers between devices: 20.4 us -> 36.3 us  [hop_by(): lax.ppermute(rows, axis, [(i, i ^ hop) for i in range(lax.axis_size(axis))])]
    all_to_all x3 -> x2, starting transfers between devices: 16 us -> 7.04 us  [exchange(): return lax.all_to_all(parts, 'grp', split_axis=0, concat_axis=0, tiled=True)]
    pallas_call x8 -> x5, Pallas kernels: 49.5 us -> 41 us  [the longest x1 18.8 us: fine_forward(): pl.pallas_call(functools.partial(fine_kernel, groups=groups, balance=bala...]
    all_to_all x2 -> x1, waiting for transfers between devices: 7.91 us -> 1.46 us  [send_shares(): return lax.all_to_all(shares, ALL, split_axis=0, concat_axis=0, tiled=True)]
    all_to_all x2 -> x1, starting transfers between devices: 9.99 us -> 6.05 us  [send_shares(): return lax.all_to_all(shares, ALL, split_axis=0, concat_axis=0, tiled=True)]
    ppermute x21 -> x28, waiting for transfers between devices: 25.2 us -> 21.3 us  [hop_by(): lax.ppermute(rows, axis, [(i, i ^ hop) for i in range(lax.axis_size(axis))])]
    unnamed x60 -> x66, local copies, waits for them, and re-layouts: 5.35 us -> 6.88 us
  transfers between devices with their start and end apart: 31 -> 36, of which waited for: 14 -> 11; matrix products, arithmetic and copies ran while one was open for 4% -> 3% of each run, Pallas kernels for 32% -> 25%
where the time goes in v3:
time: 211 us; the launch traced here: 210 us
  Pallas kernels  84.8 us (40%)
  starting transfers between devices  63.7 us (30%)
  waiting for transfers between devices  28.2 us (13%)
  blocking collectives  19 us (9%)
  local copies, waits for them, and re-layouts  9.41 us (4%)
  other arithmetic  2.58 us (1%)
  between operations  2.31 us (1%)
    ppermute x28, starting transfers between devices, hop_by(): lax.ppermute(rows, axis, [(i, i ^ hop) for i in range(lax.axis_size(axis))])  36.3 us
    ppermute x28, waiting for transfers between devices, hop_by(): lax.ppermute(rows, axis, [(i, i ^ hop) for i in range(lax.axis_size(axis))])  21.3 us
    all_to_all x1, blocking collectives, exchange(): return lax.all_to_all(parts, 'grp', split_axis=0, concat_axis=0, tiled=True)  19 us
    pallas_call x1, Pallas kernels, fine_forward(): pl.pallas_call(functools.partial(fine_kernel, groups=groups, balance=bala...  18.8 us
    pallas_call x1, Pallas kernels, spread_inner(): pl.pallas_call(functools.partial(spread_inner_kernel, rim=HALO // BLK, gr...  15.7 us
    pallas_call x1, Pallas kernels, fine_grad(): pl.pallas_call(fine_grad_kernel, grid=(total // rows,), out_shape=(jax.Sh...  14.8 us
    pallas_call x1, Pallas kernels, coarse_levels(): pl.pallas_call(functools.partial(coarse_kernel, groups), out_shape=(jax.S...  9.71 us
    ppermute x2, starting transfers between devices, halo_pair(): lax.ppermute(low, 'grp', [((i + 1) % count, i) for i in range(count)])  8.99 us
  transfers between devices with their start and end apart: 36, of which 11 were waited for; matrix products, arithmetic and copies ran while one was open for 3% of the time, Pallas kernels for 25%

profile of v3, /device:TPU:0, one launch (start us, length us, event | category | flops | bytes accessed | tf_op | source)
XLA Modules:
  0.0 210.0 jit_solution(13116933813295130964)
XLA Ops:
  1.6 6.0 %collective-permute-start.1 = (bf16[512,128]{1,0:T(8,128)(2,1)S(1)}, bf16[512,128]{1,0:T(8,128)(2,1)S(1)}, u32[]{:S(2)}, u32[]{:S(2)}) collective-permute-start(bf16[512,128]{1,0:T(8,128)(2,1)S(1)} %get-tuple-element.91), channel_id=1, source_target_pairs={{1,0},{2,1},{3,2},{4,3},{5,4},{6,5},{7,6},{0,7},{9,8},{10,9},{11,1... | collective-permute-start | bytes 393224 | tf_op jit(solution)/shard_map/ppermute | solution.py:769
  9.1 4.4 %collective-permute-start.4 = (bf16[2,64,512]{2,1,0:T(8,128)(2,1)}, bf16[2,64,512]{2,1,0:T(8,128)(2,1)S(1)}, u32[]{:S(2)}, u32[]{:S(2)}) collective-permute-start(bf16[2,64,512]{2,1,0:T(8,128)(2,1)} %refs_8_.1), channel_id=1, source_target_pairs={{0,4},{1,5},{2,6},{3,7},{4,0},{5,1},{6,2},{7,3},{8,12},{9,13},{10,... | collective-permute-start | bytes 393224 | tf_op jit(solution)/shard_map/ppermute | solution.py:774
  18.3 18.8 %fine_forward.1 = (bf16[8192,128]{1,0:T(8,128)(2,1)}, bf16[8192,128]{1,0:T(8,128)(2,1)}, bf16[8,272,128]{2,1,0:T(8,128)(2,1)}, f32[1024,128]{1,0:T(8,128)}, s32[1,256]{1,0:T(1,128)}) custom-call(s32[1]{0:T(128)} %bitcast.me, s32[128,12]{1,0:T(8,128)} %copy.24.cols, s32[16,8]{1,0:T(8,128)} %copy.25.pool_cols.cols, s32[1]{0:T(128)S(6)} %copy.30.count, ...), custom_call_target="tpu_custom_call" | custom-call | bytes 221400000 | tf_op jit(solution)/shard_map/fine_forward/pallas_call | solution.py:226
  37.1 19.0 %all_to_all.25.got.refs_17_ = bf16[8,272,128]{2,1,0:T(8,128)(2,1)} all-to-all(bf16[8,272,128]{2,1,0:T(8,128)(2,1)} %get-tuple-element.49), channel_id=1, replica_groups=mesh['slab'=4,'grp'=8] {'grp'}, dimensions={0} | all-to-all | bytes 1114112 | tf_op jit(solution)/shard_map/all_to_all | solution.py:757
  56.1 2.1 %place_own_one.1.refs_0_.refs_21_ = bf16[512,128]{1,0:T(8,128)(2,1)} custom-call(bf16[8,272,128]{2,1,0:T(8,128)(2,1)} %all_to_all.25.got.refs_17_), custom_call_target="tpu_custom_call" | custom-call | bytes 33210000 | tf_op jit(solution)/shard_map/place_own_one/pallas_call | solution.py:278
  60.3 5.6 %collective-permute-done.8.refs_4_ = bf16[512,128]{1,0:T(8,128)(2,1)S(1)} collective-permute-done((bf16[512,128]{1,0:T(8,128)(2,1)}, bf16[512,128]{1,0:T(8,128)(2,1)S(1)}, u32[]{:S(2)}, u32[]{:S(2)}) %collective-permute-start.8) | collective-permute-done | bytes 131104 | tf_op jit(solution)/shard_map/ppermute | solution.py:774
  68.7 2.3 %collective-permute-done.9.refs_5_ = bf16[512,128]{1,0:T(8,128)(2,1)S(1)} collective-permute-done((bf16[512,128]{1,0:T(8,128)(2,1)S(1)}, bf16[512,128]{1,0:T(8,128)(2,1)S(1)}, u32[]{:S(2)}, u32[]{:S(2)}) %collective-permute-start.9) | collective-permute-done | bytes 131104 | tf_op jit(solution)/shard_map/ppermute | solution.py:774
  71.5 2.5 %place_grad_up_one.1 = (bf16[512,128]{1,0:T(8,128)(2,1)}, bf16[256,128]{1,0:T(8,128)(2,1)}, s32[8,128]{1,0:T(8,128)}) custom-call(s32[4,8]{1,0:T(4,128)} %pool_cols.4, bf16[8,272,128]{2,1,0:T(8,128)(2,1)} %all_to_all.25.got.refs_17_, bf16[4,64,512]{2,1,0:T(8,128)(2,1)} %refs_19_.1), custom_call_target="tpu_custom_call" | custom-call | bytes 33210000 | tf_op jit(solution)/shard_map/place_grad_up_one/pallas_call | solution.py:302
  74.1 1.9 collective-permute-done.11.refs_7_
  76.6 3.2 %level_one_forward.1 = (bf16[512,128]{1,0:T(8,128)(2,1)}, bf16[512,128]{1,0:T(8,128)(2,1)}, bf16[256,256]{1,0:T(8,128)(2,1)}) custom-call(s32[1]{0:T(128)} %bitcast.me, s32[8,8]{1,0:T(8,128)} %cols_one.1, s32[4,8]{1,0:T(4,128)} %pool_cols.4, bf16[512,128]{1,0:T(8,128)(2,1)} %place_own_one.1.refs_0_.refs_21_, bf16[512,128]{1,0:T(8,128)(2,1)} %copy-done.24, ...), custom_call_target="tpu_custom_call" | custom-call | bytes 33210000 | tf_op jit(solution)/shard_map/level_one_forward/pallas_call | solution.py:339
  79.9 2.1 collective-permute-start.15
  84.0 2.0 collective-permute-start.21
  87.0 1.9 collective-permute-start.16
  94.4 1.8 collective-permute-start.18
  100.0 9.7 %coarse_levels.1 = (bf16[8,128,128]{2,1,0:T(8,128)(2,1)}, f32[512,128]{1,0:T(8,128)}, f32[1024,128]{1,0:T(8,128)}, bf16[512,128]{1,0:T(8,128)(2,1)}, bf16[512,12...) custom-call(s32[1]{0:T(128)} %bitcast.me, ...), custom_call_target="tpu_custom_call" | custom-call | bytes 99630000 | tf_op jit(solution)/shard_map/coarse_levels/pallas_call | solution.py:462
  112.7 3.4 %all-to-all-start.1 = ((bf16[8,128,128]{2,1,0:T(8,128)(2,1)}), bf16[8,128,128]{2,1,0:T(8,128)(2,1)S(1)}, u32[]{:S(2)}, u32[]{:S(2)}) async-start(bf16[8,128,128]{2,1,0:T(8,128)(2,1)} %get-tuple-element.69), calls=%async_computation.1 | async-start | bytes 524288 | tf_op jit(solution)/shard_map/all_to_all | solution.py:757
  116.1 1.9 collective-permute-start.26
  118.2 4.6 %collective-permute-start.29 = (bf16[512,128]{1,0:T(8,128)(2,1)}, bf16[512,128]{1,0:T(8,128)(2,1)S(1)}, u32[]{:S(2)}, u32[]{:S(2)}) collective-permute-start(bf16[512,128]{1,0:T(8,128)(2,1)} %get-tuple-element.68), channel_id=1, source_target_pairs={{0,7},{1,6},{2,5},{3,4},{4,3},{5,2},{6,1},{7,0},{8,15},{9,14},{10,... | collective-permute-start | bytes 393224 | tf_op jit(solution)/shard_map/ppermute | solution.py:774
  125.9 2.4 %collective-permute-done.29.refs_3_ = bf16[512,128]{1,0:T(8,128)(2,1)S(1)} collective-permute-done((bf16[512,128]{1,0:T(8,128)(2,1)}, bf16[512,128]{1,0:T(8,128)(2,1)S(1)}, u32[]{:S(2)}, u32[]{:S(2)}) %collective-permute-start.29) | collective-permute-done | bytes 131104 | tf_op jit(solution)/shard_map/ppermute | solution.py:774
  128.4 5.2 %collective-permute-done.25.refs_0_ = bf16[512,128]{1,0:T(8,128)(2,1)S(1)} collective-permute-done((bf16[512,128]{1,0:T(8,128)(2,1)S(1)}, bf16[512,128]{1,0:T(8,128)(2,1)S(1)}, u32[]{:S(2)}, u32[]{:S(2)}) %collective-permute-start.25) | collective-permute-done | bytes 131104 | tf_op jit(solution)/shard_map/ppermute | solution.py:774
  134.2 2.4 %grad_own_one_send.1 = bf16[8,128,128]{2,1,0:T(8,128)(2,1)} custom-call(s32[8,128]{1,0:T(8,128)} %get-tuple-element.51.refs_20_.table, f32[512,128]{1,0:T(8,128)} %get-tuple-element.61.gx, bf16[512,128]{1,0:T(8,128)(2,1)} %copy-done.30, bf16[512,128]{1,0:T(8,128)(2,1)} %copy-done.31, bf16[512,128]{1,0:T(8,128)(2,1)} %copy-done.28, bf16[512,128]{1,0:T(8,128)(2,1)} %copy-done.29), custom_call_target="tpu_custom_call" | custom-call | bytes 33210000 | tf_op jit(solution)/shard_map/grad_own_one_send/pallas_call | solution.py:506
  136.6 3.6 %all-to-all-start.2 = ((bf16[8,128,128]{2,1,0:T(8,128)(2,1)}), bf16[8,128,128]{2,1,0:T(8,128)(2,1)S(1)}, u32[]{:S(2)}, u32[]{:S(2)}) async-start(bf16[8,128,128]{2,1,0:T(8,128)(2,1)} %grad_own_one_send.1), calls=%async_computation.2 | async-start | bytes 524288 | tf_op jit(solution)/shard_map/all_to_all | solution.py:757
  140.3 8.9 %node_out.1 = bf16[8192,128]{1,0:T(8,128)(2,1)} custom-call(s32[16,8]{1,0:T(8,128)} %copy.25.pool_cols.cols, f32[1024,128]{1,0:T(8,128)} %get-tuple-element.71.place, bf16[8,128,128]{2,1,0:T(8,128)(2,1)} %copy-done.1, bf16[16,64,512]{2,1,0:T(8,128)(2,1)} %pool.5, bf16[8192,128]{1,0:T(8,128)(2,1)} %get-tuple-element.73.base), custom_call_target="tpu_custom_call" | custom-call | bytes 99630000 | tf_op jit(solution)/shard_map/node_out/pallas_call | solution.py:545
  149.9 14.8 %fine_layer_backward.1 = (f32[8192,128]{1,0:T(8,128)}, bf16[8192,128]{1,0:T(8,128)(2,1)}, bf16[32,48,128]{2,1,0:T(8,128)(2,1)}) custom-call(s32[16,8]{1,0:T(8,128)} %copy.25.pool_cols.cols, f32[1024,128]{1,0:T(8,128)} %get-tuple-element.71.place, bf16[8,128,128]{2,1,0:T(8,128)(2,1)} %copy-done.2, bf16[16,64,512]{2,1,0:T(8,128)(2,1)} %pool.5, ...), custom_call_target="tpu_custom_call" | custom-call | bytes 210330000 | tf_op jit(solution)/shard_map/fine_layer_backward/pallas_call | solution.py:596
  164.8 6.1 %all-to-all-start.3 = ((bf16[32,48,128]{2,1,0:T(8,128)(2,1)}), bf16[32,48,128]{2,1,0:T(8,128)(2,1)S(1)}, u32[]{:S(2)}, u32[]{:S(2)}) async-start(bf16[32,48,128]{2,1,0:T(8,128)(2,1)} %get-tuple-element.81), calls=%async_computation.3 | async-start | bytes 786432 | tf_op jit(solution)/shard_map/all_to_all | solution.py:827
  170.8 4.7 %spread_edge.1 = (bf16[512,128]{1,0:T(8,128)(2,1)}, bf16[512,128]{1,0:T(8,128)(2,1)}, f32[2048,128]{1,0:T(8,128)}) custom-call(s32[128,12]{1,0:T(8,128)} %copy.24.cols, bf16[128,64,768]{2,1,0:T(8,128)(2,1)} %adj_b.1, bf16[8192,128]{1,0:T(8,128)(2,1)} %get-tuple-element.78.gmsg.gmsg_a.gmsg_b, f32[8192,128]{1,0:T(8,128)} %get-tuple-element.79.gx.gx_a.gx_b), custom_call_target="tpu_custom_call" | custom-call | bytes 33210000 | tf_op jit(solution)/shard_map/spread_edge/pallas_call | solution.py:639
  175.5 1.8 collective-permute-start.30
  177.3 3.0 %collective-permute-start.31 = (bf16[512,128]{1,0:T(8,128)(2,1)}, bf16[512,128]{1,0:T(8,128)(2,1)S(1)}, u32[]{:S(2)}, u32[]{:S(2)}) collective-permute-start(bf16[512,128]{1,0:T(8,128)(2,1)} %get-tuple-element.83), channel_id=1, source_target_pairs={{1,0},{2,1},{3,2},{4,3},{5,4},{6,5},{7,6},{0,7},{9,8},{10,9},{11,1... | collective-permute-start | bytes 393224 | tf_op jit(solution)/shard_map/ppermute | solution.py:769
  180.2 5.5 %collective-permute-done.30.prev = bf16[512,128]{1,0:T(8,128)(2,1)S(1)} collective-permute-done((bf16[512,128]{1,0:T(8,128)(2,1)}, bf16[512,128]{1,0:T(8,128)(2,1)S(1)}, u32[]{:S(2)}, u32[]{:S(2)}) %collective-permute-start.30) | collective-permute-done | bytes 131104 | tf_op jit(solution)/shard_map/ppermute | solution.py:768
  188.1 3.5 %all-to-all-start.4 = ((bf16[32,48,128]{2,1,0:T(8,128)(2,1)}), bf16[32,48,128]{2,1,0:T(8,128)(2,1)S(1)}, u32[]{:S(2)}, u32[]{:S(2)}) async-start(bf16[32,48,128]{2,1,0:T(8,128)(2,1)} %broadcast_in_dim.2), calls=%async_computation.4 | async-start | bytes 786432 | tf_op jit(solution)/shard_map/all_to_all | solution.py:832
  191.6 15.7 %spread_inner.1 = bf16[8192,128]{1,0:T(8,128)(2,1)} custom-call(s32[1]{0:T(128)} %bitcast.me, s32[128,12]{1,0:T(8,128)} %copy.24.cols, bf16[128,64,768]{2,1,0:T(8,128)(2,1)} %adj_b.1, bf16[128,64,768]{2,1,0:T(8,128)(2,1)} %adj_b.1, bf16[8192,128]{1,0:T(8,128)(2,1)} %get-tuple-element.78.gmsg.gmsg_a.gmsg_b, ...), custom_call_target="tpu_custom_call" | custom-call | bytes 199260000 | tf_op jit(solution)/shard_map/spread_inner/pallas_call | solution.py:698
  208.1 1.8 scaled_sums.1
  (125 shorter events, 35.0 us)
Async XLA Ops:
  1.6 16.0 %collective-permute-start.1 = (bf16[512,128]{1,0:T(8,128)(2,1)S(1)}, bf16[512,128]{1,0:T(8,128)(2,1)S(1)}, u32[]{:S(2)}, u32[]{:S(2)}) collective-permute-start(bf16[512,128]{1,0:T(8,128)(2,1)S(1)} %get-tuple-element.91), channel_id=1, source_target_pairs={{1,0},{2,1},{3,2},{4,3},{5,4},{6,5},{7,6},{0,7},{9,8},{10,9},{11,1... | collective-permute-start | bytes 393224 | tf_op jit(solution)/shard_map/ppermute | solution.py:769
  7.7 9.9 %collective-permute-start = (bf16[512,128]{1,0:T(8,128)(2,1)S(1)}, bf16[512,128]{1,0:T(8,128)(2,1)S(1)}, u32[]{:S(2)}, u32[]{:S(2)}) collective-permute-start(bf16[512,128]{1,0:T(8,128)(2,1)S(1)} %get-tuple-element.92), channel_id=1, source_target_pairs={{0,1},{1,2},{2,3},{3,4},{4,5},{5,6},{6,7},{7,0},{8,9},{9,10},{10,1... | collective-permute-start | bytes 393224 | tf_op jit(solution)/shard_map/ppermute | solution.py:768
  7.7 29.4 %collective-permute-start.3 = (bf16[2,64,512]{2,1,0:T(8,128)(2,1)}, bf16[2,64,512]{2,1,0:T(8,128)(2,1)S(1)}, u32[]{:S(2)}, u32[]{:S(2)}) collective-permute-start(bf16[2,64,512]{2,1,0:T(8,128)(2,1)} %refs_8_.1), channel_id=1, source_target_pairs={{0,2},{1,3},{2,0},{3,1},{4,6},{5,7},{6,4},{7,5},{8,10},{9,11},{10,... | collective-permute-start | bytes 393224 | tf_op jit(solution)/shard_map/ppermute | solution.py:774
  7.7 29.4 %collective-permute-start.2 = (bf16[2,64,512]{2,1,0:T(8,128)(2,1)}, bf16[2,64,512]{2,1,0:T(8,128)(2,1)S(1)}, u32[]{:S(2)}, u32[]{:S(2)}) collective-permute-start(bf16[2,64,512]{2,1,0:T(8,128)(2,1)} %refs_8_.1), channel_id=1, source_target_pairs={{0,1},{1,0},{2,3},{3,2},{4,5},{5,4},{6,7},{7,6},{8,9},{9,8},{10,11... | collective-permute-start | bytes 393224 | tf_op jit(solution)/shard_map/ppermute | solution.py:774
  9.1 28.0 %collective-permute-start.4 = (bf16[2,64,512]{2,1,0:T(8,128)(2,1)}, bf16[2,64,512]{2,1,0:T(8,128)(2,1)S(1)}, u32[]{:S(2)}, u32[]{:S(2)}) collective-permute-start(bf16[2,64,512]{2,1,0:T(8,128)(2,1)} %refs_8_.1), channel_id=1, source_target_pairs={{0,4},{1,5},{2,6},{3,7},{4,0},{5,1},{6,2},{7,3},{8,12},{9,13},{10,... | collective-permute-start | bytes 393224 | tf_op jit(solution)/shard_map/ppermute | solution.py:774
  58.3 7.6 %collective-permute-start.8 = (bf16[512,128]{1,0:T(8,128)(2,1)}, bf16[512,128]{1,0:T(8,128)(2,1)S(1)}, u32[]{:S(2)}, u32[]{:S(2)}) collective-permute-start(bf16[512,128]{1,0:T(8,128)(2,1)} %place_own_one.1.refs_0_.refs_21_), channel_id=1, source_target_pairs={{0,4},{1,5},{2,6},{3,7},{4,0},{5,1},{6,2},{7,3},{8,12},{9,13},{10,... | collective-permute-start | bytes 393224 | tf_op jit(solution)/shard_map/ppermute | solution.py:774
  58.9 9.0 %collective-permute-start.6 = (bf16[512,128]{1,0:T(8,128)(2,1)}, bf16[512,128]{1,0:T(8,128)(2,1)S(1)}, u32[]{:S(2)}, u32[]{:S(2)}) collective-permute-start(bf16[512,128]{1,0:T(8,128)(2,1)} %place_own_one.1.refs_0_.refs_21_), channel_id=1, source_target_pairs={{0,2},{1,3},{2,0},{3,1},{4,6},{5,7},{6,4},{7,5},{8,10},{9,11},{10,... | collective-permute-start | bytes 393224 | tf_op jit(solution)/shard_map/ppermute | solution.py:774
  66.6 7.5 %collective-permute-start.5 = (bf16[512,128]{1,0:T(8,128)(2,1)}, bf16[512,128]{1,0:T(8,128)(2,1)S(1)}, u32[]{:S(2)}, u32[]{:S(2)}) collective-permute-start(bf16[512,128]{1,0:T(8,128)(2,1)} %place_own_one.1.refs_0_.refs_21_), channel_id=1, source_target_pairs={{0,1},{1,0},{2,3},{3,2},{4,5},{5,4},{6,7},{7,6},{8,9},{9,8},{10,11... | collective-permute-start | bytes 393224 | tf_op jit(solution)/shard_map/ppermute | solution.py:774
  67.9 6.2 %collective-permute-start.10 = (bf16[512,128]{1,0:T(8,128)(2,1)S(1)}, bf16[512,128]{1,0:T(8,128)(2,1)S(1)}, u32[]{:S(2)}, u32[]{:S(2)}) collective-permute-start(bf16[512,128]{1,0:T(8,128)(2,1)S(1)} %collective-permute-done.8.refs_4_), channel_id=1, source_target_pairs={{0,2},{1,3},{2,0},{3,1},{4,6},{5,7},{6,4},{7,5},{8,10},{9,11},{10,... | collective-permute-start | bytes 393224 | tf_op jit(solution)/shard_map/ppermute | solution.py:774
  67.9 6.2 %collective-permute-start.7 = (bf16[512,128]{1,0:T(8,128)(2,1)S(1)}, bf16[512,128]{1,0:T(8,128)(2,1)S(1)}, u32[]{:S(2)}, u32[]{:S(2)}) collective-permute-start(bf16[512,128]{1,0:T(8,128)(2,1)S(1)} %collective-permute-done.6.refs_2_), channel_id=1, source_target_pairs={{0,1},{1,0},{2,3},{3,2},{4,5},{5,4},{6,7},{7,6},{8,9},{9,8},{10,11... | collective-permute-start | bytes 393224 | tf_op jit(solution)/shard_map/ppermute | solution.py:774
  79.9 7.1 %collective-permute-start.15 = (bf16[256,256]{1,0:T(8,128)(2,1)}, bf16[256,256]{1,0:T(8,128)(2,1)S(1)}, u32[]{:S(2)}, u32[]{:S(2)}) collective-permute-start(bf16[256,256]{1,0:T(8,128)(2,1)} %get-tuple-element.53.refs_0_), channel_id=1, source_target_pairs={{0,4},{1,5},{2,6},{3,7},{4,0},{5,1},{6,2},{7,3},{8,12},{9,13},{10,... | collective-permute-start | bytes 393224 | tf_op jit(solution)/shard_map/ppermute | solution.py:774
  81.9 6.9 %collective-permute-start.20 = (bf16[2,64,512]{2,1,0:T(8,128)(2,1)S(1)}, bf16[2,64,512]{2,1,0:T(8,128)(2,1)S(1)}, u32[]{:S(2)}, u32[]{:S(2)}) collective-permute-start(bf16[2,64,512]{2,1,0:T(8,128)(2,1)S(1)} %collective-permute-done.4.refs_12_), channel_id=1, source_target_pairs={{0,1},{1,0},{2,3},{3,2},{4,5},{5,4},{6,7},{7,6},{8,9},{9,8},{10,11... | collective-permute-start | bytes 393224 | tf_op jit(solution)/shard_map/ppermute | solution.py:774
  82.8 7.6 %collective-permute-start.19 = (bf16[2,64,512]{2,1,0:T(8,128)(2,1)S(1)}, bf16[2,64,512]{2,1,0:T(8,128)(2,1)S(1)}, u32[]{:S(2)}, u32[]{:S(2)}) collective-permute-start(bf16[2,64,512]{2,1,0:T(8,128)(2,1)S(1)} %collective-permute-done.3.refs_10_), channel_id=1, source_target_pairs={{0,1},{1,0},{2,3},{3,2},{4,5},{5,4},{6,7},{7,6},{8,9},{9,8},{10,11... | collective-permute-start | bytes 393224 | tf_op jit(solution)/shard_map/ppermute | solution.py:774
  84.0 8.0 %collective-permute-start.21 = (bf16[2,64,512]{2,1,0:T(8,128)(2,1)S(1)}, bf16[2,64,512]{2,1,0:T(8,128)(2,1)S(1)}, u32[]{:S(2)}, u32[]{:S(2)}) collective-permute-start(bf16[2,64,512]{2,1,0:T(8,128)(2,1)S(1)} %collective-permute-done.4.refs_12_), channel_id=1, source_target_pairs={{0,2},{1,3},{2,0},{3,1},{4,6},{5,7},{6,4},{7,5},{8,10},{9,11},{10,... | collective-permute-start | bytes 393224 | tf_op jit(solution)/shard_map/ppermute | solution.py:774
  86.0 7.6 %collective-permute-start.13 = (bf16[256,256]{1,0:T(8,128)(2,1)}, bf16[256,256]{1,0:T(8,128)(2,1)S(1)}, u32[]{:S(2)}, u32[]{:S(2)}) collective-permute-start(bf16[256,256]{1,0:T(8,128)(2,1)} %get-tuple-element.53.refs_0_), channel_id=1, source_target_pairs={{0,2},{1,3},{2,0},{3,1},{4,6},{5,7},{6,4},{7,5},{8,10},{9,11},{10,... | collective-permute-start | bytes 393224 | tf_op jit(solution)/shard_map/ppermute | solution.py:774
  87.0 7.4 %collective-permute-start.16 = (bf16[256,256]{1,0:T(8,128)(2,1)S(1)}, bf16[256,256]{1,0:T(8,128)(2,1)S(1)}, u32[]{:S(2)}, u32[]{:S(2)}) collective-permute-start(bf16[256,256]{1,0:T(8,128)(2,1)S(1)} %collective-permute-done.15.refs_4_), channel_id=1, source_target_pairs={{0,1},{1,0},{2,3},{3,2},{4,5},{5,4},{6,7},{7,6},{8,9},{9,8},{10,11... | collective-permute-start | bytes 393224 | tf_op jit(solution)/shard_map/ppermute | solution.py:774
  88.8 8.7 %collective-permute-start.22 = (bf16[2,64,512]{2,1,0:T(8,128)(2,1)S(1)}, bf16[2,64,512]{2,1,0:T(8,128)(2,1)S(1)}, u32[]{:S(2)}, u32[]{:S(2)}) collective-permute-start(bf16[2,64,512]{2,1,0:T(8,128)(2,1)S(1)} %collective-permute-done.20.refs_13_), channel_id=1, source_target_pairs={{0,2},{1,3},{2,0},{3,1},{4,6},{5,7},{6,4},{7,5},{8,10},{9,11},{10,... | collective-permute-start | bytes 393224 | tf_op jit(solution)/shard_map/ppermute | solution.py:774
  90.4 7.1 %collective-permute-start.12 = (bf16[256,256]{1,0:T(8,128)(2,1)}, bf16[256,256]{1,0:T(8,128)(2,1)S(1)}, u32[]{:S(2)}, u32[]{:S(2)}) collective-permute-start(bf16[256,256]{1,0:T(8,128)(2,1)} %get-tuple-element.53.refs_0_), channel_id=1, source_target_pairs={{0,1},{1,0},{2,3},{3,2},{4,5},{5,4},{6,7},{7,6},{8,9},{9,8},{10,11... | collective-permute-start | bytes 393224 | tf_op jit(solution)/shard_map/ppermute | solution.py:774
  92.0 5.5 %collective-permute-start.17 = (bf16[256,256]{1,0:T(8,128)(2,1)S(1)}, bf16[256,256]{1,0:T(8,128)(2,1)S(1)}, u32[]{:S(2)}, u32[]{:S(2)}) collective-permute-start(bf16[256,256]{1,0:T(8,128)(2,1)S(1)} %collective-permute-done.15.refs_4_), channel_id=1, source_target_pairs={{0,2},{1,3},{2,0},{3,1},{4,6},{5,7},{6,4},{7,5},{8,10},{9,11},{10,... | collective-permute-start | bytes 393224 | tf_op jit(solution)/shard_map/ppermute | solution.py:774
  109.7 13.1 %collective-permute-start.23 = (bf16[512,128]{1,0:T(8,128)(2,1)}, bf16[512,128]{1,0:T(8,128)(2,1)S(1)}, u32[]{:S(2)}, u32[]{:S(2)}) collective-permute-start(bf16[512,128]{1,0:T(8,128)(2,1)} %get-tuple-element.63), channel_id=1, source_target_pairs={{0,1},{1,0},{2,3},{3,2},{4,5},{5,4},{6,7},{7,6},{8,9},{9,8},{10,11... | collective-permute-start | bytes 393224 | tf_op jit(solution)/shard_map/ppermute | solution.py:774
  111.0 11.7 %collective-permute-start.24 = (bf16[512,128]{1,0:T(8,128)(2,1)}, bf16[512,128]{1,0:T(8,128)(2,1)S(1)}, u32[]{:S(2)}, u32[]{:S(2)}) collective-permute-start(bf16[512,128]{1,0:T(8,128)(2,1)} %get-tuple-element.64), channel_id=1, source_target_pairs={{0,2},{1,3},{2,0},{3,1},{4,6},{5,7},{6,4},{7,5},{8,10},{9,11},{10,... | collective-permute-start | bytes 393224 | tf_op jit(solution)/shard_map/ppermute | solution.py:774
  112.7 24.0 %all-to-all-start.1 = ((bf16[8,128,128]{2,1,0:T(8,128)(2,1)}), bf16[8,128,128]{2,1,0:T(8,128)(2,1)S(1)}, u32[]{:S(2)}, u32[]{:S(2)}) async-start(bf16[8,128,128]{2,1,0:T(8,128)(2,1)} %get-tuple-element.69), calls=%async_computation.1 | async-start | bytes 524288 | tf_op jit(solution)/shard_map/all_to_all | solution.py:757
  116.1 7.7 %collective-permute-start.26 = (bf16[512,128]{1,0:T(8,128)(2,1)}, bf16[512,128]{1,0:T(8,128)(2,1)S(1)}, u32[]{:S(2)}, u32[]{:S(2)}) collective-permute-start(bf16[512,128]{1,0:T(8,128)(2,1)} %get-tuple-element.66), channel_id=1, source_target_pairs={{0,1},{1,0},{2,3},{3,2},{4,5},{5,4},{6,7},{7,6},{8,9},{9,8},{10,11... | collective-permute-start | bytes 393224 | tf_op jit(solution)/shard_map/ppermute | solution.py:774
  118.0 7.9 %collective-permute-start.28 = (bf16[512,128]{1,0:T(8,128)(2,1)}, bf16[512,128]{1,0:T(8,128)(2,1)S(1)}, u32[]{:S(2)}, u32[]{:S(2)}) collective-permute-start(bf16[512,128]{1,0:T(8,128)(2,1)} %get-tuple-element.67), channel_id=1, source_target_pairs={{0,1},{1,0},{2,3},{3,2},{4,5},{5,4},{6,7},{7,6},{8,9},{9,8},{10,11... | collective-permute-start | bytes 393224 | tf_op jit(solution)/shard_map/ppermute | solution.py:774
  118.2 10.2 %collective-permute-start.29 = (bf16[512,128]{1,0:T(8,128)(2,1)}, bf16[512,128]{1,0:T(8,128)(2,1)S(1)}, u32[]{:S(2)}, u32[]{:S(2)}) collective-permute-start(bf16[512,128]{1,0:T(8,128)(2,1)} %get-tuple-element.68), channel_id=1, source_target_pairs={{0,7},{1,6},{2,5},{3,4},{4,3},{5,2},{6,1},{7,0},{8,15},{9,14},{10,... | collective-permute-start | bytes 393224 | tf_op jit(solution)/shard_map/ppermute | solution.py:774
  123.8 9.8 %collective-permute-start.25 = (bf16[512,128]{1,0:T(8,128)(2,1)S(1)}, bf16[512,128]{1,0:T(8,128)(2,1)S(1)}, u32[]{:S(2)}, u32[]{:S(2)}) collective-permute-start(bf16[512,128]{1,0:T(8,128)(2,1)S(1)} %add_convert_fusion.1), channel_id=1, source_target_pairs={{0,4},{1,5},{2,6},{3,7},{4,0},{5,1},{6,2},{7,3},{8,12},{9,13},{10,... | collective-permute-start | bytes 393224 | tf_op jit(solution)/shard_map/ppermute | solution.py:774
  124.8 8.7 %collective-permute-start.27 = (bf16[512,128]{1,0:T(8,128)(2,1)S(1)}, bf16[512,128]{1,0:T(8,128)(2,1)S(1)}, u32[]{:S(2)}, u32[]{:S(2)}) collective-permute-start(bf16[512,128]{1,0:T(8,128)(2,1)S(1)} %add_convert_fusion), channel_id=1, source_target_pairs={{0,2},{1,3},{2,0},{3,1},{4,6},{5,7},{6,4},{7,5},{8,10},{9,11},{10,... | collective-permute-start | bytes 393224 | tf_op jit(solution)/shard_map/ppermute | solution.py:774
  136.6 12.5 %all-to-all-start.2 = ((bf16[8,128,128]{2,1,0:T(8,128)(2,1)}), bf16[8,128,128]{2,1,0:T(8,128)(2,1)S(1)}, u32[]{:S(2)}, u32[]{:S(2)}) async-start(bf16[8,128,128]{2,1,0:T(8,128)(2,1)} %grad_own_one_send.1), calls=%async_computation.2 | async-start | bytes 524288 | tf_op jit(solution)/shard_map/all_to_all | solution.py:757
  164.8 22.4 %all-to-all-start.3 = ((bf16[32,48,128]{2,1,0:T(8,128)(2,1)}), bf16[32,48,128]{2,1,0:T(8,128)(2,1)S(1)}, u32[]{:S(2)}, u32[]{:S(2)}) async-start(bf16[32,48,128]{2,1,0:T(8,128)(2,1)} %get-tuple-element.81), calls=%async_computation.3 | async-start | bytes 786432 | tf_op jit(solution)/shard_map/all_to_all | solution.py:827
  175.5 10.2 %collective-permute-start.30 = (bf16[512,128]{1,0:T(8,128)(2,1)}, bf16[512,128]{1,0:T(8,128)(2,1)S(1)}, u32[]{:S(2)}, u32[]{:S(2)}) collective-permute-start(bf16[512,128]{1,0:T(8,128)(2,1)} %get-tuple-element.82), channel_id=1, source_target_pairs={{0,1},{1,2},{2,3},{3,4},{4,5},{5,6},{6,7},{7,0},{8,9},{9,10},{10,1... | collective-permute-start | bytes 393224 | tf_op jit(solution)/shard_map/ppermute | solution.py:768
  177.3 8.4 %collective-permute-start.31 = (bf16[512,128]{1,0:T(8,128)(2,1)}, bf16[512,128]{1,0:T(8,128)(2,1)S(1)}, u32[]{:S(2)}, u32[]{:S(2)}) collective-permute-start(bf16[512,128]{1,0:T(8,128)(2,1)} %get-tuple-element.83), channel_id=1, source_target_pairs={{1,0},{2,1},{3,2},{4,3},{5,4},{6,5},{7,6},{0,7},{9,8},{10,9},{11,1... | collective-permute-start | bytes 393224 | tf_op jit(solution)/shard_map/ppermute | solution.py:769
  188.1 19.3 %all-to-all-start.4 = ((bf16[32,48,128]{2,1,0:T(8,128)(2,1)}), bf16[32,48,128]{2,1,0:T(8,128)(2,1)S(1)}, u32[]{:S(2)}, u32[]{:S(2)}) async-start(bf16[32,48,128]{2,1,0:T(8,128)(2,1)} %broadcast_in_dim.2), calls=%async_computation.4 | async-start | bytes 786432 | tf_op jit(solution)/shard_map/all_to_all | solution.py:832
  (36 other events, 274.9 us)

commit v4 on v3

--- a/solution.py
+++ b/solution.py
@@ -892,22 +892,21 @@
         adjacency_one, pool_two, table_one, own_one, message_one, result1, grad_up_one,
         *weights, padded_rows(2 * level + 2),
     )
-    up_got = exchange(up_send)
     grad_send = owner_sum(table_one, gx_one, scatter_hops(parts_back))
-    grad_send, up_got = lax.optimization_barrier((grad_send, up_got))
     grad_got = exchange(grad_send)
-    node_out = node_out_rows(pool_one_columns, place_cols, up_got, pool_one, result0)
-    grad_got, node_out = lax.optimization_barrier((grad_got, node_out))
+    up_got = exchange(after_all(up_send, grad_got))
 
     sum_rows = padded_rows(level + 1)
     gx_zero, gmsg_zero, sums_send = fine_grad(
         pool_one_columns, place_cols, grad_got, pool_one, coarse_sums, cotangent, node_feats, message0, *weights,
         sum_rows, lax.axis_size(ALL),
     )
+    sums_send, up_got = lax.optimization_barrier((sums_send, up_got))
     shares = send_shares(sums_send)
     rim_low, rim_high, carry = spread_edge(fine_columns, fine_adjacency, gmsg_zero, gx_zero)
     from_prev, from_after = halo_pair(rim_low, rim_high)
-    shares, from_prev, from_after = lax.optimization_barrier((shares, from_prev, from_after))
+    node_out = node_out_rows(pool_one_columns, place_cols, after_all(up_got, carry), pool_one, result0)
+    shares, from_prev, from_after, node_out = lax.optimization_barrier((shares, from_prev, from_after, node_out))
     mine = jnp.sum(shares.astype(F32), axis=0).astype(BF)
     sums = share_sums(mine)
     from_prev = after_all(from_prev, mine)

time: 211 us -> 209 us (level)
  blocking collectives: 19 us -> 31.7 us
  waiting for transfers between devices: 28.2 us -> 19.9 us
  starting transfers between devices: 63.7 us -> 57.8 us
    all_to_all x1 -> x2, blocking collectives: 19 us -> 31.7 us  [exchange(): return lax.all_to_all(parts, 'grp', split_axis=0, concat_axis=0, tiled=True)]
    ppermute x2, waiting for transfers between devices: 5.45 us -> 0.01 us  [halo_pair(): lax.ppermute(high, 'grp', [(i, (i + 1) % count) for i in range(count)])]
    all_to_all x2 -> x1, starting transfers between devices: 7.04 us -> 3.63 us  [exchange(): return lax.all_to_all(parts, 'grp', split_axis=0, concat_axis=0, tiled=True)]
    unnamed x66 -> x64, local copies, waits for them, and re-layouts: 6.88 us -> 6.16 us
  transfers between devices with their start and end apart: 36 -> 35, of which waited for: 11 -> 11; matrix products, arithmetic and copies ran while one was open for 3% -> 3% of each run, Pallas kernels for 25% -> 31%
where the time goes in v4:
time: 209 us; the launch traced here: 208 us
  Pallas kernels  84.7 us (41%)
  starting transfers between devices  57.8 us (28%)
  blocking collectives  31.7 us (15%)
  waiting for transfers between devices  19.9 us (10%)
  local copies, waits for them, and re-layouts  8.67 us (4%)
  other arithmetic  2.58 us (1%)
  between operations  2.31 us (1%)
    ppermute x28, starting transfers between devices, hop_by(): lax.ppermute(rows, axis, [(i, i ^ hop) for i in range(lax.axis_size(axis))])  34.6 us
    all_to_all x2, blocking collectives, exchange(): return lax.all_to_all(parts, 'grp', split_axis=0, concat_axis=0, tiled=True)  31.7 us
    ppermute x28, waiting for transfers between devices, hop_by(): lax.ppermute(rows, axis, [(i, i ^ hop) for i in range(lax.axis_size(axis))])  19.9 us
    pallas_call x1, Pallas kernels, fine_forward(): pl.pallas_call(functools.partial(fine_kernel, groups=groups, balance=bala...  18.8 us
    pallas_call x1, Pallas kernels, spread_inner(): pl.pallas_call(functools.partial(spread_inner_kernel, rim=HALO // BLK, gr...  15.7 us
    pallas_call x1, Pallas kernels, fine_grad(): pl.pallas_call(fine_grad_kernel, grid=(total // rows,), out_shape=(jax.Sh...  14.9 us
    pallas_call x1, Pallas kernels, coarse_levels(): pl.pallas_call(functools.partial(coarse_kernel, groups), out_shape=(jax.S...  9.7 us
    ppermute x2, starting transfers between devices, halo_pair(): lax.ppermute(low, 'grp', [((i + 1) % count, i) for i in range(count)])  8.99 us
  transfers between devices with their start and end apart: 35, of which 11 were waited for; matrix products, arithmetic and copies ran while one was open for 3% of the time, Pallas kernels for 31%

profile of v4, /device:TPU:0, one launch (start us, length us, event | category | flops | bytes accessed | tf_op | source)
XLA Modules:
  0.0 207.8 jit_solution(16079726213222556304)
XLA Ops:
  1.6 6.0 %collective-permute-start.1 = (bf16[512,128]{1,0:T(8,128)(2,1)S(1)}, bf16[512,128]{1,0:T(8,128)(2,1)S(1)}, u32[]{:S(2)}, u32[]{:S(2)}) collective-permute-start(bf16[512,128]{1,0:T(8,128)(2,1)S(1)} %get-tuple-element.93), channel_id=1, source_target_pairs={{1,0},{2,1},{3,2},{4,3},{5,4},{6,5},{7,6},{0,7},{9,8},{10,9},{11,1... | collective-permute-start | bytes 393224 | tf_op jit(solution)/shard_map/ppermute | solution.py:769
  9.1 4.4 %collective-permute-start.4 = (bf16[2,64,512]{2,1,0:T(8,128)(2,1)}, bf16[2,64,512]{2,1,0:T(8,128)(2,1)S(1)}, u32[]{:S(2)}, u32[]{:S(2)}) collective-permute-start(bf16[2,64,512]{2,1,0:T(8,128)(2,1)} %refs_8_.1), channel_id=1, source_target_pairs={{0,4},{1,5},{2,6},{3,7},{4,0},{5,1},{6,2},{7,3},{8,12},{9,13},{10,... | collective-permute-start | bytes 393224 | tf_op jit(solution)/shard_map/ppermute | solution.py:774
  18.3 18.8 %fine_forward.1 = (bf16[8192,128]{1,0:T(8,128)(2,1)}, bf16[8192,128]{1,0:T(8,128)(2,1)}, bf16[8,272,128]{2,1,0:T(8,128)(2,1)}, f32[1024,128]{1,0:T(8,128)}, s32[1,256]{1,0:T(1,128)}) custom-call(s32[1]{0:T(128)} %bitcast.me, s32[128,12]{1,0:T(8,128)} %copy.24.cols, s32[16,8]{1,0:T(8,128)} %copy.26.pool_cols.cols, s32[1]{0:T(128)S(6)} %copy.30.count, ...), custom_call_target="tpu_custom_call" | custom-call | bytes 221400000 | tf_op jit(solution)/shard_map/fine_forward/pallas_call | solution.py:226
  37.1 19.0 %all_to_all.25.got.refs_17_ = bf16[8,272,128]{2,1,0:T(8,128)(2,1)} all-to-all(bf16[8,272,128]{2,1,0:T(8,128)(2,1)} %get-tuple-element.51), channel_id=1, replica_groups=mesh['slab'=4,'grp'=8] {'grp'}, dimensions={0} | all-to-all | bytes 1114112 | tf_op jit(solution)/shard_map/all_to_all | solution.py:757
  56.2 2.1 %place_own_one.1.refs_0_.refs_21_ = bf16[512,128]{1,0:T(8,128)(2,1)} custom-call(bf16[8,272,128]{2,1,0:T(8,128)(2,1)} %all_to_all.25.got.refs_17_), custom_call_target="tpu_custom_call" | custom-call | bytes 33210000 | tf_op jit(solution)/shard_map/place_own_one/pallas_call | solution.py:278
  60.3 5.6 %collective-permute-done.8.refs_4_ = bf16[512,128]{1,0:T(8,128)(2,1)S(1)} collective-permute-done((bf16[512,128]{1,0:T(8,128)(2,1)}, bf16[512,128]{1,0:T(8,128)(2,1)S(1)}, u32[]{:S(2)}, u32[]{:S(2)}) %collective-permute-start.8) | collective-permute-done | bytes 131104 | tf_op jit(solution)/shard_map/ppermute | solution.py:774
  68.7 2.3 %collective-permute-done.9.refs_5_ = bf16[512,128]{1,0:T(8,128)(2,1)S(1)} collective-permute-done((bf16[512,128]{1,0:T(8,128)(2,1)S(1)}, bf16[512,128]{1,0:T(8,128)(2,1)S(1)}, u32[]{:S(2)}, u32[]{:S(2)}) %collective-permute-start.9) | collective-permute-done | bytes 131104 | tf_op jit(solution)/shard_map/ppermute | solution.py:774
  71.6 2.5 %place_grad_up_one.1 = (bf16[512,128]{1,0:T(8,128)(2,1)}, bf16[256,128]{1,0:T(8,128)(2,1)}, s32[8,128]{1,0:T(8,128)}) custom-call(s32[4,8]{1,0:T(4,128)} %pool_cols.4, bf16[8,272,128]{2,1,0:T(8,128)(2,1)} %all_to_all.25.got.refs_17_, bf16[4,64,512]{2,1,0:T(8,128)(2,1)} %refs_19_.1), custom_call_target="tpu_custom_call" | custom-call | bytes 33210000 | tf_op jit(solution)/shard_map/place_grad_up_one/pallas_call | solution.py:302
  74.1 1.9 collective-permute-done.11.refs_7_
  76.7 3.2 %level_one_forward.1 = (bf16[512,128]{1,0:T(8,128)(2,1)}, bf16[512,128]{1,0:T(8,128)(2,1)}, bf16[256,256]{1,0:T(8,128)(2,1)}) custom-call(s32[1]{0:T(128)} %bitcast.me, s32[8,8]{1,0:T(8,128)} %cols_one.1, s32[4,8]{1,0:T(4,128)} %pool_cols.4, bf16[512,128]{1,0:T(8,128)(2,1)} %place_own_one.1.refs_0_.refs_21_, bf16[512,128]{1,0:T(8,128)(2,1)} %copy-done.23, ...), custom_call_target="tpu_custom_call" | custom-call | bytes 33210000 | tf_op jit(solution)/shard_map/level_one_forward/pallas_call | solution.py:339
  79.9 2.1 collective-permute-start.15
  84.0 2.0 collective-permute-start.21
  86.9 2.0 collective-permute-start.16
  90.4 1.6 collective-permute-start.12
  91.9 1.8 collective-permute-start.17
  94.3 1.8 collective-permute-start.18
  100.0 9.7 %coarse_levels.1 = (bf16[8,128,128]{2,1,0:T(8,128)(2,1)}, f32[512,128]{1,0:T(8,128)}, f32[1024,128]{1,0:T(8,128)}, bf16[512,128]{1,0:T(8,128)(2,1)}, bf16[512,12...) custom-call(s32[1]{0:T(128)} %bitcast.me, ...), custom_call_target="tpu_custom_call" | custom-call | bytes 99630000 | tf_op jit(solution)/shard_map/coarse_levels/pallas_call | solution.py:462
  116.3 1.9 collective-permute-done.24
  120.5 2.3 %collective-permute-start.27 = (bf16[512,128]{1,0:T(8,128)(2,1)S(1)}, bf16[512,128]{1,0:T(8,128)(2,1)S(1)}, u32[]{:S(2)}, u32[]{:S(2)}) collective-permute-start(bf16[512,128]{1,0:T(8,128)(2,1)S(1)} %add_convert_fusion), channel_id=1, source_target_pairs={{0,2},{1,3},{2,0},{3,1},{4,6},{5,7},{6,4},{7,5},{8,10},{9,11},{10,... | collective-permute-start | bytes 393224 | tf_op jit(solution)/shard_map/ppermute | solution.py:774
  122.9 3.8 %collective-permute-done.25.refs_0_ = bf16[512,128]{1,0:T(8,128)(2,1)S(1)} collective-permute-done((bf16[512,128]{1,0:T(8,128)(2,1)S(1)}, bf16[512,128]{1,0:T(8,128)(2,1)S(1)}, u32[]{:S(2)}, u32[]{:S(2)}) %collective-permute-start.25) | collective-permute-done | bytes 131104 | tf_op jit(solution)/shard_map/ppermute | solution.py:774
  127.7 2.4 %grad_own_one_send.1 = bf16[8,128,128]{2,1,0:T(8,128)(2,1)} custom-call(s32[8,128]{1,0:T(8,128)} %get-tuple-element.53.refs_20_.table, f32[512,128]{1,0:T(8,128)} %get-tuple-element.63.gx, bf16[512,128]{1,0:T(8,128)(2,1)} %copy-done.29, bf16[512,128]{1,0:T(8,128)(2,1)} %copy-done.30, bf16[512,128]{1,0:T(8,128)(2,1)} %copy-done.27, bf16[512,128]{1,0:T(8,128)(2,1)} %copy-done.28), custom_call_target="tpu_custom_call" | custom-call | bytes 33210000 | tf_op jit(solution)/shard_map/grad_own_one_send/pallas_call | solution.py:506
  130.1 12.7 %all_to_all.26.got = bf16[8,128,128]{2,1,0:T(8,128)(2,1)} all-to-all(bf16[8,128,128]{2,1,0:T(8,128)(2,1)} %grad_own_one_send.1), channel_id=1, replica_groups=mesh['slab'=4,'grp'=8] {'grp'}, dimensions={0} | all-to-all | bytes 524288 | tf_op jit(solution)/shard_map/all_to_all | solution.py:757
  142.8 3.6 %all-to-all-start.2 = ((bf16[8,128,128]{2,1,0:T(8,128)(2,1)}), bf16[8,128,128]{2,1,0:T(8,128)(2,1)S(1)}, u32[]{:S(2)}, u32[]{:S(2)}) async-start(bf16[8,128,128]{2,1,0:T(8,128)(2,1)} %get-tuple-element.75), calls=%async_computation.2 | async-start | bytes 524288 | tf_op jit(solution)/shard_map/all_to_all | solution.py:757
  146.4 14.9 %fine_layer_backward.1 = (f32[8192,128]{1,0:T(8,128)}, bf16[8192,128]{1,0:T(8,128)(2,1)}, bf16[32,48,128]{2,1,0:T(8,128)(2,1)}) custom-call(s32[16,8]{1,0:T(8,128)} %copy.26.pool_cols.cols, f32[1024,128]{1,0:T(8,128)} %get-tuple-element.49.place, bf16[8,128,128]{2,1,0:T(8,128)(2,1)} %all_to_all.26.got, bf16[16,64,512]{2,1,0:T(8,128)(2,1)} %pool.5, ...), custom_call_target="tpu_custom_call" | custom-call | bytes 210330000 | tf_op jit(solution)/shard_map/fine_layer_backward/pallas_call | solution.py:596
  161.3 5.8 %all-to-all-start.3 = ((bf16[32,48,128]{2,1,0:T(8,128)(2,1)}), bf16[32,48,128]{2,1,0:T(8,128)(2,1)S(1)}, u32[]{:S(2)}, u32[]{:S(2)}) async-start(bf16[32,48,128]{2,1,0:T(8,128)(2,1)} %get-tuple-element.76), calls=%async_computation.3 | async-start | bytes 786432 | tf_op jit(solution)/shard_map/all_to_all | solution.py:827
  167.1 4.7 %spread_edge.1 = (bf16[512,128]{1,0:T(8,128)(2,1)}, bf16[512,128]{1,0:T(8,128)(2,1)}, f32[2048,128]{1,0:T(8,128)}) custom-call(s32[128,12]{1,0:T(8,128)} %copy.24.cols, bf16[128,64,768]{2,1,0:T(8,128)(2,1)} %adj_b.1, bf16[8192,128]{1,0:T(8,128)(2,1)} %get-tuple-element.77.gmsg.gmsg_a.gmsg_b, f32[8192,128]{1,0:T(8,128)} %get-tuple-element.78.gx.gx_a.gx_b), custom_call_target="tpu_custom_call" | custom-call | bytes 33210000 | tf_op jit(solution)/shard_map/spread_edge/pallas_call | solution.py:639
  171.8 1.8 collective-permute-start.30
  173.5 3.0 %collective-permute-start.31 = (bf16[512,128]{1,0:T(8,128)(2,1)}, bf16[512,128]{1,0:T(8,128)(2,1)S(1)}, u32[]{:S(2)}, u32[]{:S(2)}) collective-permute-start(bf16[512,128]{1,0:T(8,128)(2,1)} %get-tuple-element.80), channel_id=1, source_target_pairs={{1,0},{2,1},{3,2},{4,3},{5,4},{6,5},{7,6},{0,7},{9,8},{10,9},{11,1... | collective-permute-start | bytes 393224 | tf_op jit(solution)/shard_map/ppermute | solution.py:769
  176.5 8.9 %node_out.1 = bf16[8192,128]{1,0:T(8,128)(2,1)} custom-call(s32[16,8]{1,0:T(8,128)} %copy.26.pool_cols.cols, f32[1024,128]{1,0:T(8,128)} %get-tuple-element.49.place, bf16[8,128,128]{2,1,0:T(8,128)(2,1)} %copy-done.1, bf16[16,64,512]{2,1,0:T(8,128)(2,1)} %pool.5, bf16[8192,128]{1,0:T(8,128)(2,1)} %get-tuple-element.84.base), custom_call_target="tpu_custom_call" | custom-call | bytes 99630000 | tf_op jit(solution)/shard_map/node_out/pallas_call | solution.py:545
  186.3 3.1 %all-to-all-start.4 = ((bf16[32,48,128]{2,1,0:T(8,128)(2,1)}), bf16[32,48,128]{2,1,0:T(8,128)(2,1)S(1)}, u32[]{:S(2)}, u32[]{:S(2)}) async-start(bf16[32,48,128]{2,1,0:T(8,128)(2,1)} %broadcast_in_dim.2), calls=%async_computation.4 | async-start | bytes 786432 | tf_op jit(solution)/shard_map/all_to_all | solution.py:832
  189.4 15.7 %spread_inner.1 = bf16[8192,128]{1,0:T(8,128)(2,1)} custom-call(s32[1]{0:T(128)} %bitcast.me, s32[128,12]{1,0:T(8,128)} %copy.24.cols, bf16[128,64,768]{2,1,0:T(8,128)(2,1)} %adj_b.1, bf16[128,64,768]{2,1,0:T(8,128)(2,1)} %adj_b.1, bf16[8192,128]{1,0:T(8,128)(2,1)} %get-tuple-element.77.gmsg.gmsg_a.gmsg_b, ...), custom_call_target="tpu_custom_call" | custom-call | bytes 199260000 | tf_op jit(solution)/shard_map/spread_inner/pallas_call | solution.py:698
  205.9 1.8 scaled_sums.1
  (122 shorter events, 32.3 us)
Async XLA Ops:
  1.6 16.0 %collective-permute-start.1 = (bf16[512,128]{1,0:T(8,128)(2,1)S(1)}, bf16[512,128]{1,0:T(8,128)(2,1)S(1)}, u32[]{:S(2)}, u32[]{:S(2)}) collective-permute-start(bf16[512,128]{1,0:T(8,128)(2,1)S(1)} %get-tuple-element.93), channel_id=1, source_target_pairs={{1,0},{2,1},{3,2},{4,3},{5,4},{6,5},{7,6},{0,7},{9,8},{10,9},{11,1... | collective-permute-start | bytes 393224 | tf_op jit(solution)/shard_map/ppermute | solution.py:769
  7.7 9.9 %collective-permute-start = (bf16[512,128]{1,0:T(8,128)(2,1)S(1)}, bf16[512,128]{1,0:T(8,128)(2,1)S(1)}, u32[]{:S(2)}, u32[]{:S(2)}) collective-permute-start(bf16[512,128]{1,0:T(8,128)(2,1)S(1)} %get-tuple-element.94), channel_id=1, source_target_pairs={{0,1},{1,2},{2,3},{3,4},{4,5},{5,6},{6,7},{7,0},{8,9},{9,10},{10,1... | collective-permute-start | bytes 393224 | tf_op jit(solution)/shard_map/ppermute | solution.py:768
  7.7 29.4 %collective-permute-start.3 = (bf16[2,64,512]{2,1,0:T(8,128)(2,1)}, bf16[2,64,512]{2,1,0:T(8,128)(2,1)S(1)}, u32[]{:S(2)}, u32[]{:S(2)}) collective-permute-start(bf16[2,64,512]{2,1,0:T(8,128)(2,1)} %refs_8_.1), channel_id=1, source_target_pairs={{0,2},{1,3},{2,0},{3,1},{4,6},{5,7},{6,4},{7,5},{8,10},{9,11},{10,... | collective-permute-start | bytes 393224 | tf_op jit(solution)/shard_map/ppermute | solution.py:774
  7.7 29.4 %collective-permute-start.2 = (bf16[2,64,512]{2,1,0:T(8,128)(2,1)}, bf16[2,64,512]{2,1,0:T(8,128)(2,1)S(1)}, u32[]{:S(2)}, u32[]{:S(2)}) collective-permute-start(bf16[2,64,512]{2,1,0:T(8,128)(2,1)} %refs_8_.1), channel_id=1, source_target_pairs={{0,1},{1,0},{2,3},{3,2},{4,5},{5,4},{6,7},{7,6},{8,9},{9,8},{10,11... | collective-permute-start | bytes 393224 | tf_op jit(solution)/shard_map/ppermute | solution.py:774
  9.1 28.0 %collective-permute-start.4 = (bf16[2,64,512]{2,1,0:T(8,128)(2,1)}, bf16[2,64,512]{2,1,0:T(8,128)(2,1)S(1)}, u32[]{:S(2)}, u32[]{:S(2)}) collective-permute-start(bf16[2,64,512]{2,1,0:T(8,128)(2,1)} %refs_8_.1), channel_id=1, source_target_pairs={{0,4},{1,5},{2,6},{3,7},{4,0},{5,1},{6,2},{7,3},{8,12},{9,13},{10,... | collective-permute-start | bytes 393224 | tf_op jit(solution)/shard_map/ppermute | solution.py:774
  58.3 7.6 %collective-permute-start.8 = (bf16[512,128]{1,0:T(8,128)(2,1)}, bf16[512,128]{1,0:T(8,128)(2,1)S(1)}, u32[]{:S(2)}, u32[]{:S(2)}) collective-permute-start(bf16[512,128]{1,0:T(8,128)(2,1)} %place_own_one.1.refs_0_.refs_21_), channel_id=1, source_target_pairs={{0,4},{1,5},{2,6},{3,7},{4,0},{5,1},{6,2},{7,3},{8,12},{9,13},{10,... | collective-permute-start | bytes 393224 | tf_op jit(solution)/shard_map/ppermute | solution.py:774
  58.9 9.0 %collective-permute-start.6 = (bf16[512,128]{1,0:T(8,128)(2,1)}, bf16[512,128]{1,0:T(8,128)(2,1)S(1)}, u32[]{:S(2)}, u32[]{:S(2)}) collective-permute-start(bf16[512,128]{1,0:T(8,128)(2,1)} %place_own_one.1.refs_0_.refs_21_), channel_id=1, source_target_pairs={{0,2},{1,3},{2,0},{3,1},{4,6},{5,7},{6,4},{7,5},{8,10},{9,11},{10,... | collective-permute-start | bytes 393224 | tf_op jit(solution)/shard_map/ppermute | solution.py:774
  65.9 5.2 %collective-permute-start.9 = (bf16[512,128]{1,0:T(8,128)(2,1)S(1)}, bf16[512,128]{1,0:T(8,128)(2,1)S(1)}, u32[]{:S(2)}, u32[]{:S(2)}) collective-permute-start(bf16[512,128]{1,0:T(8,128)(2,1)S(1)} %collective-permute-done.8.refs_4_), channel_id=1, source_target_pairs={{0,1},{1,0},{2,3},{3,2},{4,5},{5,4},{6,7},{7,6},{8,9},{9,8},{10,11... | collective-permute-start | bytes 393224 | tf_op jit(solution)/shard_map/ppermute | solution.py:774
  66.6 7.5 %collective-permute-start.5 = (bf16[512,128]{1,0:T(8,128)(2,1)}, bf16[512,128]{1,0:T(8,128)(2,1)S(1)}, u32[]{:S(2)}, u32[]{:S(2)}) collective-permute-start(bf16[512,128]{1,0:T(8,128)(2,1)} %place_own_one.1.refs_0_.refs_21_), channel_id=1, source_target_pairs={{0,1},{1,0},{2,3},{3,2},{4,5},{5,4},{6,7},{7,6},{8,9},{9,8},{10,11... | collective-permute-start | bytes 393224 | tf_op jit(solution)/shard_map/ppermute | solution.py:774
  67.9 6.2 %collective-permute-start.10 = (bf16[512,128]{1,0:T(8,128)(2,1)S(1)}, bf16[512,128]{1,0:T(8,128)(2,1)S(1)}, u32[]{:S(2)}, u32[]{:S(2)}) collective-permute-start(bf16[512,128]{1,0:T(8,128)(2,1)S(1)} %collective-permute-done.8.refs_4_), channel_id=1, source_target_pairs={{0,2},{1,3},{2,0},{3,1},{4,6},{5,7},{6,4},{7,5},{8,10},{9,11},{10,... | collective-permute-start | bytes 393224 | tf_op jit(solution)/shard_map/ppermute | solution.py:774
  67.9 6.2 %collective-permute-start.7 = (bf16[512,128]{1,0:T(8,128)(2,1)S(1)}, bf16[512,128]{1,0:T(8,128)(2,1)S(1)}, u32[]{:S(2)}, u32[]{:S(2)}) collective-permute-start(bf16[512,128]{1,0:T(8,128)(2,1)S(1)} %collective-permute-done.6.refs_2_), channel_id=1, source_target_pairs={{0,1},{1,0},{2,3},{3,2},{4,5},{5,4},{6,7},{7,6},{8,9},{9,8},{10,11... | collective-permute-start | bytes 393224 | tf_op jit(solution)/shard_map/ppermute | solution.py:774
  79.9 7.0 %collective-permute-start.15 = (bf16[256,256]{1,0:T(8,128)(2,1)}, bf16[256,256]{1,0:T(8,128)(2,1)S(1)}, u32[]{:S(2)}, u32[]{:S(2)}) collective-permute-start(bf16[256,256]{1,0:T(8,128)(2,1)} %get-tuple-element.55.refs_0_), channel_id=1, source_target_pairs={{0,4},{1,5},{2,6},{3,7},{4,0},{5,1},{6,2},{7,3},{8,12},{9,13},{10,... | collective-permute-start | bytes 393224 | tf_op jit(solution)/shard_map/ppermute | solution.py:774
  82.0 6.9 %collective-permute-start.20 = (bf16[2,64,512]{2,1,0:T(8,128)(2,1)S(1)}, bf16[2,64,512]{2,1,0:T(8,128)(2,1)S(1)}, u32[]{:S(2)}, u32[]{:S(2)}) collective-permute-start(bf16[2,64,512]{2,1,0:T(8,128)(2,1)S(1)} %collective-permute-done.4.refs_12_), channel_id=1, source_target_pairs={{0,1},{1,0},{2,3},{3,2},{4,5},{5,4},{6,7},{7,6},{8,9},{9,8},{10,11... | collective-permute-start | bytes 393224 | tf_op jit(solution)/shard_map/ppermute | solution.py:774
  82.8 7.5 %collective-permute-start.19 = (bf16[2,64,512]{2,1,0:T(8,128)(2,1)S(1)}, bf16[2,64,512]{2,1,0:T(8,128)(2,1)S(1)}, u32[]{:S(2)}, u32[]{:S(2)}) collective-permute-start(bf16[2,64,512]{2,1,0:T(8,128)(2,1)S(1)} %collective-permute-done.3.refs_10_), channel_id=1, source_target_pairs={{0,1},{1,0},{2,3},{3,2},{4,5},{5,4},{6,7},{7,6},{8,9},{9,8},{10,11... | collective-permute-start | bytes 393224 | tf_op jit(solution)/shard_map/ppermute | solution.py:774
  84.0 7.9 %collective-permute-start.21 = (bf16[2,64,512]{2,1,0:T(8,128)(2,1)S(1)}, bf16[2,64,512]{2,1,0:T(8,128)(2,1)S(1)}, u32[]{:S(2)}, u32[]{:S(2)}) collective-permute-start(bf16[2,64,512]{2,1,0:T(8,128)(2,1)S(1)} %collective-permute-done.4.refs_12_), channel_id=1, source_target_pairs={{0,2},{1,3},{2,0},{3,1},{4,6},{5,7},{6,4},{7,5},{8,10},{9,11},{10,... | collective-permute-start | bytes 393224 | tf_op jit(solution)/shard_map/ppermute | solution.py:774
  86.0 7.7 %collective-permute-start.13 = (bf16[256,256]{1,0:T(8,128)(2,1)}, bf16[256,256]{1,0:T(8,128)(2,1)S(1)}, u32[]{:S(2)}, u32[]{:S(2)}) collective-permute-start(bf16[256,256]{1,0:T(8,128)(2,1)} %get-tuple-element.55.refs_0_), channel_id=1, source_target_pairs={{0,2},{1,3},{2,0},{3,1},{4,6},{5,7},{6,4},{7,5},{8,10},{9,11},{10,... | collective-permute-start | bytes 393224 | tf_op jit(solution)/shard_map/ppermute | solution.py:774
  86.9 7.4 %collective-permute-start.16 = (bf16[256,256]{1,0:T(8,128)(2,1)S(1)}, bf16[256,256]{1,0:T(8,128)(2,1)S(1)}, u32[]{:S(2)}, u32[]{:S(2)}) collective-permute-start(bf16[256,256]{1,0:T(8,128)(2,1)S(1)} %collective-permute-done.15.refs_4_), channel_id=1, source_target_pairs={{0,1},{1,0},{2,3},{3,2},{4,5},{5,4},{6,7},{7,6},{8,9},{9,8},{10,11... | collective-permute-start | bytes 393224 | tf_op jit(solution)/shard_map/ppermute | solution.py:774
  88.9 8.6 %collective-permute-start.22 = (bf16[2,64,512]{2,1,0:T(8,128)(2,1)S(1)}, bf16[2,64,512]{2,1,0:T(8,128)(2,1)S(1)}, u32[]{:S(2)}, u32[]{:S(2)}) collective-permute-start(bf16[2,64,512]{2,1,0:T(8,128)(2,1)S(1)} %collective-permute-done.20.refs_13_), channel_id=1, source_target_pairs={{0,2},{1,3},{2,0},{3,1},{4,6},{5,7},{6,4},{7,5},{8,10},{9,11},{10,... | collective-permute-start | bytes 393224 | tf_op jit(solution)/shard_map/ppermute | solution.py:774
  90.4 7.1 %collective-permute-start.12 = (bf16[256,256]{1,0:T(8,128)(2,1)}, bf16[256,256]{1,0:T(8,128)(2,1)S(1)}, u32[]{:S(2)}, u32[]{:S(2)}) collective-permute-start(bf16[256,256]{1,0:T(8,128)(2,1)} %get-tuple-element.55.refs_0_), channel_id=1, source_target_pairs={{0,1},{1,0},{2,3},{3,2},{4,5},{5,4},{6,7},{7,6},{8,9},{9,8},{10,11... | collective-permute-start | bytes 393224 | tf_op jit(solution)/shard_map/ppermute | solution.py:774
  91.9 5.6 %collective-permute-start.17 = (bf16[256,256]{1,0:T(8,128)(2,1)S(1)}, bf16[256,256]{1,0:T(8,128)(2,1)S(1)}, u32[]{:S(2)}, u32[]{:S(2)}) collective-permute-start(bf16[256,256]{1,0:T(8,128)(2,1)S(1)} %collective-permute-done.15.refs_4_), channel_id=1, source_target_pairs={{0,2},{1,3},{2,0},{3,1},{4,6},{5,7},{6,4},{7,5},{8,10},{9,11},{10,... | collective-permute-start | bytes 393224 | tf_op jit(solution)/shard_map/ppermute | solution.py:774
  109.7 6.7 %collective-permute-start.23 = (bf16[512,128]{1,0:T(8,128)(2,1)}, bf16[512,128]{1,0:T(8,128)(2,1)S(1)}, u32[]{:S(2)}, u32[]{:S(2)}) collective-permute-start(bf16[512,128]{1,0:T(8,128)(2,1)} %get-tuple-element.65), channel_id=1, source_target_pairs={{0,1},{1,0},{2,3},{3,2},{4,5},{5,4},{6,7},{7,6},{8,9},{9,8},{10,11... | collective-permute-start | bytes 393224 | tf_op jit(solution)/shard_map/ppermute | solution.py:774
  111.2 7.0 %collective-permute-start.24 = (bf16[512,128]{1,0:T(8,128)(2,1)}, bf16[512,128]{1,0:T(8,128)(2,1)S(1)}, u32[]{:S(2)}, u32[]{:S(2)}) collective-permute-start(bf16[512,128]{1,0:T(8,128)(2,1)} %get-tuple-element.66), channel_id=1, source_target_pairs={{0,2},{1,3},{2,0},{3,1},{4,6},{5,7},{6,4},{7,5},{8,10},{9,11},{10,... | collective-permute-start | bytes 393224 | tf_op jit(solution)/shard_map/ppermute | solution.py:774
  112.7 6.9 %collective-permute-start.26 = (bf16[512,128]{1,0:T(8,128)(2,1)}, bf16[512,128]{1,0:T(8,128)(2,1)S(1)}, u32[]{:S(2)}, u32[]{:S(2)}) collective-permute-start(bf16[512,128]{1,0:T(8,128)(2,1)} %get-tuple-element.68), channel_id=1, source_target_pairs={{0,1},{1,0},{2,3},{3,2},{4,5},{5,4},{6,7},{7,6},{8,9},{9,8},{10,11... | collective-permute-start | bytes 393224 | tf_op jit(solution)/shard_map/ppermute | solution.py:774
  113.6 9.3 %collective-permute-start.28 = (bf16[512,128]{1,0:T(8,128)(2,1)}, bf16[512,128]{1,0:T(8,128)(2,1)S(1)}, u32[]{:S(2)}, u32[]{:S(2)}) collective-permute-start(bf16[512,128]{1,0:T(8,128)(2,1)} %get-tuple-element.69), channel_id=1, source_target_pairs={{0,1},{1,0},{2,3},{3,2},{4,5},{5,4},{6,7},{7,6},{8,9},{9,8},{10,11... | collective-permute-start | bytes 393224 | tf_op jit(solution)/shard_map/ppermute | solution.py:774
  114.7 8.1 %collective-permute-start.29 = (bf16[512,128]{1,0:T(8,128)(2,1)}, bf16[512,128]{1,0:T(8,128)(2,1)S(1)}, u32[]{:S(2)}, u32[]{:S(2)}) collective-permute-start(bf16[512,128]{1,0:T(8,128)(2,1)} %get-tuple-element.70), channel_id=1, source_target_pairs={{0,7},{1,6},{2,5},{3,4},{4,3},{5,2},{6,1},{7,0},{8,15},{9,14},{10,... | collective-permute-start | bytes 393224 | tf_op jit(solution)/shard_map/ppermute | solution.py:774
  119.2 7.4 %collective-permute-start.25 = (bf16[512,128]{1,0:T(8,128)(2,1)S(1)}, bf16[512,128]{1,0:T(8,128)(2,1)S(1)}, u32[]{:S(2)}, u32[]{:S(2)}) collective-permute-start(bf16[512,128]{1,0:T(8,128)(2,1)S(1)} %add_convert_fusion.1), channel_id=1, source_target_pairs={{0,4},{1,5},{2,6},{3,7},{4,0},{5,1},{6,2},{7,3},{8,12},{9,13},{10,... | collective-permute-start | bytes 393224 | tf_op jit(solution)/shard_map/ppermute | solution.py:774
  120.5 6.5 %collective-permute-start.27 = (bf16[512,128]{1,0:T(8,128)(2,1)S(1)}, bf16[512,128]{1,0:T(8,128)(2,1)S(1)}, u32[]{:S(2)}, u32[]{:S(2)}) collective-permute-start(bf16[512,128]{1,0:T(8,128)(2,1)S(1)} %add_convert_fusion), channel_id=1, source_target_pairs={{0,2},{1,3},{2,0},{3,1},{4,6},{5,7},{6,4},{7,5},{8,10},{9,11},{10,... | collective-permute-start | bytes 393224 | tf_op jit(solution)/shard_map/ppermute | solution.py:774
  142.8 18.5 %all-to-all-start.2 = ((bf16[8,128,128]{2,1,0:T(8,128)(2,1)}), bf16[8,128,128]{2,1,0:T(8,128)(2,1)S(1)}, u32[]{:S(2)}, u32[]{:S(2)}) async-start(bf16[8,128,128]{2,1,0:T(8,128)(2,1)} %get-tuple-element.75), calls=%async_computation.2 | async-start | bytes 524288 | tf_op jit(solution)/shard_map/all_to_all | solution.py:757
  161.3 24.1 %all-to-all-start.3 = ((bf16[32,48,128]{2,1,0:T(8,128)(2,1)}), bf16[32,48,128]{2,1,0:T(8,128)(2,1)S(1)}, u32[]{:S(2)}, u32[]{:S(2)}) async-start(bf16[32,48,128]{2,1,0:T(8,128)(2,1)} %get-tuple-element.76), calls=%async_computation.3 | async-start | bytes 786432 | tf_op jit(solution)/shard_map/all_to_all | solution.py:827
  171.8 13.6 %collective-permute-start.30 = (bf16[512,128]{1,0:T(8,128)(2,1)}, bf16[512,128]{1,0:T(8,128)(2,1)S(1)}, u32[]{:S(2)}, u32[]{:S(2)}) collective-permute-start(bf16[512,128]{1,0:T(8,128)(2,1)} %get-tuple-element.79), channel_id=1, source_target_pairs={{0,1},{1,2},{2,3},{3,4},{4,5},{5,6},{6,7},{7,0},{8,9},{9,10},{10,1... | collective-permute-start | bytes 393224 | tf_op jit(solution)/shard_map/ppermute | solution.py:768
  173.5 11.8 %collective-permute-start.31 = (bf16[512,128]{1,0:T(8,128)(2,1)}, bf16[512,128]{1,0:T(8,128)(2,1)S(1)}, u32[]{:S(2)}, u32[]{:S(2)}) collective-permute-start(bf16[512,128]{1,0:T(8,128)(2,1)} %get-tuple-element.80), channel_id=1, source_target_pairs={{1,0},{2,1},{3,2},{4,3},{5,4},{6,5},{7,6},{0,7},{9,8},{10,9},{11,1... | collective-permute-start | bytes 393224 | tf_op jit(solution)/shard_map/ppermute | solution.py:769
  186.3 18.9 %all-to-all-start.4 = ((bf16[32,48,128]{2,1,0:T(8,128)(2,1)}), bf16[32,48,128]{2,1,0:T(8,128)(2,1)S(1)}, u32[]{:S(2)}, u32[]{:S(2)}) async-start(bf16[32,48,128]{2,1,0:T(8,128)(2,1)} %broadcast_in_dim.2), calls=%async_computation.4 | async-start | bytes 786432 | tf_op jit(solution)/shard_map/all_to_all | solution.py:832
  (34 other events, 267.1 us)
